TPU v7x, 512 devices: a whole 4x8x8 slice. The times are simulated.
512 devices in a mesh: group: 4 (over z_lo), expert: 128 (over y, z_hi, x, core).
Axes of the slice: x: 4, y: 8, z: 8 (z_hi: 2, z_lo: 4; z = z_hi * 4 + z_lo), core: 2. Of those that a mesh axis runs over, the one named last changes fastest.
Arguments:
- master_weights: float32 [128, 2048, 384], P('group', 'expert'), may hold values from -0.125 to 0.125
- first_moment: float32 [128, 2048, 384], P('group', 'expert'), may hold values from -3 to 3
- second_moment: float32 [128, 2048, 384], P('group', 'expert'), may hold values from 1 to 16
- gradient: bfloat16 [128, 2048, 384], P('group', 'expert'), may hold values from -24 to 24
- placement: int32 [4, 128], replicated, may hold values from 0 to 127, each once within a row
- tokens: bfloat16 [4, 512, 2048], P('group', 'expert'), may hold values from -6 to 6
- routed_expert_index: int32 [4, 512, 8], P('group', 'expert'), may hold values from 0 to 15, all different within a row; in each aligned block of 4 rows (0 to 3, 4 to 7, ..., all dimensions but the last counted through in order) at most 3 rows name the same one
- gate_weights: float32 [4, 512, 8], P('group', 'expert'), may hold values from 0.2 to 1
Outputs:
- master_out: float32 [128, 2048, 384], P('group', 'expert')
- rollout_weights: bfloat16 [4, 128, 2048, 384], P('group', 'expert')
- decoded: bfloat16 [4, 512, 2048], P('group', 'expert')
Inputs may be any that keep to these rules, and one draw needn't show every extreme that they name: Each row of placement is a permutation; entry u names the device of that group that holds slab u, hidden units (u % 8) * 128 onward of expert u // 8. `routed_expert_index`: each row names 8 different experts. Among the rows of one device no expert is named by more than 3 rows, and in every draw some device has an expert named by exactly 3 rows.
All inputs are finite; a program needn't handle non-finite values.
Results may differ from a plain program's by a relative error of at most 0.0055.
The roundings to bfloat16 on the way count: a program that leaves them out, or rounds other values in their place, can miss the bound.
Values may be sent and summed in bfloat16 or wider, within the bound.
No kernel may reach another device: no remote copies, remote signals or barrier semaphores. Data moves between devices by JAX's collectives and lax.ppermute only.
A program may use at most 64 MiB of HBM per device.

v0:
```python
import jax
import jax.numpy as jnp
from jax import lax
from jax.sharding import PartitionSpec as P

FFW = 1024


adam_step = 1000.0
adam_eps = 1e-08
learn_rate = 0.005
weight_decay = 0.1
beta_one = 0.9
beta_two = 0.999


def per_device(
    master_weights,
    first_moment,
    second_moment,
    gradient,
    placement,
    tokens,
    routed_expert_index,
    gate_weights,
):
    grad_float = gradient.astype(jnp.float32)
    first_new = beta_one * first_moment + (1.0 - beta_one) * grad_float
    second_new = beta_two * second_moment + (1.0 - beta_two) * grad_float * grad_float
    update = (
        first_new
        / (1.0 - beta_one**adam_step)
        / (jnp.sqrt(second_new / (1.0 - beta_two**adam_step)) + adam_eps)
    )
    master_out = master_weights - learn_rate * (update + weight_decay * master_weights)
    rounded_down_value = master_out.astype(jnp.bfloat16)
    unit_count = placement.shape[1]
    unit_ids = jnp.arange(unit_count, dtype=jnp.int32)
    own_row = lax.dynamic_index_in_dim(placement, lax.axis_index("group"), 0, keepdims=False)
    matches = own_row[:, None] == unit_ids[None, :]
    holder = jnp.sum(jnp.where(matches, unit_ids[:, None], 0), axis=0)
    gathered = lax.all_gather(rounded_down_value, "group", axis=0, tiled=True)
    ordered = jnp.take(gathered, holder, axis=0)
    own_slab = lax.all_to_all(ordered, "expert", split_axis=0, concat_axis=1, tiled=True)
    rollout_out = own_slab[None]
    weights = own_slab[0]
    slab_width = weights.shape[1] // 3
    slab_count = FFW // slab_width
    count_of_rows = tokens.shape[1]
    experts_here = holder // slab_count
    hit_table = routed_expert_index[0][:, :, None] == experts_here[None, None, :]
    routing_hit_count = jnp.sum(hit_table.astype(jnp.int32), axis=1)
    coefficient = jnp.sum(jnp.where(hit_table, gate_weights[0][:, :, None], 0.0), axis=1)
    slot_rank = jnp.broadcast_to(
        jnp.arange(count_of_rows, dtype=jnp.int32)[:, None], routing_hit_count.shape
    )
    slot_ids = jnp.arange(count_of_rows, dtype=jnp.int32)
    selected = (routing_hit_count.T[:, None, :] > 0) & (
        slot_rank.T[:, None, :] == slot_ids[None, :, None]
    )
    expert_selection_mask = jnp.where(selected, 1.0, 0.0)
    dispatch = jnp.einsum(
        "gvf,fz->gvz",
        expert_selection_mask.astype(jnp.bfloat16),
        tokens[0],
        preferred_element_type=jnp.float32,
    ).astype(jnp.bfloat16)
    received = lax.all_to_all(dispatch, "expert", split_axis=0, concat_axis=0, tiled=True)
    flattened = received.reshape(-1, received.shape[2])
    gate_up = jnp.dot(flattened, weights[:, : 2 * slab_width], preferred_element_type=jnp.float32)
    hidden = (jax.nn.silu(gate_up[:, :slab_width]) * gate_up[:, slab_width:]).astype(jnp.bfloat16)
    partial_value = lax.dot_general(
        hidden,
        weights[:, 2 * slab_width :],
        (((1,), (1,)), ((), ())),
        preferred_element_type=jnp.float32,
    ).astype(jnp.bfloat16)
    partial_value = partial_value.reshape(received.shape)
    gathered_back_rows = lax.all_to_all(
        partial_value, "expert", split_axis=0, concat_axis=0, tiled=True
    )
    expert_mixture_weights = expert_selection_mask * coefficient.T[:, None, :]
    decoded = jnp.einsum(
        "jts,jto->so",
        expert_mixture_weights,
        gathered_back_rows.astype(jnp.float32),
        precision=lax.Precision.HIGHEST,
    )
    return (master_out, rollout_out, decoded.astype(jnp.bfloat16)[None])


def solution(mesh):
    return jax.shard_map(
        per_device,
        mesh=mesh,
        in_specs=(
            P("group", "expert", None),
            P("group", "expert", None),
            P("group", "expert", None),
            P("group", "expert", None),
            P(),
            P("group", "expert", None),
            P("group", "expert", None),
            P("group", "expert", None),
        ),
        out_specs=(
            P("group", "expert", None),
            P("group", "expert", None, None),
            P("group", "expert", None),
        ),
        check_vma=False,
    )
```

profile of v0, /device:TPU:6, one launch (start us, length us, event | category | flops | bytes accessed | tf_op | source)
XLA Modules:
  0.0 255.4 jit_solution(9530355507599167402)
XLA Ops:
  7.2 0.0 copy-start
  7.2 0.7 dynamic-slice_bitcast_fusion
  7.9 0.1 select_reduce_fusion
  8.0 0.8 fusion.18
  8.8 0.0 copy-done
  8.8 0.8 convolution_convert_fusion.1
  9.5 3.0 %copy.16 = bf16[128,4,2048]{2,1,0:T(4,128)(2,1)} copy(bf16[128,4,2048]{2,0,1:T(8,128)(2,1)S(1)} %convolution_convert_fusion.1) | data formatting | bytes 4194304 | tf_op jit(solution)/shard_map/convert_element_type | solution.py:67
  12.5 0.0 copy-start.2
  12.5 0.0 copy-start.3
  12.5 20.0 %all-to-all-start.1 = ((bf16[128,4,2048]{2,1,0:T(4,128)(2,1)}), bf16[128,4,2048]{2,1,0:T(4,128)(2,1)S(1)}, u32[]{:S(2)}, u32[]{:S(2)}) async-start(bf16[128,4,2048]{2,1,0:T(4,128)(2,1)} %copy.16), calls=%async_computation.1 | async-start | bytes 4194304 | tf_op jit(solution)/shard_map/all_to_all | solution.py:68
  32.5 0.0 all-gather.2.cloned.1.call-start
  32.5 0.0 copy-done.2
  32.5 0.0 copy-done.3
  32.5 3.0 %fusion.36 = (bf16[32,16,384]{2,1,0:T(8,128)(2,1)}, f32[32,16,384]{2,1,0:T(8,128)}) fusion(f32[32,16,384]{2,1,0:T(8,128)S(1)} %copy-done.2, f32[32,16,384]{2,1,0:T(8,128)} %param.10, bf16[32,16,384]{2,1,0:T(8,128)(2,1)S(1)} %copy-done.3, f32[32,16,384]{2,1,0:T(8,128)} %param.9), kind=kLoop, calls=%fused_computation.59 | loop fusion | flops 3145728 | bytes 3932160 | tf_op jit(solution)/shard_map/convert_element_type | solution.py:36
  35.5 0.0 all-gather.2.cloned.1.call-update
  35.6 71.9 %all-gather.2.cloned.1.call-done = bf16[128,16,384]{2,1,0:T(8,128)(2,1)} async-done(((bf16[32,16,384]{2,1,0:T(8,128)(2,1)}), bf16[128,16,384]{2,1,0:T(8,128)(2,1)}) %all-gather.2.cloned.1.call-update) | async-done | bytes 1572880 | tf_op jit(solution)/shard_map/all_gather | solution.py:42
  107.5 3.3 %gather_fusion = bf16[128,16,384]{2,1,0:T(8,128)(2,1)} fusion(bf16[128,16,384]{2,1,0:T(8,128)(2,1)} %all-gather.2.cloned.1.call-done, s32[1024]{0:T(1024)S(1)} %pad_clamp_fusion), kind=kCustom, calls=%fused_computation | custom fusion | bytes 3146240 | tf_op jit(solution)/shard_map/jit(_take)/gather | solution.py:43
  110.8 2.8 %broadcast_select_fusion = bf16[128,16,384]{2,1,0:T(8,128)(2,1)} fusion(bf16[128,16,384]{2,1,0:T(8,128)(2,1)} %gather_fusion, pred[128]{0:T(512)(128)(4,1)S(1)} %compare_and_fusion), kind=kLoop, calls=%fused_computation.7 | loop fusion | flops 786432 | bytes 3145856 | tf_op jit(solution)/shard_map/jit(_take)/select_n | solution.py:43
  113.6 0.0 all-to-all-done.1
  113.6 0.0 copy-start.1
  113.6 1.3 copy-done.1
  115.0 13.4 %all-to-all-start = ((bf16[128,16,384]{2,1,0:T(8,128)(2,1)}), bf16[128,16,384]{2,1,0:T(8,128)(2,1)S(1)}, u32[]{:S(2)}, u32[]{:S(2)}) async-start(bf16[128,16,384]{2,1,0:T(8,128)(2,1)} %broadcast_select_fusion), calls=%async_computation | async-start | bytes 3145728 | tf_op jit(solution)/shard_map/all_to_all | solution.py:44
  128.4 3.9 %reshape.60 = bf16[512,2048]{1,0:T(8,128)(2,1)} reshape(bf16[128,4,2048]{2,1,0:T(4,128)(2,1)} %copy-done.1) | data formatting | bytes 4194304 | tf_op jit(solution)/shard_map/reshape | solution.py:69
  132.3 39.1 %all-to-all-done = bf16[128,16,384]{2,1,0:T(8,128)(2,1)S(1)} async-done(((bf16[128,16,384]{2,1,0:T(8,128)(2,1)}), bf16[128,16,384]{2,1,0:T(8,128)(2,1)S(1)}, u32[]{:S(2)}, u32[]{:S(2)}) %all-to-all-start) | async-done | bytes 1572896 | tf_op jit(solution)/shard_map/all_to_all | solution.py:44
  171.4 2.3 fusion.3
  173.7 2.0 convolution_convert_fusion
  175.7 4.1 %reshape.61 = bf16[128,4,2048]{2,1,0:T(4,128)(2,1)} reshape(bf16[512,2048]{1,0:T(8,128)(2,1)} %convolution_convert_fusion) | data formatting | bytes 4194304 | tf_op jit(solution)/shard_map/reshape | solution.py:78
  179.8 0.0 copy-start.4
  179.8 0.0 copy-start.5
  179.8 8.8 %all-to-all-start.2 = ((bf16[128,4,2048]{2,1,0:T(4,128)(2,1)}), bf16[128,4,2048]{2,1,0:T(4,128)(2,1)}, u32[]{:S(2)}, u32[]{:S(2)}) async-start(bf16[128,4,2048]{2,1,0:T(4,128)(2,1)} %reshape.61), calls=%async_computation.2 | async-start | bytes 4194304 | tf_op jit(solution)/shard_map/all_to_all | solution.py:79
  188.6 0.0 copy-done.4
  188.6 0.0 copy-done.5
  188.6 0.1 fusion.19
  188.7 53.6 %all-to-all-done.2 = bf16[128,4,2048]{2,1,0:T(4,128)(2,1)} async-done(((bf16[128,4,2048]{2,1,0:T(4,128)(2,1)}), bf16[128,4,2048]{2,1,0:T(4,128)(2,1)}, u32[]{:S(2)}, u32[]{:S(2)}) %all-to-all-start.2) | async-done | bytes 2097184 | tf_op jit(solution)/shard_map/all_to_all | solution.py:79
  242.3 5.2 %fusion.1 = bf16[1,4,2048]{2,1,0:T(4,128)(2,1)} fusion(bf16[128,4,2048]{2,1,0:T(4,128)(2,1)} %all-to-all-done.2, f32[128,4]{0,1:T(4,128)S(1)} %bitcast.31, pred[128,4]{0,1:T(4,128)(4,1)S(1)} %compare_bitcast_fusion), kind=kOutput, calls=%fused_computation.5 | convolution fusion | flops 50348032 | bytes 2116096 | tf_op jit(solution)/shard_map/jts,jto->so/dot_general | solution.py:83
  247.5 1.1 copy.21
  (5 shorter events, 0.0 us)
Async XLA Ops:
  7.2 1.6 copy-start
  12.5 20.0 %copy-start.2 = (f32[32,16,384]{2,1,0:T(8,128)S(1)}, f32[32,16,384]{2,1,0:T(8,128)}, u32[]{:S(2)}) copy-start(f32[32,16,384]{2,1,0:T(8,128)} %param.8) | copy-start | bytes 2359300
  12.5 20.0 %copy-start.3 = (bf16[32,16,384]{2,1,0:T(8,128)(2,1)S(1)}, bf16[32,16,384]{2,1,0:T(8,128)(2,1)}, u32[]{:S(2)}) copy-start(bf16[32,16,384]{2,1,0:T(8,128)(2,1)} %param.11) | copy-start | bytes 1179652
  12.5 101.1 %all-to-all-start.1 = ((bf16[128,4,2048]{2,1,0:T(4,128)(2,1)}), bf16[128,4,2048]{2,1,0:T(4,128)(2,1)S(1)}, u32[]{:S(2)}, u32[]{:S(2)}) async-start(bf16[128,4,2048]{2,1,0:T(4,128)(2,1)} %copy.16), calls=%async_computation.1 | async-start | bytes 4194304 | tf_op jit(solution)/shard_map/all_to_all | solution.py:68
  32.5 75.0 %all-gather.2.cloned.1.call-start = ((), (), s32[]{:S(2)}) async-start(), calls=%async_computation.3 | async-start | bytes 1966080 | tf_op jit(solution)/shard_map/all_gather | solution.py:42
  113.6 1.3 copy-start.1
  115.0 56.4 %all-to-all-start = ((bf16[128,16,384]{2,1,0:T(8,128)(2,1)}), bf16[128,16,384]{2,1,0:T(8,128)(2,1)S(1)}, u32[]{:S(2)}, u32[]{:S(2)}) async-start(bf16[128,16,384]{2,1,0:T(8,128)(2,1)} %broadcast_select_fusion), calls=%async_computation | async-start | bytes 3145728 | tf_op jit(solution)/shard_map/all_to_all | solution.py:44
  179.8 8.8 %copy-start.4 = (s32[1,4,8]{2,1,0:T(4,128)S(1)}, s32[1,4,8]{2,1,0:T(4,128)}, u32[]{:S(2)}) copy-start(s32[1,4,8]{2,1,0:T(4,128)} %param.14) | copy-start | bytes 388
  179.8 8.8 %copy-start.5 = (f32[1,4,8]{2,1,0:T(4,128)S(1)}, f32[1,4,8]{2,1,0:T(4,128)}, u32[]{:S(2)}) copy-start(f32[1,4,8]{2,1,0:T(4,128)} %param.15) | copy-start | bytes 388
  179.8 62.5 %all-to-all-start.2 = ((bf16[128,4,2048]{2,1,0:T(4,128)(2,1)}), bf16[128,4,2048]{2,1,0:T(4,128)(2,1)}, u32[]{:S(2)}, u32[]{:S(2)}) async-start(bf16[128,4,2048]{2,1,0:T(4,128)(2,1)} %reshape.61), calls=%async_computation.2 | async-start | bytes 4194304 | tf_op jit(solution)/shard_map/all_to_all | solution.py:79
Sparse Core Ops, SparseCore 0:
  36.0 71.4 all-gather.1
where the time goes:
time: 258 us; the launch traced here: 255 us
  waiting for transfers between devices  165 us (64%)
  starting transfers between devices  42.2 us (16%)
  local copies, waits for them, and re-layouts  17.5 us (7%)
  between operations  14.1 us (5%)
  matrix products  10.3 us (4%)
  other arithmetic  6.8 us (3%)
    all_gather x1, waiting for transfers between devices, per_device(): gathered = lax.all_gather(rounded_down_value, 'group', axis=0, tiled=True)  71.9 us
    all_to_all x1, waiting for transfers between devices, per_device(): lax.all_to_all(partial_value, 'expert', split_axis=0, concat_axis=0, tile...  53.6 us
    all_to_all x1, waiting for transfers between devices, per_device(): lax.all_to_all(ordered, 'expert', split_axis=0, concat_axis=1, tiled=True)  39.1 us
    all_to_all x1, starting transfers between devices, per_device(): lax.all_to_all(dispatch, 'expert', split_axis=0, concat_axis=0, tiled=True)  20 us
    all_to_all x1, starting transfers between devices, per_device(): lax.all_to_all(ordered, 'expert', split_axis=0, concat_axis=1, tiled=True)  13.4 us
    all_to_all x1, starting transfers between devices, per_device(): lax.all_to_all(partial_value, 'expert', split_axis=0, concat_axis=0, tile...  8.77 us
  transfers between devices with their start and end apart: 4, of which 3 were waited for; matrix products, arithmetic and copies ran while one was open for 5% of the time, Pallas kernels for 0%

commit v1 on v0

v1 whole, which is shorter than its diff:
```python
import jax
import jax.numpy as jnp
from jax import lax
from jax.experimental import pallas as pl
from jax.experimental.pallas import tpu as pltpu
from jax.sharding import Mesh, PartitionSpec as P

adam_step = 1000.0
adam_eps = 1e-08
learn_rate = 0.005
weight_decay = 0.1
beta_one = 0.9
beta_two = 0.999

GROUPS, YS, ZHS, XS, CORES = 4, 8, 2, 4, 2
ALONG = ("y", "zh", "x", "c")
EXPERT_COUNT = 16
EXTRA = 128


def pick_slabs(order, parts):
    count, rows, cols = parts[0].shape
    total = count * len(parts)

    def kernel(order_ref, a, b, c, d, out_ref, held, sems):
        copies = [
            pltpu.make_async_copy(ref, held.at[pl.ds(k * count, count)], sems.at[k])
            for k, ref in enumerate((a, b, c, d))
        ]
        for copy in copies:
            copy.start()
        for copy in copies:
            copy.wait()

        def body(i, _):
            out_ref[i] = held[order_ref[i]]
            return 0

        lax.fori_loop(0, total, body, 0, unroll=8)

    return pl.pallas_call(
        kernel,
        out_shape=jax.ShapeDtypeStruct((total, rows, cols), parts[0].dtype),
        in_specs=[pl.BlockSpec(memory_space=pltpu.SMEM)] + [pl.BlockSpec(memory_space=pl.ANY)] * 4,
        out_specs=pl.BlockSpec(memory_space=pltpu.VMEM),
        scratch_shapes=[
            pltpu.VMEM((total, rows, cols), parts[0].dtype),
            pltpu.SemaphoreType.DMA((4,)),
        ],
        compiler_params=pltpu.CompilerParams(vmem_limit_bytes=16 * 2**20),
    )(order, *parts)


def hidden_and_down(expert_id, rows_ext, weights):
    row_count = rows_ext.shape[0]
    depth = weights.shape[0]
    plane = XS * CORES
    piece = depth // plane

    def kernel(expert_ref, rows_ref, w_ref, out_ref):
        gate_up = jnp.dot(
            rows_ref[:, :depth], w_ref[:, :256], preferred_element_type=jnp.float32
        )
        gate, up = gate_up[:, :128], gate_up[:, 128:]
        hidden = (gate / (1.0 + jnp.exp(-gate)) * up).astype(jnp.bfloat16).astype(jnp.float32)
        lane = lax.broadcasted_iota(jnp.int32, (row_count, EXTRA), 1)
        own = (lane == expert_ref[0]) | (lane == expert_ref[0] + EXPERT_COUNT)
        extra = rows_ref[:, depth:].astype(jnp.float32)
        coefficient = jnp.sum(jnp.where(own, extra, 0.0), axis=1, keepdims=True)
        scaled = (hidden * coefficient).astype(jnp.bfloat16)
        for k in range(plane):
            out_ref[k, :row_count, :] = scaled
            out_ref[k, row_count:, :] = w_ref[k * piece : (k + 1) * piece, 256:]

    return pl.pallas_call(
        kernel,
        out_shape=jax.ShapeDtypeStruct((plane, row_count + piece, 128), jnp.bfloat16),
        in_specs=[pl.BlockSpec(memory_space=pltpu.SMEM)] + [pl.BlockSpec(memory_space=pltpu.VMEM)] * 2,
        out_specs=pl.BlockSpec(memory_space=pltpu.VMEM),
        compiler_params=pltpu.CompilerParams(vmem_limit_bytes=32 * 2**20),
    )(expert_id, rows_ext, weights)


def down_sum(blocks, row_count):
    plane, both, width = blocks.shape
    piece = both - row_count

    def kernel(ref, out_ref):
        total = jnp.zeros((row_count, piece), jnp.float32)
        for k in range(plane):
            total += lax.dot_general(
                ref[k, :row_count, :],
                ref[k, row_count:, :],
                (((1,), (1,)), ((), ())),
                preferred_element_type=jnp.float32,
            )
        out_ref[...] = total.astype(jnp.bfloat16)

    return pl.pallas_call(
        kernel,
        out_shape=jax.ShapeDtypeStruct((row_count, piece), jnp.bfloat16),
        in_specs=[pl.BlockSpec(memory_space=pltpu.VMEM)],
        out_specs=pl.BlockSpec(memory_space=pltpu.VMEM),
        compiler_params=pltpu.CompilerParams(vmem_limit_bytes=32 * 2**20),
    )(blocks)


def per_device(
    master_weights,
    first_moment,
    second_moment,
    gradient,
    placement,
    tokens,
    routed_expert_index,
    gate_weights,
):
    group = lax.axis_index("g")
    place = lax.axis_index(ALONG)
    row_count, depth = tokens.shape[1:]

    experts = jnp.arange(EXPERT_COUNT, dtype=jnp.int32)
    named = routed_expert_index[0][:, :, None] == experts[None, None, :]
    coefficient = jnp.sum(jnp.where(named, gate_weights[0][:, :, None], 0.0), axis=1)
    high = coefficient.astype(jnp.bfloat16)
    low = (coefficient - high.astype(jnp.float32)).astype(jnp.bfloat16)
    fill = jnp.zeros((row_count, EXTRA - 2 * EXPERT_COUNT), jnp.bfloat16)
    own_rows = jnp.concatenate([tokens[0], high, low, fill], axis=1)
    spread = jnp.broadcast_to(own_rows[None], (YS * ZHS,) + own_rows.shape)
    some_rows = lax.all_to_all(spread, ("y", "zh"), split_axis=0, concat_axis=0, tiled=True)
    all_rows = lax.all_gather(some_rows, ("x", "c"), axis=0, tiled=False)
    all_rows = all_rows.transpose(1, 0, 2, 3).reshape(-1, depth + EXTRA)

    grad_float = gradient.astype(jnp.float32)
    first_new = beta_one * first_moment + (1.0 - beta_one) * grad_float
    second_new = beta_two * second_moment + (1.0 - beta_two) * grad_float * grad_float
    update = (
        first_new
        / (1.0 - beta_one**adam_step)
        / (jnp.sqrt(second_new / (1.0 - beta_two**adam_step)) + adam_eps)
    )
    master_out = master_weights - learn_rate * (update + weight_decay * master_weights)
    rounded = master_out.astype(jnp.bfloat16)

    parts = [rounded] + [
        lax.ppermute(rounded, "g", [(i, (i + s) % GROUPS) for i in range(GROUPS)])
        for s in range(1, GROUPS)
    ]
    unit_count = placement.shape[1]
    per_group = unit_count // GROUPS
    unit_ids = jnp.arange(unit_count, dtype=jnp.int32)
    own_row = lax.dynamic_index_in_dim(placement, group, 0, keepdims=False)
    matches = own_row[:, None] == unit_ids[None, :]
    holder = jnp.sum(jnp.where(matches, unit_ids[:, None], 0), axis=0)
    order = ((group - holder // per_group) % GROUPS) * per_group + holder % per_group
    ordered = pick_slabs(order, parts)
    own_slab = lax.all_to_all(ordered, ALONG, split_axis=0, concat_axis=0, tiled=True)
    weights = own_slab.reshape(depth, -1)
    rollout_out = weights[None, None]

    slabs_each = unit_count // EXPERT_COUNT
    expert_id = jnp.sum(jnp.where(unit_ids == place, holder, 0), keepdims=True) // slabs_each
    blocks = hidden_and_down(expert_id, all_rows, weights)
    blocks = lax.all_to_all(blocks, ("x", "c"), split_axis=0, concat_axis=0, tiled=True)
    partial = down_sum(blocks, all_rows.shape[0])
    piece = partial.shape[1]
    lanes = piece // 128
    chunks = partial.reshape(unit_count, row_count, lanes, 128).transpose(0, 2, 1, 3)
    chunks = chunks.reshape(unit_count, lanes * row_count, 128)
    returned = lax.all_to_all(chunks, ALONG, split_axis=0, concat_axis=0, tiled=True)
    returned = returned.reshape(YS * ZHS, XS * CORES, lanes, row_count, 128)
    decoded = jnp.sum(returned.astype(jnp.float32), axis=0)
    decoded = decoded.transpose(2, 0, 1, 3).reshape(1, row_count, depth)
    return (master_out, rollout_out, decoded.astype(jnp.bfloat16))


def solution(mesh):
    names = ("g",) + ALONG
    fine = Mesh(mesh.devices.reshape(GROUPS, YS, ZHS, XS, CORES), names)
    split = P("g", ALONG, None)
    return jax.shard_map(
        per_device,
        mesh=fine,
        in_specs=(split, split, split, split, P(), split, split, split),
        out_specs=(split, P("g", ALONG, None, None), split),
        check_vma=False,
    )
```

time: 258 us -> 202 us (0.78)
  the two profiles are of different devices: /device:TPU:6 before, /device:TPU:1 now
where the time goes in v1:
time: 202 us; the launch traced here: 201 us
  waiting for transfers between devices  75.6 us (37%)
  blocking collectives  57.3 us (28%)
  starting transfers between devices  28 us (14%)
  between operations  16.8 us (8%)
  local copies, waits for them, and re-layouts  14.8 us (7%)
  other arithmetic  4.52 us (2%)
  Pallas kernels  4.25 us (2%)
    all_to_all x1, waiting for transfers between devices, per_device(): lax.all_to_all(ordered, ALONG, split_axis=0, concat_axis=0, tiled=True)  31.1 us
    all_to_all x1, blocking collectives, per_device(): lax.all_to_all(spread, ('y', 'zh'), split_axis=0, concat_axis=0, tiled=True)  30.7 us
    all_to_all x1, blocking collectives, per_device(): lax.all_to_all(blocks, ('x', 'c'), split_axis=0, concat_axis=0, tiled=True)  26.6 us
    ppermute x3, waiting for transfers between devices, per_device(): lax.ppermute(rounded, 'g', [(i, (i + s) % GROUPS) for i in range(GROUPS)])  26.1 us
    all_to_all x1, waiting for transfers between devices, per_device(): lax.all_to_all(chunks, ALONG, split_axis=0, concat_axis=0, tiled=True)  18.3 us
    all_to_all x1, starting transfers between devices, per_device(): lax.all_to_all(ordered, ALONG, split_axis=0, concat_axis=0, tiled=True)  12.1 us
    ppermute x3, starting transfers between devices, per_device(): lax.ppermute(rounded, 'g', [(i, (i + s) % GROUPS) for i in range(GROUPS)])  9.28 us
    all_to_all x1, starting transfers between devices, per_device(): lax.all_to_all(chunks, ALONG, split_axis=0, concat_axis=0, tiled=True)  6.57 us
  transfers between devices with their start and end apart: 6, of which 4 were waited for; matrix products, arithmetic and copies ran while one was open for 6% of the time, Pallas kernels for 1%

profile of v1, /device:TPU:1, one launch (start us, length us, event | category | flops | bytes accessed | tf_op | source)
XLA Modules:
  0.0 201.2 jit_solution(3557429796839574303)
XLA Ops:
  7.2 0.0 copy-start
  7.2 0.0 copy-start.3
  7.2 0.0 copy-start.2
  7.2 0.0 all-gather.3.cloned.1.call-start
  7.2 0.9 select_reduce_fusion.1
  8.2 0.8 concatenate.3
  9.0 0.1 broadcast_in_dim.51
  9.1 30.7 %all_to_all.20 = bf16[16,4,2176]{2,1,0:T(4,128)(2,1)S(1)} all-to-all(bf16[16,4,2176]{2,1,0:T(4,128)(2,1)S(1)} %broadcast_in_dim.51), channel_id=1, replica_groups=mesh['g'=4,'y'=8,'zh'=2,'x'=4,'c'=2] {'y','zh'}, dimensions={0} | all-to-all | bytes 557056 | tf_op jit(solution)/shard_map/all_to_all | solution.py:130
  39.8 0.7 copy.24
  40.5 0.0 all-gather.3.cloned.1.call-update
  40.5 0.0 copy-done.3
  40.5 0.0 copy-done.2
  40.5 2.8 %fusion.13 = (bf16[32,16,384]{2,1,0:T(8,128)(2,1)S(1)}, f32[32,16,384]{2,1,0:T(8,128)}) fusion(f32[32,16,384]{2,1,0:T(8,128)S(1)} %copy-done.2, f32[32,16,384]{2,1,0:T(8,128)S(1)} %copy-done.3, bf16[32,16,384]{2,1,0:T(8,128)(2,1)} %param.11, f32[32,16,384]{2,1,0:T(8,128)} %param.9), kind=kLoop, calls=%fused_computation.31 | loop fusion | flops 3145728 | bytes 3932160 | tf_op jit(solution)/shard_map/convert_element_type | solution.py:143
  43.3 4.9 %collective-permute-start.2 = (bf16[32,16,384]{2,1,0:T(8,128)(2,1)S(1)}, bf16[32,16,384]{2,1,0:T(8,128)(2,1)S(1)}, u32[]{:S(2)}, u32[]{:S(2)}) collective-permute-start(bf16[32,16,384]{2,1,0:T(8,128)(2,1)S(1)} %get-tuple-element.5.a), channel_id=1, source_target_pairs={{0,384},{128,0},{256,128},{384,256},{1,385},{129,1},{257,129},{385... | collective-permute-start | bytes 1179656 | tf_op jit(solution)/shard_map/ppermute | solution.py:146
  48.2 1.9 collective-permute-start.1
  50.1 2.5 %collective-permute-start = (bf16[32,16,384]{2,1,0:T(8,128)(2,1)S(1)}, bf16[32,16,384]{2,1,0:T(8,128)(2,1)S(1)}, u32[]{:S(2)}, u32[]{:S(2)}) collective-permute-start(bf16[32,16,384]{2,1,0:T(8,128)(2,1)S(1)} %get-tuple-element.5.a), channel_id=1, source_target_pairs={{0,128},{128,256},{256,384},{384,0},{1,129},{129,257},{257,385},{3... | collective-permute-start | bytes 1179656 | tf_op jit(solution)/shard_map/ppermute | solution.py:146
  52.6 0.0 copy-done
  52.6 0.1 select_reduce_fusion
  52.7 0.6 fusion.11
  53.4 0.8 collective-permute-done.2.d
  54.2 25.3 %collective-permute-done.1.c = bf16[32,16,384]{2,1,0:T(8,128)(2,1)S(1)} collective-permute-done((bf16[32,16,384]{2,1,0:T(8,128)(2,1)S(1)}, bf16[32,16,384]{2,1,0:T(8,128)(2,1)S(1)}, u32[]{:S(2)}, u32[]{:S(2)}) %collective-permute-start.1) | collective-permute-done | bytes 393248 | tf_op jit(solution)/shard_map/ppermute | solution.py:146
  79.5 0.0 collective-permute-done.b
  79.5 2.8 %shard_map.103 = bf16[128,16,384]{2,1,0:T(8,128)(2,1)} custom-call(s32[128]{0:T(128)S(1)} %get-tuple-element.8.order_ref, bf16[32,16,384]{2,1,0:T(8,128)(2,1)S(1)} %get-tuple-element.5.a, bf16[32,16,384]{2,1,0:T(8,128)(2,1)S(1)} %collective-permute-done.b, bf16[32,16,384]{2,1,0:T(8,128)(2,1)S(1)} %collective-permute-done.1.c, ...), custom_call_target="tpu_custom_call" | custom-call | tf_op jit(solution)/shard_map/pallas_call | solution.py:41
  82.3 12.1 %all-to-all-start = ((bf16[128,16,384]{2,1,0:T(8,128)(2,1)}), bf16[128,16,384]{2,1,0:T(8,128)(2,1)S(1)}, u32[]{:S(2)}, u32[]{:S(2)}) async-start(bf16[128,16,384]{2,1,0:T(8,128)(2,1)} %shard_map.103), calls=%async_computation | async-start | bytes 3145728 | tf_op jit(solution)/shard_map/all_to_all | solution.py:157
  97.0 0.0 all-gather.3.cloned.1.call-done
  97.0 4.7 %copy.25 = bf16[16,8,4,2176]{3,2,1,0:T(4,128)(2,1)} copy(bf16[16,8,4,2176]{3,0,1,2:T(8,128)(2,1)} %bitcast.20) | data formatting | bytes 4456448 | tf_op jit(solution)/shard_map/transpose | solution.py:132
  101.7 4.0 %reshape.44.rows_ref = bf16[512,2176]{1,0:T(8,128)(2,1)} reshape(bf16[16,8,4,2176]{3,2,1,0:T(4,128)(2,1)} %copy.25) | data formatting | bytes 4456448 | tf_op jit(solution)/shard_map/reshape | solution.py:132
  105.7 31.1 %all-to-all-done = bf16[128,16,384]{2,1,0:T(8,128)(2,1)S(1)} async-done(((bf16[128,16,384]{2,1,0:T(8,128)(2,1)}), bf16[128,16,384]{2,1,0:T(8,128)(2,1)S(1)}, u32[]{:S(2)}, u32[]{:S(2)}) %all-to-all-start) | async-done | bytes 1572896 | tf_op jit(solution)/shard_map/all_to_all | solution.py:157
  136.8 0.0 copy-start.1
  136.8 1.6 copy-done.1
  138.5 0.8 shard_map.104
  139.2 26.6 %all_to_all.21.ref = bf16[8,768,128]{2,1,0:T(8,128)(2,1)S(1)} all-to-all(bf16[8,768,128]{2,1,0:T(8,128)(2,1)S(1)} %shard_map.104), channel_id=1, replica_groups=mesh['g'=4,'y'=8,'zh'=2,'x'=4,'c'=2] {'x','c'}, dimensions={0} | all-to-all | bytes 3145728 | tf_op jit(solution)/shard_map/all_to_all | solution.py:164
  165.9 0.7 shard_map.105
  166.6 0.1 reshape.46
  166.7 0.9 copy.27
  167.6 6.6 %all-to-all-start.3 = ((bf16[128,8,128]{2,1,0:T(8,128)(2,1)}), bf16[128,8,128]{2,1,0:T(8,128)(2,1)S(1)}, u32[]{:S(2)}, u32[]{:S(2)}) async-start(bf16[128,8,128]{2,1,0:T(8,128)(2,1)} %copy.27), calls=%async_computation.3 | async-start | bytes 524288 | tf_op jit(solution)/shard_map/all_to_all | solution.py:170
  174.1 18.3 %all-to-all-done.3 = bf16[128,8,128]{2,1,0:T(8,128)(2,1)S(1)} async-done(((bf16[128,8,128]{2,1,0:T(8,128)(2,1)}), bf16[128,8,128]{2,1,0:T(8,128)(2,1)S(1)}, u32[]{:S(2)}, u32[]{:S(2)}) %all-to-all-start.3) | async-done | bytes 262176 | tf_op jit(solution)/shard_map/all_to_all | solution.py:170
  192.5 0.1 reduce
  192.6 0.6 convert_element_type.47
  193.2 1.1 copy.34
  (6 shorter events, 0.1 us)
Async XLA Ops:
  7.2 45.5 %copy-start = (s32[4,128]{1,0:T(4,128)S(1)}, s32[4,128]{1,0:T(4,128)}, u32[]{:S(2)}) copy-start(s32[4,128]{1,0:T(4,128)} %param.12) | copy-start | bytes 6148
  7.2 33.3 %copy-start.3 = (f32[32,16,384]{2,1,0:T(8,128)S(1)}, f32[32,16,384]{2,1,0:T(8,128)}, u32[]{:S(2)}) copy-start(f32[32,16,384]{2,1,0:T(8,128)} %param.10) | copy-start | bytes 2359300
  7.2 33.3 %copy-start.2 = (f32[32,16,384]{2,1,0:T(8,128)S(1)}, f32[32,16,384]{2,1,0:T(8,128)}, u32[]{:S(2)}) copy-start(f32[32,16,384]{2,1,0:T(8,128)} %param.8) | copy-start | bytes 2359300
  7.2 89.8 %all-gather.3.cloned.1.call-start = ((), (), s32[]{:S(2)}) async-start(), calls=%async_computation.4 | async-start | bytes 2506752 | tf_op jit(solution)/shard_map/all_gather | solution.py:131
  43.3 10.9 %collective-permute-start.2 = (bf16[32,16,384]{2,1,0:T(8,128)(2,1)S(1)}, bf16[32,16,384]{2,1,0:T(8,128)(2,1)S(1)}, u32[]{:S(2)}, u32[]{:S(2)}) collective-permute-start(bf16[32,16,384]{2,1,0:T(8,128)(2,1)S(1)} %get-tuple-element.5.a), channel_id=1, source_target_pairs={{0,384},{128,0},{256,128},{384,256},{1,385},{129,1},{257,129},{385... | collective-permute-start | bytes 1179656 | tf_op jit(solution)/shard_map/ppermute | solution.py:146
  48.2 31.3 %collective-permute-start.1 = (bf16[32,16,384]{2,1,0:T(8,128)(2,1)S(1)}, bf16[32,16,384]{2,1,0:T(8,128)(2,1)S(1)}, u32[]{:S(2)}, u32[]{:S(2)}) collective-permute-start(bf16[32,16,384]{2,1,0:T(8,128)(2,1)S(1)} %get-tuple-element.5.a), channel_id=1, source_target_pairs={{0,256},{128,384},{256,0},{384,128},{1,257},{129,385},{257,1},{385... | collective-permute-start | bytes 1179656 | tf_op jit(solution)/shard_map/ppermute | solution.py:146
  50.1 29.4 %collective-permute-start = (bf16[32,16,384]{2,1,0:T(8,128)(2,1)S(1)}, bf16[32,16,384]{2,1,0:T(8,128)(2,1)S(1)}, u32[]{:S(2)}, u32[]{:S(2)}) collective-permute-start(bf16[32,16,384]{2,1,0:T(8,128)(2,1)S(1)} %get-tuple-element.5.a), channel_id=1, source_target_pairs={{0,128},{128,256},{256,384},{384,0},{1,129},{129,257},{257,385},{3... | collective-permute-start | bytes 1179656 | tf_op jit(solution)/shard_map/ppermute | solution.py:146
  82.3 54.6 %all-to-all-start = ((bf16[128,16,384]{2,1,0:T(8,128)(2,1)}), bf16[128,16,384]{2,1,0:T(8,128)(2,1)S(1)}, u32[]{:S(2)}, u32[]{:S(2)}) async-start(bf16[128,16,384]{2,1,0:T(8,128)(2,1)} %shard_map.103), calls=%async_computation | async-start | bytes 3145728 | tf_op jit(solution)/shard_map/all_to_all | solution.py:157
  136.8 1.6 copy-start.1
  167.6 24.9 %all-to-all-start.3 = ((bf16[128,8,128]{2,1,0:T(8,128)(2,1)}), bf16[128,8,128]{2,1,0:T(8,128)(2,1)S(1)}, u32[]{:S(2)}, u32[]{:S(2)}) async-start(bf16[128,8,128]{2,1,0:T(8,128)(2,1)} %copy.27), calls=%async_computation.3 | async-start | bytes 524288 | tf_op jit(solution)/shard_map/all_to_all | solution.py:170
Sparse Core Ops, SparseCore 0:
  40.6 27.4 all-gather.2

commit v2 on v1

v2 whole, which is shorter than its diff:
```python
import jax
import jax.numpy as jnp
from jax import lax
from jax.experimental import pallas as pl
from jax.experimental.pallas import tpu as pltpu
from jax.sharding import Mesh, PartitionSpec as P

adam_step = 1000.0
adam_eps = 1e-08
learn_rate = 0.005
weight_decay = 0.1
beta_one = 0.9
beta_two = 0.999

GROUPS, YS, ZHS, XS, CORES = 4, 8, 2, 4, 2
ALONG = ("y", "zh", "x", "c")
EXPERT_COUNT = 16
EXTRA = 128


def place_slabs(places, parts):
    count, rows, cols = parts[0].shape
    total = count * len(parts)

    def kernel(places_ref, a, b, c, d, out_ref):
        for k, ref in enumerate((a, b, c, d)):

            def body(i, _, k=k, ref=ref):
                out_ref[places_ref[k * count + i]] = ref[i]
                return 0

            lax.fori_loop(0, count, body, 0, unroll=8)

    return pl.pallas_call(
        kernel,
        out_shape=jax.ShapeDtypeStruct((total, rows, cols), parts[0].dtype),
        in_specs=[pl.BlockSpec(memory_space=pltpu.SMEM)] + [pl.BlockSpec(memory_space=pltpu.VMEM)] * 4,
        out_specs=pl.BlockSpec(memory_space=pltpu.VMEM),
        compiler_params=pltpu.CompilerParams(vmem_limit_bytes=16 * 2**20),
    )(places, *parts)


def hidden_units(numbers, rows_ext, weights):
    row_count = rows_ext.shape[0]
    depth, cols = weights.shape
    half = row_count // CORES
    blocks = 4
    block = row_count // blocks

    def kernel(numbers_ref, rows_hbm, w_ref, send_ref, keep_ref, slab_hbm, rows_ref, scaled_ref, row_sems, slab_sem):
        copies = [
            pltpu.make_async_copy(
                rows_hbm.at[pl.ds(k * block, block)], rows_ref.at[pl.ds(k * block, block)], row_sems.at[k]
            )
            for k in range(blocks)
        ]
        for copy in copies:
            copy.start()
        slab_copy = pltpu.make_async_copy(w_ref, slab_hbm, slab_sem)
        slab_copy.start()
        send_ref[half:, :] = w_ref[:, 256:]
        expert = numbers_ref[0]
        core = numbers_ref[1]
        for k in range(blocks):
            copies[k].wait()
            span = slice(k * block, (k + 1) * block)
            gate_up = jnp.dot(
                rows_ref[span, :depth], w_ref[:, :256], preferred_element_type=jnp.float32
            )
            gate, up = gate_up[:, :128], gate_up[:, 128:]
            hidden = (gate / (1.0 + jnp.exp(-gate)) * up).astype(jnp.bfloat16).astype(jnp.float32)
            lane = lax.broadcasted_iota(jnp.int32, (block, EXTRA), 1)
            own = (lane == expert) | (lane == expert + EXPERT_COUNT)
            extra = rows_ref[span, depth:].astype(jnp.float32)
            coefficient = jnp.sum(jnp.where(own, extra, 0.0), axis=1, keepdims=True)
            scaled_ref[span, :] = (hidden * coefficient).astype(jnp.bfloat16)
        at = lax.broadcasted_iota(jnp.int32, (half, row_count), 0)
        of = lax.broadcasted_iota(jnp.int32, (half, row_count), 1)
        each, column = row_count // (XS * CORES * YS * ZHS), YS * ZHS
        row = at % each
        x = at // each % XS
        y_zh = at // (each * XS)
        base = x * CORES * column * each + y_zh * each + row

        def rows_of(k):
            pick = jnp.where(of == base + k * (column * each), 1.0, 0.0).astype(jnp.bfloat16)
            return jnp.dot(pick, scaled_ref[...], preferred_element_type=jnp.float32).astype(jnp.bfloat16)

        send_ref[:half, :] = rows_of(1 - core)
        keep_ref[...] = rows_of(core)
        slab_copy.wait()

    return pl.pallas_call(
        kernel,
        out_shape=(
            jax.ShapeDtypeStruct((half + depth, 128), jnp.bfloat16),
            jax.ShapeDtypeStruct((half, 128), jnp.bfloat16),
            jax.ShapeDtypeStruct((depth, cols), jnp.bfloat16),
        ),
        in_specs=[
            pl.BlockSpec(memory_space=pltpu.SMEM),
            pl.BlockSpec(memory_space=pltpu.HBM),
            pl.BlockSpec(memory_space=pltpu.VMEM),
        ],
        out_specs=(
            pl.BlockSpec(memory_space=pltpu.VMEM),
            pl.BlockSpec(memory_space=pltpu.VMEM),
            pl.BlockSpec(memory_space=pltpu.HBM),
        ),
        scratch_shapes=[
            pltpu.VMEM(rows_ext.shape, jnp.bfloat16),
            pltpu.VMEM((row_count, 128), jnp.bfloat16),
            pltpu.SemaphoreType.DMA((blocks,)),
            pltpu.SemaphoreType.DMA,
        ],
        compiler_params=pltpu.CompilerParams(vmem_limit_bytes=52 * 2**20),
    )(numbers, rows_ext, weights)


def pair_outputs(keep, weights, received):
    half = keep.shape[0]
    depth = weights.shape[0]
    chips = half // 4
    lanes = depth // 128

    def kernel(keep_ref, w_ref, recv_ref, out_ref, part_ref):
        across = (((1,), (1,)), ((), ()))
        for k in range(4):
            span = slice(k * depth // 4, (k + 1) * depth // 4)
            part_ref[:, span] = lax.dot_general(
                keep_ref[...], w_ref[span, 256:], across, preferred_element_type=jnp.float32
            ) + lax.dot_general(
                recv_ref[:half, :],
                recv_ref[half + span.start : half + span.stop, :],
                across,
                preferred_element_type=jnp.float32,
            )
        low = lax.broadcasted_iota(jnp.int32, (chips // 2, 8, 128), 1) < 4

        def tile(q):
            return part_ref[:, q * 128 : (q + 1) * 128].reshape(chips // 2, 8, 128)

        for q in range(0, lanes, 4):
            first, second = [], []
            for p in (q, q + 2):
                a, b = tile(p), tile(p + 1)
                first.append(jnp.where(low, a, pltpu.roll(b, 4, 1)))
                second.append(jnp.where(low, pltpu.roll(a, 4, 1), b))
            out_ref[:, 0, 4 * q : 4 * q + 16, :] = jnp.concatenate(first, axis=1).astype(jnp.bfloat16)
            out_ref[:, 1, 4 * q : 4 * q + 16, :] = jnp.concatenate(second, axis=1).astype(jnp.bfloat16)

    out = pl.pallas_call(
        kernel,
        out_shape=jax.ShapeDtypeStruct((chips // 2, 2, 4 * lanes, 128), jnp.bfloat16),
        in_specs=[pl.BlockSpec(memory_space=pltpu.VMEM)] * 3,
        out_specs=pl.BlockSpec(memory_space=pltpu.VMEM),
        scratch_shapes=[pltpu.VMEM((half, depth), jnp.float32)],
        compiler_params=pltpu.CompilerParams(vmem_limit_bytes=32 * 2**20),
    )(keep, weights, received)
    return out.reshape(chips, 4 * lanes, 128)


def sum_chunks(chunks):
    count, tall, _ = chunks.shape
    lanes = tall // 4

    def kernel(ref, out_ref):
        total = ref[0].astype(jnp.float32)
        for k in range(1, count):
            total += ref[k].astype(jnp.float32)
        out_ref[...] = jnp.concatenate(
            [total[4 * q : 4 * q + 4, :] for q in range(lanes)], axis=1
        ).astype(jnp.bfloat16)

    return pl.pallas_call(
        kernel,
        out_shape=jax.ShapeDtypeStruct((4, lanes * 128), jnp.bfloat16),
        in_specs=[pl.BlockSpec(memory_space=pltpu.VMEM)],
        out_specs=pl.BlockSpec(memory_space=pltpu.VMEM),
        compiler_params=pltpu.CompilerParams(vmem_limit_bytes=32 * 2**20),
    )(chunks)


def per_device(
    master_weights,
    first_moment,
    second_moment,
    gradient,
    placement,
    tokens,
    routed_expert_index,
    gate_weights,
):
    group = lax.axis_index("g")
    core = lax.axis_index("c")
    place = lax.axis_index(ALONG)
    row_count, depth = tokens.shape[1:]

    grad_float = gradient.astype(jnp.float32)
    first_new = beta_one * first_moment + (1.0 - beta_one) * grad_float
    second_new = beta_two * second_moment + (1.0 - beta_two) * grad_float * grad_float
    update = (
        first_new
        / (1.0 - beta_one**adam_step)
        / (jnp.sqrt(second_new / (1.0 - beta_two**adam_step)) + adam_eps)
    )
    master_out = master_weights - learn_rate * (update + weight_decay * master_weights)
    rounded = master_out.astype(jnp.bfloat16)

    experts = jnp.arange(EXPERT_COUNT, dtype=jnp.int32)
    named = routed_expert_index[0][:, :, None] == experts[None, None, :]
    coefficient = jnp.sum(jnp.where(named, gate_weights[0][:, :, None], 0.0), axis=1)
    high = coefficient.astype(jnp.bfloat16)
    low = (coefficient - high.astype(jnp.float32)).astype(jnp.bfloat16)
    fill = jnp.zeros((row_count, EXTRA - 2 * EXPERT_COUNT), jnp.bfloat16)
    own_rows = jnp.concatenate([tokens[0], high, low, fill], axis=1)
    spread = jnp.broadcast_to(own_rows[None], (YS * ZHS,) + own_rows.shape)
    rounded, spread = lax.optimization_barrier((rounded, spread))

    parts = [rounded] + [
        lax.ppermute(rounded, "g", [(i, (i + s) % GROUPS) for i in range(GROUPS)])
        for s in range(1, GROUPS)
    ]
    some_rows = lax.all_to_all(spread, ("y", "zh"), split_axis=0, concat_axis=0, tiled=True)
    some_rows = some_rows.reshape(-1, depth + EXTRA)
    parts, _ = lax.optimization_barrier((parts, some_rows))

    unit_count = placement.shape[1]
    unit_ids = jnp.arange(unit_count, dtype=jnp.int32)
    own_row = lax.dynamic_index_in_dim(placement, group, 0, keepdims=False)
    by_group = own_row.reshape(GROUPS, -1)
    places = jnp.take(by_group, (group - jnp.arange(GROUPS)) % GROUPS, axis=0).reshape(-1)
    ordered = place_slabs(places, parts)
    own_slab = lax.all_to_all(ordered, ALONG, split_axis=0, concat_axis=0, tiled=True)
    weights = own_slab.reshape(depth, -1)

    all_rows = lax.all_gather(some_rows, ("x", "c"), axis=0, tiled=True)

    slabs_each = unit_count // EXPERT_COUNT
    expert_id = jnp.sum(jnp.where(own_row == place, unit_ids, 0)) // slabs_each
    numbers = jnp.stack([expert_id, core]).astype(jnp.int32)
    send, keep, slab = hidden_units(numbers, all_rows, weights)
    received = lax.ppermute(send, "c", [(0, 1), (1, 0)])
    chunks = pair_outputs(keep, weights, received)
    chunks = lax.all_to_all(chunks, ("y", "zh", "x"), split_axis=0, concat_axis=0, tiled=True)
    decoded = sum_chunks(chunks)
    return (master_out, slab[None, None], decoded[None])


def solution(mesh):
    names = ("g",) + ALONG
    fine = Mesh(mesh.devices.reshape(GROUPS, YS, ZHS, XS, CORES), names)
    split = P("g", ALONG, None)
    return jax.shard_map(
        per_device,
        mesh=fine,
        in_specs=(split, split, split, split, P(), split, split, split),
        out_specs=(split, P("g", ALONG, None, None), split),
        check_vma=False,
    )
```

time: 202 us -> 195 us (0.965)
  the two profiles are of different devices: /device:TPU:1 before, /device:TPU:6 now
where the time goes in v2:
time: 195 us
  blocking collectives  70.9 us (36%)
  waiting for transfers between devices  67.8 us (35%)
  starting transfers between devices  21.3 us (11%)
  between operations  16.6 us (9%)
  Pallas kernels  8.38 us (4%)
  local copies, waits for them, and re-layouts  5.02 us (3%)
  other arithmetic  4.86 us (2%)
    all_to_all x1, waiting for transfers between devices, per_device(): lax.all_to_all(ordered, ALONG, split_axis=0, concat_axis=0, tiled=True)  39.8 us
    all_to_all x1, blocking collectives, per_device(): lax.all_to_all(chunks, ('y', 'zh', 'x'), split_axis=0, concat_axis=0, til...  39.1 us
    all_to_all x1, blocking collectives, per_device(): lax.all_to_all(spread, ('y', 'zh'), split_axis=0, concat_axis=0, tiled=True)  31.8 us
    ppermute x3, waiting for transfers between devices, per_device(): lax.ppermute(rounded, 'g', [(i, (i + s) % GROUPS) for i in range(GROUPS)])  26 us
    ppermute x3, starting transfers between devices, per_device(): lax.ppermute(rounded, 'g', [(i, (i + s) % GROUPS) for i in range(GROUPS)])  10.1 us
    all_to_all x1, starting transfers between devices, per_device(): lax.all_to_all(ordered, ALONG, split_axis=0, concat_axis=0, tiled=True)  9.13 us
    pallas_call x1, Pallas kernels, hidden_units(): pl.pallas_call(kernel, out_shape=(jax.ShapeDtypeStruct((half + depth, 128...  4.93 us
  transfers between devices with their start and end apart: 6, of which 4 were waited for; matrix products, arithmetic and copies ran while one was open for 1% of the time, Pallas kernels for 1%

profile of v2, /device:TPU:6, one launch (start us, length us, event | category | flops | bytes accessed | tf_op | source)
XLA Modules:
  0.0 194.8 jit_solution(5811869240648190911)
XLA Ops:
  7.2 0.0 all-gather.2.cloned.1.call-start
  7.2 0.8 select_reduce_fusion
  8.0 0.8 concatenate.3
  8.8 3.2 %fusion.14 = (bf16[32,16,384]{2,1,0:T(8,128)(2,1)S(1)}, f32[32,16,384]{2,1,0:T(8,128)}) fusion(f32[32,16,384]{2,1,0:T(8,128)} %param.8, f32[32,16,384]{2,1,0:T(8,128)} %param.10, bf16[32,16,384]{2,1,0:T(8,128)(2,1)} %param.11, f32[32,16,384]{2,1,0:T(8,128)} %param.9), kind=kLoop, calls=%fused_computation.34 | loop fusion | flops 3145728 | bytes 3932160 | tf_op jit(solution)/shard_map/convert_element_type | solution.py:208
  12.0 0.0 copy-start.2
  12.0 0.1 broadcast_in_dim.49
  12.1 31.8 %all_to_all.15 = bf16[16,4,2176]{2,1,0:T(4,128)(2,1)S(1)} all-to-all(bf16[16,4,2176]{2,1,0:T(4,128)(2,1)S(1)} %broadcast_in_dim.49), channel_id=1, replica_groups=mesh['g'=4,'y'=8,'zh'=2,'x'=4,'c'=2] {'y','zh'}, dimensions={0} | all-to-all | bytes 557056 | tf_op jit(solution)/shard_map/all_to_all | solution.py:224
  43.9 0.8 reshape.83
  44.7 0.0 all-gather.2.cloned.1.call-update
  44.7 5.1 %collective-permute-start.2 = (bf16[32,16,384]{2,1,0:T(8,128)(2,1)S(1)}, bf16[32,16,384]{2,1,0:T(8,128)(2,1)S(1)}, u32[]{:S(2)}, u32[]{:S(2)}) collective-permute-start(bf16[32,16,384]{2,1,0:T(8,128)(2,1)S(1)} %get-tuple-element.14.a), channel_id=1, source_target_pairs={{0,384},{128,0},{256,128},{384,256},{1,385},{129,1},{257,129},{385... | collective-permute-start | bytes 1179656 | tf_op jit(solution)/shard_map/ppermute | solution.py:221
  49.9 1.9 collective-permute-start.1
  51.8 3.1 %collective-permute-start = (bf16[32,16,384]{2,1,0:T(8,128)(2,1)S(1)}, bf16[32,16,384]{2,1,0:T(8,128)(2,1)S(1)}, u32[]{:S(2)}, u32[]{:S(2)}) collective-permute-start(bf16[32,16,384]{2,1,0:T(8,128)(2,1)S(1)} %get-tuple-element.14.a), channel_id=1, source_target_pairs={{0,128},{128,256},{256,384},{384,0},{1,129},{129,257},{257,385},{3... | collective-permute-start | bytes 1179656 | tf_op jit(solution)/shard_map/ppermute | solution.py:221
  54.9 0.0 copy-done.2
  54.9 0.1 reshape.84
  55.0 0.6 gather_fusion
  55.6 0.1 broadcast_select_fusion
  55.7 0.1 select_n.67.places_ref
  55.7 3.7 %collective-permute-done.2.d = bf16[32,16,384]{2,1,0:T(8,128)(2,1)S(1)} collective-permute-done((bf16[32,16,384]{2,1,0:T(8,128)(2,1)S(1)}, bf16[32,16,384]{2,1,0:T(8,128)(2,1)S(1)}, u32[]{:S(2)}, u32[]{:S(2)}) %collective-permute-start.2) | collective-permute-done | bytes 393248 | tf_op jit(solution)/shard_map/ppermute | solution.py:221
  59.4 22.3 %collective-permute-done.1.c = bf16[32,16,384]{2,1,0:T(8,128)(2,1)S(1)} collective-permute-done((bf16[32,16,384]{2,1,0:T(8,128)(2,1)S(1)}, bf16[32,16,384]{2,1,0:T(8,128)(2,1)S(1)}, u32[]{:S(2)}, u32[]{:S(2)}) %collective-permute-start.1) | collective-permute-done | bytes 393248 | tf_op jit(solution)/shard_map/ppermute | solution.py:221
  81.8 0.0 collective-permute-done.b
  81.8 2.0 %shard_map.103 = bf16[128,16,384]{2,1,0:T(8,128)(2,1)} custom-call(s32[128]{0:T(128)S(1)} %select_n.67.places_ref, bf16[32,16,384]{2,1,0:T(8,128)(2,1)S(1)} %get-tuple-element.14.a, bf16[32,16,384]{2,1,0:T(8,128)(2,1)S(1)} %collective-permute-done.b, bf16[32,16,384]{2,1,0:T(8,128)(2,1)S(1)} %collective-permute-done.1.c, ...), custom_call_target="tpu_custom_call" | custom-call | tf_op jit(solution)/shard_map/pallas_call | solution.py:34
  83.7 9.1 %all-to-all-start.1 = ((bf16[128,16,384]{2,1,0:T(8,128)(2,1)}), bf16[128,16,384]{2,1,0:T(8,128)(2,1)S(1)}, u32[]{:S(2)}, u32[]{:S(2)}) async-start(bf16[128,16,384]{2,1,0:T(8,128)(2,1)} %shard_map.103), calls=%async_computation.1 | async-start | bytes 3145728 | tf_op jit(solution)/shard_map/all_to_all | solution.py:234
  92.9 0.7 fusion.9
  96.0 0.1 pad_add_fusion.numbers_ref
  96.1 39.8 %all-to-all-done.1 = bf16[128,16,384]{2,1,0:T(8,128)(2,1)S(1)} async-done(((bf16[128,16,384]{2,1,0:T(8,128)(2,1)}), bf16[128,16,384]{2,1,0:T(8,128)(2,1)S(1)}, u32[]{:S(2)}, u32[]{:S(2)}) %all-to-all-start.1) | async-done | bytes 1572896 | tf_op jit(solution)/shard_map/all_to_all | solution.py:234
  135.9 0.0 copy-start
  135.9 0.0 all-gather.2.cloned.1.call-done.rows_hbm
  135.9 1.2 copy-done
  137.1 4.9 %shard_map.104 = (bf16[2304,128]{1,0:T(8,128)(2,1)S(1)}, bf16[256,128]{1,0:T(8,128)(2,1)S(1)}, bf16[2048,384]{1,0:T(8,128)(2,1)}) custom-call(s32[2]{0:T(128)S(1)} %pad_add_fusion.numbers_ref, bf16[512,2176]{1,0:T(8,128)(2,1)} %all-gather.2.cloned.1.call-done.rows_hbm, bf16[2048,384]{1,0:T(8,128)(2,1)} %bitcast.15), custom_call_target="tpu_custom_call" | custom-call | tf_op jit(solution)/shard_map/pallas_call | solution.py:93
  142.0 2.0 %collective-permute-start.3 = (bf16[2304,128]{1,0:T(8,128)(2,1)S(1)}, bf16[2304,128]{1,0:T(8,128)(2,1)S(1)}, u32[]{:S(2)}, u32[]{:S(2)}) collective-permute-start(bf16[2304,128]{1,0:T(8,128)(2,1)S(1)} %get-tuple-element.20), channel_id=1, source_target_pairs={{0,1},{1,0},{2,3},{3,2},{4,5},{5,4},{6,7},{7,6},{8,9},{9,8},{10,11... | collective-permute-start | bytes 1769480 | tf_op jit(solution)/shard_map/ppermute | solution.py:243
  144.0 1.9 collective-permute-done.3.recv_ref
  145.9 0.0 copy-start.1
  145.9 1.4 copy-done.1
  147.3 0.7 shard_map.105
  148.0 39.1 %all_to_all.16.ref = bf16[64,64,128]{2,1,0:T(8,128)(2,1)S(1)} all-to-all(bf16[64,64,128]{2,1,0:T(8,128)(2,1)S(1)} %bitcast.17), channel_id=1, replica_groups=mesh['g'=4,'y'=8,'zh'=2,'x'=4,'c'=2] {'y','zh','x'}, dimensions={0} | all-to-all | bytes 2097152 | tf_op jit(solution)/shard_map/all_to_all | solution.py:245
  187.2 0.8 shard_map.106
  (6 shorter events, 0.1 us)
Async XLA Ops:
  7.2 128.7 %all-gather.2.cloned.1.call-start = ((), (), s32[]{:S(2)}) async-start(), calls=%async_computation.3 | async-start | bytes 2506752 | tf_op jit(solution)/shard_map/all_gather | solution.py:237
  12.0 42.8 %copy-start.2 = (s32[4,128]{1,0:T(4,128)S(1)}, s32[4,128]{1,0:T(4,128)}, u32[]{:S(2)}) copy-start(s32[4,128]{1,0:T(4,128)} %param.12) | copy-start | bytes 6148
  44.7 14.7 %collective-permute-start.2 = (bf16[32,16,384]{2,1,0:T(8,128)(2,1)S(1)}, bf16[32,16,384]{2,1,0:T(8,128)(2,1)S(1)}, u32[]{:S(2)}, u32[]{:S(2)}) collective-permute-start(bf16[32,16,384]{2,1,0:T(8,128)(2,1)S(1)} %get-tuple-element.14.a), channel_id=1, source_target_pairs={{0,384},{128,0},{256,128},{384,256},{1,385},{129,1},{257,129},{385... | collective-permute-start | bytes 1179656 | tf_op jit(solution)/shard_map/ppermute | solution.py:221
  49.9 31.9 %collective-permute-start.1 = (bf16[32,16,384]{2,1,0:T(8,128)(2,1)S(1)}, bf16[32,16,384]{2,1,0:T(8,128)(2,1)S(1)}, u32[]{:S(2)}, u32[]{:S(2)}) collective-permute-start(bf16[32,16,384]{2,1,0:T(8,128)(2,1)S(1)} %get-tuple-element.14.a), channel_id=1, source_target_pairs={{0,256},{128,384},{256,0},{384,128},{1,257},{129,385},{257,1},{385... | collective-permute-start | bytes 1179656 | tf_op jit(solution)/shard_map/ppermute | solution.py:221
  51.8 30.0 %collective-permute-start = (bf16[32,16,384]{2,1,0:T(8,128)(2,1)S(1)}, bf16[32,16,384]{2,1,0:T(8,128)(2,1)S(1)}, u32[]{:S(2)}, u32[]{:S(2)}) collective-permute-start(bf16[32,16,384]{2,1,0:T(8,128)(2,1)S(1)} %get-tuple-element.14.a), channel_id=1, source_target_pairs={{0,128},{128,256},{256,384},{384,0},{1,129},{129,257},{257,385},{3... | collective-permute-start | bytes 1179656 | tf_op jit(solution)/shard_map/ppermute | solution.py:221
  83.7 52.2 %all-to-all-start.1 = ((bf16[128,16,384]{2,1,0:T(8,128)(2,1)}), bf16[128,16,384]{2,1,0:T(8,128)(2,1)S(1)}, u32[]{:S(2)}, u32[]{:S(2)}) async-start(bf16[128,16,384]{2,1,0:T(8,128)(2,1)} %shard_map.103), calls=%async_computation.1 | async-start | bytes 3145728 | tf_op jit(solution)/shard_map/all_to_all | solution.py:234
  135.9 1.2 copy-start
  142.0 3.9 %collective-permute-start.3 = (bf16[2304,128]{1,0:T(8,128)(2,1)S(1)}, bf16[2304,128]{1,0:T(8,128)(2,1)S(1)}, u32[]{:S(2)}, u32[]{:S(2)}) collective-permute-start(bf16[2304,128]{1,0:T(8,128)(2,1)S(1)} %get-tuple-element.20), channel_id=1, source_target_pairs={{0,1},{1,0},{2,3},{3,2},{4,5},{5,4},{6,7},{7,6},{8,9},{9,8},{10,11... | collective-permute-start | bytes 1769480 | tf_op jit(solution)/shard_map/ppermute | solution.py:243
  145.9 1.4 copy-start.1
Sparse Core Ops, SparseCore 0:
  44.8 24.0 all-gather.1

commit v3 on v2

--- a/solution.py
+++ b/solution.py
@@ -42,98 +42,84 @@
 
 def hidden_units(numbers, rows_ext, weights):
     row_count = rows_ext.shape[0]
-    depth, cols = weights.shape
+    depth = weights.shape[0]
     half = row_count // CORES
-    blocks = 4
-    block = row_count // blocks
-
-    def kernel(numbers_ref, rows_hbm, w_ref, send_ref, keep_ref, slab_hbm, rows_ref, scaled_ref, row_sems, slab_sem):
+
+    def kernel(numbers_ref, rows_hbm, w_hbm, send_ref, keep_ref, slab_hbm, rows_ref, w_ref, scaled_ref, sems):
         copies = [
-            pltpu.make_async_copy(
-                rows_hbm.at[pl.ds(k * block, block)], rows_ref.at[pl.ds(k * block, block)], row_sems.at[k]
-            )
-            for k in range(blocks)
+            pltpu.make_async_copy(w_hbm, w_ref, sems.at[0]),
+            pltpu.make_async_copy(rows_hbm, rows_ref, sems.at[1]),
         ]
         for copy in copies:
             copy.start()
-        slab_copy = pltpu.make_async_copy(w_ref, slab_hbm, slab_sem)
-        slab_copy.start()
-        send_ref[half:, :] = w_ref[:, 256:]
         expert = numbers_ref[0]
         core = numbers_ref[1]
-        for k in range(blocks):
-            copies[k].wait()
-            span = slice(k * block, (k + 1) * block)
-            gate_up = jnp.dot(
-                rows_ref[span, :depth], w_ref[:, :256], preferred_element_type=jnp.float32
-            )
-            gate, up = gate_up[:, :128], gate_up[:, 128:]
-            hidden = (gate / (1.0 + jnp.exp(-gate)) * up).astype(jnp.bfloat16).astype(jnp.float32)
-            lane = lax.broadcasted_iota(jnp.int32, (block, EXTRA), 1)
-            own = (lane == expert) | (lane == expert + EXPERT_COUNT)
-            extra = rows_ref[span, depth:].astype(jnp.float32)
-            coefficient = jnp.sum(jnp.where(own, extra, 0.0), axis=1, keepdims=True)
-            scaled_ref[span, :] = (hidden * coefficient).astype(jnp.bfloat16)
         at = lax.broadcasted_iota(jnp.int32, (half, row_count), 0)
         of = lax.broadcasted_iota(jnp.int32, (half, row_count), 1)
         each, column = row_count // (XS * CORES * YS * ZHS), YS * ZHS
         row = at % each
         x = at // each % XS
         y_zh = at // (each * XS)
-        base = x * CORES * column * each + y_zh * each + row
+        away = of - (x * CORES * column * each + y_zh * each + row)
+        lane = lax.broadcasted_iota(jnp.int32, (row_count, EXTRA), 1)
+        own = (lane == expert) | (lane == expert + EXPERT_COUNT)
+        for copy in copies:
+            copy.wait()
+        slab_copy = pltpu.make_async_copy(w_ref, slab_hbm, sems.at[2])
+        slab_copy.start()
+        gate_up = jnp.dot(
+            rows_ref[:, :depth], w_ref[:, :256], preferred_element_type=jnp.float32
+        )
+        gate, up = gate_up[:, :128], gate_up[:, 128:]
+        hidden = (gate / (1.0 + jnp.exp(-gate)) * up).astype(jnp.bfloat16).astype(jnp.float32)
+        extra = rows_ref[:, depth:].astype(jnp.float32)
+        coefficient = jnp.sum(jnp.where(own, extra, 0.0), axis=1, keepdims=True)
+        scaled_ref[...] = (hidden * coefficient).astype(jnp.bfloat16)
+        send_ref[half:, :] = w_ref[:, 256:]
+        keep_ref[half:, :] = w_ref[:, 256:]
 
         def rows_of(k):
-            pick = jnp.where(of == base + k * (column * each), 1.0, 0.0).astype(jnp.bfloat16)
+            pick = jnp.where(away == k * (column * each), 1.0, 0.0).astype(jnp.bfloat16)
             return jnp.dot(pick, scaled_ref[...], preferred_element_type=jnp.float32).astype(jnp.bfloat16)
 
         send_ref[:half, :] = rows_of(1 - core)
-        keep_ref[...] = rows_of(core)
+        keep_ref[:half, :] = rows_of(core)
         slab_copy.wait()
 
     return pl.pallas_call(
         kernel,
-        out_shape=(
-            jax.ShapeDtypeStruct((half + depth, 128), jnp.bfloat16),
-            jax.ShapeDtypeStruct((half, 128), jnp.bfloat16),
-            jax.ShapeDtypeStruct((depth, cols), jnp.bfloat16),
-        ),
+        out_shape=(jax.ShapeDtypeStruct((half + depth, 128), jnp.bfloat16),) * 2
+        + (jax.ShapeDtypeStruct(weights.shape, jnp.bfloat16),),
         in_specs=[
             pl.BlockSpec(memory_space=pltpu.SMEM),
             pl.BlockSpec(memory_space=pltpu.HBM),
-            pl.BlockSpec(memory_space=pltpu.VMEM),
+            pl.BlockSpec(memory_space=pltpu.HBM),
         ],
-        out_specs=(
-            pl.BlockSpec(memory_space=pltpu.VMEM),
-            pl.BlockSpec(memory_space=pltpu.VMEM),
-            pl.BlockSpec(memory_space=pltpu.HBM),
-        ),
+        out_specs=(pl.BlockSpec(memory_space=pltpu.VMEM),) * 2 + (pl.BlockSpec(memory_space=pltpu.HBM),),
         scratch_shapes=[
             pltpu.VMEM(rows_ext.shape, jnp.bfloat16),
+            pltpu.VMEM(weights.shape, jnp.bfloat16),
             pltpu.VMEM((row_count, 128), jnp.bfloat16),
-            pltpu.SemaphoreType.DMA((blocks,)),
-            pltpu.SemaphoreType.DMA,
+            pltpu.SemaphoreType.DMA((3,)),
         ],
         compiler_params=pltpu.CompilerParams(vmem_limit_bytes=52 * 2**20),
     )(numbers, rows_ext, weights)
 
 
-def pair_outputs(keep, weights, received):
-    half = keep.shape[0]
-    depth = weights.shape[0]
-    chips = half // 4
+def pair_outputs(kept, received):
+    chips = YS * ZHS * XS
+    half = chips * 4
+    depth = kept.shape[0] - half
     lanes = depth // 128
 
-    def kernel(keep_ref, w_ref, recv_ref, out_ref, part_ref):
-        across = (((1,), (1,)), ((), ()))
+    def kernel(kept_ref, recv_ref, out_ref, part_ref):
         for k in range(4):
-            span = slice(k * depth // 4, (k + 1) * depth // 4)
-            part_ref[:, span] = lax.dot_general(
-                keep_ref[...], w_ref[span, 256:], across, preferred_element_type=jnp.float32
-            ) + lax.dot_general(
-                recv_ref[:half, :],
-                recv_ref[half + span.start : half + span.stop, :],
-                across,
-                preferred_element_type=jnp.float32,
+            span = slice(half + k * depth // 4, half + (k + 1) * depth // 4)
+            part_ref[:, k * depth // 4 : (k + 1) * depth // 4] = sum(
+                lax.dot_general(
+                    ref[:half, :], ref[span, :], (((1,), (1,)), ((), ())), preferred_element_type=jnp.float32
+                )
+                for ref in (kept_ref, recv_ref)
             )
         low = lax.broadcasted_iota(jnp.int32, (chips // 2, 8, 128), 1) < 4
 
@@ -152,11 +138,11 @@
     out = pl.pallas_call(
         kernel,
         out_shape=jax.ShapeDtypeStruct((chips // 2, 2, 4 * lanes, 128), jnp.bfloat16),
-        in_specs=[pl.BlockSpec(memory_space=pltpu.VMEM)] * 3,
+        in_specs=[pl.BlockSpec(memory_space=pltpu.VMEM)] * 2,
         out_specs=pl.BlockSpec(memory_space=pltpu.VMEM),
         scratch_shapes=[pltpu.VMEM((half, depth), jnp.float32)],
-        compiler_params=pltpu.CompilerParams(vmem_limit_bytes=32 * 2**20),
-    )(keep, weights, received)
+        compiler_params=pltpu.CompilerParams(vmem_limit_bytes=24 * 2**20),
+    )(kept, received)
     return out.reshape(chips, 4 * lanes, 128)
 
 
@@ -207,6 +193,14 @@
     master_out = master_weights - learn_rate * (update + weight_decay * master_weights)
     rounded = master_out.astype(jnp.bfloat16)
 
+    parts = [rounded] + [
+        lax.ppermute(rounded, "g", [(i, (i + s) % GROUPS) for i in range(GROUPS)])
+        for s in range(1, GROUPS)
+    ]
+
+    parts[1], tokens, routed_expert_index, gate_weights = lax.optimization_barrier(
+        (parts[1], tokens, routed_expert_index, gate_weights)
+    )
     experts = jnp.arange(EXPERT_COUNT, dtype=jnp.int32)
     named = routed_expert_index[0][:, :, None] == experts[None, None, :]
     coefficient = jnp.sum(jnp.where(named, gate_weights[0][:, :, None], 0.0), axis=1)
@@ -215,12 +209,6 @@
     fill = jnp.zeros((row_count, EXTRA - 2 * EXPERT_COUNT), jnp.bfloat16)
     own_rows = jnp.concatenate([tokens[0], high, low, fill], axis=1)
     spread = jnp.broadcast_to(own_rows[None], (YS * ZHS,) + own_rows.shape)
-    rounded, spread = lax.optimization_barrier((rounded, spread))
-
-    parts = [rounded] + [
-        lax.ppermute(rounded, "g", [(i, (i + s) % GROUPS) for i in range(GROUPS)])
-        for s in range(1, GROUPS)
-    ]
     some_rows = lax.all_to_all(spread, ("y", "zh"), split_axis=0, concat_axis=0, tiled=True)
     some_rows = some_rows.reshape(-1, depth + EXTRA)
     parts, _ = lax.optimization_barrier((parts, some_rows))
@@ -239,9 +227,9 @@
     slabs_each = unit_count // EXPERT_COUNT
     expert_id = jnp.sum(jnp.where(own_row == place, unit_ids, 0)) // slabs_each
     numbers = jnp.stack([expert_id, core]).astype(jnp.int32)
-    send, keep, slab = hidden_units(numbers, all_rows, weights)
-    received = lax.ppermute(send, "c", [(0, 1), (1, 0)])
-    chunks = pair_outputs(keep, weights, received)
+    sent, kept, slab = hidden_units(numbers, all_rows, weights)
+    received = lax.ppermute(sent, "c", [(0, 1), (1, 0)])
+    chunks = pair_outputs(kept, received)
     chunks = lax.all_to_all(chunks, ("y", "zh", "x"), split_axis=0, concat_axis=0, tiled=True)
     decoded = sum_chunks(chunks)
     return (master_out, slab[None, None], decoded[None])

time: 195 us -> 194 us (level)
  waiting for transfers between devices: 67.8 us -> 74.2 us
  blocking collectives: 70.9 us -> 67.6 us
  local copies, waits for them, and re-layouts: 5.02 us -> 2.87 us
    ppermute x3, waiting for transfers between devices: 26 us -> 32.5 us  [per_device(): lax.ppermute(rounded, 'g', [(i, (i + s) % GROUPS) for i in range(GROUPS)])]
    all_to_all x1, blocking collectives: 31.8 us -> 28.5 us  [per_device(): lax.all_to_all(spread, ('y', 'zh'), split_axis=0, concat_axis=0, tiled=True)]
  transfers between devices with their start and end apart: 6 -> 6, of which waited for: 4 -> 5; matrix products, arithmetic and copies ran while one was open for 1% -> 1% of each run, Pallas kernels for 1% -> 1%
where the time goes in v3:
time: 194 us; the launch traced here: 193 us
  waiting for transfers between devices  74.2 us (38%)
  blocking collectives  67.6 us (35%)
  starting transfers between devices  20.2 us (10%)
  between operations  16.7 us (9%)
  Pallas kernels  7.48 us (4%)
  other arithmetic  4.15 us (2%)
  local copies, waits for them, and re-layouts  2.87 us (1%)
    all_to_all x1, waiting for transfers between devices, per_device(): lax.all_to_all(ordered, ALONG, split_axis=0, concat_axis=0, tiled=True)  39.8 us
    all_to_all x1, blocking collectives, per_device(): lax.all_to_all(chunks, ('y', 'zh', 'x'), split_axis=0, concat_axis=0, til...  39.1 us
    ppermute x3, waiting for transfers between devices, per_device(): lax.ppermute(rounded, 'g', [(i, (i + s) % GROUPS) for i in range(GROUPS)])  32.5 us
    all_to_all x1, blocking collectives, per_device(): lax.all_to_all(spread, ('y', 'zh'), split_axis=0, concat_axis=0, tiled=True)  28.5 us
    ppermute x3, starting transfers between devices, per_device(): lax.ppermute(rounded, 'g', [(i, (i + s) % GROUPS) for i in range(GROUPS)])  9.72 us
    all_to_all x1, starting transfers between devices, per_device(): lax.all_to_all(ordered, ALONG, split_axis=0, concat_axis=0, tiled=True)  8.54 us
    pallas_call x1, Pallas kernels, hidden_units(): pl.pallas_call(kernel, out_shape=(jax.ShapeDtypeStruct((half + depth, 128...  4.02 us
  transfers between devices with their start and end apart: 6, of which 5 were waited for; matrix products, arithmetic and copies ran while one was open for 1% of the time, Pallas kernels for 1%

profile of v3, /device:TPU:6, one launch (start us, length us, event | category | flops | bytes accessed | tf_op | source)
XLA Modules:
  0.0 193.2 jit_solution(1955296141541746303)
XLA Ops:
  7.2 0.0 copy-start.2
  7.2 0.0 copy-start.3
  7.2 0.0 copy-start.1
  7.2 0.0 all-gather.2.cloned.1.call-start
  7.2 3.2 %fusion.14 = (bf16[32,16,384]{2,1,0:T(8,128)(2,1)S(1)}, f32[32,16,384]{2,1,0:T(8,128)}) fusion(f32[32,16,384]{2,1,0:T(8,128)} %param.8, f32[32,16,384]{2,1,0:T(8,128)} %param.10, bf16[32,16,384]{2,1,0:T(8,128)(2,1)} %param.11, f32[32,16,384]{2,1,0:T(8,128)} %param.9), kind=kLoop, calls=%fused_computation.34 | loop fusion | flops 3145728 | bytes 3932160 | tf_op jit(solution)/shard_map/convert_element_type | solution.py:194
  10.5 0.0 copy-start.4
  10.5 4.4 %collective-permute-start = (bf16[32,16,384]{2,1,0:T(8,128)(2,1)S(1)}, bf16[32,16,384]{2,1,0:T(8,128)(2,1)S(1)}, u32[]{:S(2)}, u32[]{:S(2)}) collective-permute-start(bf16[32,16,384]{2,1,0:T(8,128)(2,1)S(1)} %get-tuple-element.18.a), channel_id=1, source_target_pairs={{0,128},{128,256},{256,384},{384,0},{1,129},{129,257},{257,385},{3... | collective-permute-start | bytes 1179656 | tf_op jit(solution)/shard_map/ppermute | solution.py:197
  14.9 12.7 %collective-permute-done.b = bf16[32,16,384]{2,1,0:T(8,128)(2,1)S(1)} collective-permute-done((bf16[32,16,384]{2,1,0:T(8,128)(2,1)S(1)}, bf16[32,16,384]{2,1,0:T(8,128)(2,1)S(1)}, u32[]{:S(2)}, u32[]{:S(2)}) %collective-permute-start) | collective-permute-done | bytes 393248 | tf_op jit(solution)/shard_map/ppermute | solution.py:197
  27.6 0.0 copy-done.2
  27.6 0.0 copy-done.3
  27.6 0.1 select_reduce_fusion
  27.7 0.0 copy-done.1
  27.7 0.1 concatenate.3
  27.8 0.1 broadcast_in_dim.49
  27.9 28.5 %all_to_all.15 = bf16[16,4,2176]{2,1,0:T(4,128)(2,1)S(1)} all-to-all(bf16[16,4,2176]{2,1,0:T(4,128)(2,1)S(1)} %broadcast_in_dim.49), channel_id=1, replica_groups=mesh['g'=4,'y'=8,'zh'=2,'x'=4,'c'=2] {'y','zh'}, dimensions={0} | all-to-all | bytes 557056 | tf_op jit(solution)/shard_map/all_to_all | solution.py:212
  56.4 0.8 reshape.83
  57.2 0.0 all-gather.2.cloned.1.call-update
  57.2 3.4 %collective-permute-start.2 = (bf16[32,16,384]{2,1,0:T(8,128)(2,1)S(1)}, bf16[32,16,384]{2,1,0:T(8,128)(2,1)S(1)}, u32[]{:S(2)}, u32[]{:S(2)}) collective-permute-start(bf16[32,16,384]{2,1,0:T(8,128)(2,1)S(1)} %get-tuple-element.18.a), channel_id=1, source_target_pairs={{0,384},{128,0},{256,128},{384,256},{1,385},{129,1},{257,129},{385... | collective-permute-start | bytes 1179656 | tf_op jit(solution)/shard_map/ppermute | solution.py:197
  60.6 1.9 collective-permute-start.1
  62.5 0.0 copy-done.4
  62.6 0.1 reshape.84
  62.7 0.6 gather_fusion
  63.3 0.1 broadcast_select_fusion
  63.3 0.1 select_n.67.places_ref
  63.4 6.7 %collective-permute-done.2.d = bf16[32,16,384]{2,1,0:T(8,128)(2,1)S(1)} collective-permute-done((bf16[32,16,384]{2,1,0:T(8,128)(2,1)S(1)}, bf16[32,16,384]{2,1,0:T(8,128)(2,1)S(1)}, u32[]{:S(2)}, u32[]{:S(2)}) %collective-permute-start.2) | collective-permute-done | bytes 393248 | tf_op jit(solution)/shard_map/ppermute | solution.py:197
  70.1 13.0 %collective-permute-done.1.c = bf16[32,16,384]{2,1,0:T(8,128)(2,1)S(1)} collective-permute-done((bf16[32,16,384]{2,1,0:T(8,128)(2,1)S(1)}, bf16[32,16,384]{2,1,0:T(8,128)(2,1)S(1)}, u32[]{:S(2)}, u32[]{:S(2)}) %collective-permute-start.1) | collective-permute-done | bytes 393248 | tf_op jit(solution)/shard_map/ppermute | solution.py:197
  83.2 2.0 %shard_map.103 = bf16[128,16,384]{2,1,0:T(8,128)(2,1)} custom-call(s32[128]{0:T(128)S(1)} %select_n.67.places_ref, bf16[32,16,384]{2,1,0:T(8,128)(2,1)S(1)} %get-tuple-element.18.a, bf16[32,16,384]{2,1,0:T(8,128)(2,1)S(1)} %collective-permute-done.b, bf16[32,16,384]{2,1,0:T(8,128)(2,1)S(1)} %collective-permute-done.1.c, ...), custom_call_target="tpu_custom_call" | custom-call | tf_op jit(solution)/shard_map/pallas_call | solution.py:34
  85.1 8.5 %all-to-all-start.1 = ((bf16[128,16,384]{2,1,0:T(8,128)(2,1)}), bf16[128,16,384]{2,1,0:T(8,128)(2,1)S(1)}, u32[]{:S(2)}, u32[]{:S(2)}) async-start(bf16[128,16,384]{2,1,0:T(8,128)(2,1)} %shard_map.103), calls=%async_computation.1 | async-start | bytes 3145728 | tf_op jit(solution)/shard_map/all_to_all | solution.py:222
  93.7 0.6 fusion.9
  96.9 0.1 pad_add_fusion.numbers_ref
  97.0 39.8 %all-to-all-done.1 = bf16[128,16,384]{2,1,0:T(8,128)(2,1)S(1)} async-done(((bf16[128,16,384]{2,1,0:T(8,128)(2,1)}), bf16[128,16,384]{2,1,0:T(8,128)(2,1)S(1)}, u32[]{:S(2)}, u32[]{:S(2)}) %all-to-all-start.1) | async-done | bytes 1572896 | tf_op jit(solution)/shard_map/all_to_all | solution.py:222
  136.7 0.0 copy-start
  136.7 0.0 all-gather.2.cloned.1.call-done.rows_hbm
  136.7 1.2 copy-done
  137.9 4.0 %shard_map.104 = (bf16[2304,128]{1,0:T(8,128)(2,1)S(1)}, bf16[2304,128]{1,0:T(8,128)(2,1)S(1)}, bf16[2048,384]{1,0:T(8,128)(2,1)}) custom-call(s32[2]{0:T(128)S(1)} %pad_add_fusion.numbers_ref, bf16[512,2176]{1,0:T(8,128)(2,1)} %all-gather.2.cloned.1.call-done.rows_hbm, bf16[2048,384]{1,0:T(8,128)(2,1)} %bitcast.16), custom_call_target="tpu_custom_call" | custom-call | tf_op jit(solution)/shard_map/pallas_call | solution.py:89
  141.9 1.9 %collective-permute-start.3 = (bf16[2304,128]{1,0:T(8,128)(2,1)S(1)}, bf16[2304,128]{1,0:T(8,128)(2,1)S(1)}, u32[]{:S(2)}, u32[]{:S(2)}) collective-permute-start(bf16[2304,128]{1,0:T(8,128)(2,1)S(1)} %get-tuple-element.24), channel_id=1, source_target_pairs={{0,1},{1,0},{2,3},{3,2},{4,5},{5,4},{6,7},{7,6},{8,9},{9,8},{10,11... | collective-permute-start | bytes 1769480 | tf_op jit(solution)/shard_map/ppermute | solution.py:231
  143.9 2.0 %collective-permute-done.3.recv_ref = bf16[2304,128]{1,0:T(8,128)(2,1)S(1)} collective-permute-done((bf16[2304,128]{1,0:T(8,128)(2,1)S(1)}, bf16[2304,128]{1,0:T(8,128)(2,1)S(1)}, u32[]{:S(2)}, u32[]{:S(2)}) %collective-permute-start.3) | collective-permute-done | bytes 589856 | tf_op jit(solution)/shard_map/ppermute | solution.py:231
  145.8 0.7 shard_map.105
  146.5 39.1 %all_to_all.16.ref = bf16[64,64,128]{2,1,0:T(8,128)(2,1)S(1)} all-to-all(bf16[64,64,128]{2,1,0:T(8,128)(2,1)S(1)} %bitcast.15), channel_id=1, replica_groups=mesh['g'=4,'y'=8,'zh'=2,'x'=4,'c'=2] {'y','zh','x'}, dimensions={0} | all-to-all | bytes 2097152 | tf_op jit(solution)/shard_map/all_to_all | solution.py:233
  185.6 0.8 shard_map.106
  (6 shorter events, 0.1 us)
Async XLA Ops:
  7.2 20.4 %copy-start.2 = (f32[1,4,8]{2,1,0:T(4,128)S(1)}, f32[1,4,8]{2,1,0:T(4,128)}, u32[]{:S(2)}) copy-start(f32[1,4,8]{2,1,0:T(4,128)} %param.15) | copy-start | bytes 388
  7.2 20.4 %copy-start.3 = (s32[1,4,8]{2,1,0:T(4,128)S(1)}, s32[1,4,8]{2,1,0:T(4,128)}, u32[]{:S(2)}) copy-start(s32[1,4,8]{2,1,0:T(4,128)} %param.14) | copy-start | bytes 388
  7.2 20.5 %copy-start.1 = (bf16[1,4,2048]{2,1,0:T(4,128)(2,1)S(1)}, bf16[1,4,2048]{2,1,0:T(4,128)(2,1)}, u32[]{:S(2)}) copy-start(bf16[1,4,2048]{2,1,0:T(4,128)(2,1)} %param.13) | copy-start | bytes 49156
  7.2 129.5 %all-gather.2.cloned.1.call-start = ((), (), s32[]{:S(2)}) async-start(), calls=%async_computation.3 | async-start | bytes 2506752 | tf_op jit(solution)/shard_map/all_gather | solution.py:225
  10.5 52.1 %copy-start.4 = (s32[4,128]{1,0:T(4,128)S(1)}, s32[4,128]{1,0:T(4,128)}, u32[]{:S(2)}) copy-start(s32[4,128]{1,0:T(4,128)} %param.12) | copy-start | bytes 6148
  10.5 17.1 %collective-permute-start = (bf16[32,16,384]{2,1,0:T(8,128)(2,1)S(1)}, bf16[32,16,384]{2,1,0:T(8,128)(2,1)S(1)}, u32[]{:S(2)}, u32[]{:S(2)}) collective-permute-start(bf16[32,16,384]{2,1,0:T(8,128)(2,1)S(1)} %get-tuple-element.18.a), channel_id=1, source_target_pairs={{0,128},{128,256},{256,384},{384,0},{1,129},{129,257},{257,385},{3... | collective-permute-start | bytes 1179656 | tf_op jit(solution)/shard_map/ppermute | solution.py:197
  57.2 13.0 %collective-permute-start.2 = (bf16[32,16,384]{2,1,0:T(8,128)(2,1)S(1)}, bf16[32,16,384]{2,1,0:T(8,128)(2,1)S(1)}, u32[]{:S(2)}, u32[]{:S(2)}) collective-permute-start(bf16[32,16,384]{2,1,0:T(8,128)(2,1)S(1)} %get-tuple-element.18.a), channel_id=1, source_target_pairs={{0,384},{128,0},{256,128},{384,256},{1,385},{129,1},{257,129},{385... | collective-permute-start | bytes 1179656 | tf_op jit(solution)/shard_map/ppermute | solution.py:197
  60.6 22.6 %collective-permute-start.1 = (bf16[32,16,384]{2,1,0:T(8,128)(2,1)S(1)}, bf16[32,16,384]{2,1,0:T(8,128)(2,1)S(1)}, u32[]{:S(2)}, u32[]{:S(2)}) collective-permute-start(bf16[32,16,384]{2,1,0:T(8,128)(2,1)S(1)} %get-tuple-element.18.a), channel_id=1, source_target_pairs={{0,256},{128,384},{256,0},{384,128},{1,257},{129,385},{257,1},{385... | collective-permute-start | bytes 1179656 | tf_op jit(solution)/shard_map/ppermute | solution.py:197
  85.1 51.6 %all-to-all-start.1 = ((bf16[128,16,384]{2,1,0:T(8,128)(2,1)}), bf16[128,16,384]{2,1,0:T(8,128)(2,1)S(1)}, u32[]{:S(2)}, u32[]{:S(2)}) async-start(bf16[128,16,384]{2,1,0:T(8,128)(2,1)} %shard_map.103), calls=%async_computation.1 | async-start | bytes 3145728 | tf_op jit(solution)/shard_map/all_to_all | solution.py:222
  136.7 1.2 copy-start
  141.9 3.9 %collective-permute-start.3 = (bf16[2304,128]{1,0:T(8,128)(2,1)S(1)}, bf16[2304,128]{1,0:T(8,128)(2,1)S(1)}, u32[]{:S(2)}, u32[]{:S(2)}) collective-permute-start(bf16[2304,128]{1,0:T(8,128)(2,1)S(1)} %get-tuple-element.24), channel_id=1, source_target_pairs={{0,1},{1,0},{2,3},{3,2},{4,5},{5,4},{6,7},{7,6},{8,9},{9,8},{10,11... | collective-permute-start | bytes 1769480 | tf_op jit(solution)/shard_map/ppermute | solution.py:231
Sparse Core Ops, SparseCore 0:
  57.3 21.9 all-gather.1

commit v4 on v3

--- a/solution.py
+++ b/solution.py
@@ -16,6 +16,7 @@
 ALONG = ("y", "zh", "x", "c")
 EXPERT_COUNT = 16
 EXTRA = 128
+ROOM = 32
 
 
 def place_slabs(places, parts):
@@ -40,50 +41,34 @@
     )(places, *parts)
 
 
-def hidden_units(numbers, rows_ext, weights):
+def hidden_units(expert_id, pick, rows_ext, weights):
     row_count = rows_ext.shape[0]
     depth = weights.shape[0]
     half = row_count // CORES
 
-    def kernel(numbers_ref, rows_hbm, w_hbm, send_ref, keep_ref, slab_hbm, rows_ref, w_ref, scaled_ref, sems):
-        copies = [
-            pltpu.make_async_copy(w_hbm, w_ref, sems.at[0]),
-            pltpu.make_async_copy(rows_hbm, rows_ref, sems.at[1]),
-        ]
-        for copy in copies:
-            copy.start()
-        expert = numbers_ref[0]
-        core = numbers_ref[1]
-        at = lax.broadcasted_iota(jnp.int32, (half, row_count), 0)
-        of = lax.broadcasted_iota(jnp.int32, (half, row_count), 1)
-        each, column = row_count // (XS * CORES * YS * ZHS), YS * ZHS
-        row = at % each
-        x = at // each % XS
-        y_zh = at // (each * XS)
-        away = of - (x * CORES * column * each + y_zh * each + row)
-        lane = lax.broadcasted_iota(jnp.int32, (row_count, EXTRA), 1)
-        own = (lane == expert) | (lane == expert + EXPERT_COUNT)
-        for copy in copies:
-            copy.wait()
-        slab_copy = pltpu.make_async_copy(w_ref, slab_hbm, sems.at[2])
+    def kernel(expert_ref, pick_ref, rows_hbm, w_ref, send_ref, keep_ref, slab_hbm, rows_ref, scaled_ref, sems):
+        rows_copy = pltpu.make_async_copy(rows_hbm, rows_ref, sems.at[0])
+        rows_copy.start()
+        slab_copy = pltpu.make_async_copy(w_ref, slab_hbm, sems.at[1])
         slab_copy.start()
+        send_ref[half:, :] = w_ref[:, 256:]
+        keep_ref[half:, :] = w_ref[:, 256:]
+        expert = expert_ref[0]
+        lane = lax.broadcasted_iota(jnp.int32, (1, EXTRA), 1)
+        own = jnp.where((lane == expert) | (lane == expert + EXPERT_COUNT), 1.0, 0.0)
+        rows_copy.wait()
         gate_up = jnp.dot(
             rows_ref[:, :depth], w_ref[:, :256], preferred_element_type=jnp.float32
         )
         gate, up = gate_up[:, :128], gate_up[:, 128:]
         hidden = (gate / (1.0 + jnp.exp(-gate)) * up).astype(jnp.bfloat16).astype(jnp.float32)
         extra = rows_ref[:, depth:].astype(jnp.float32)
-        coefficient = jnp.sum(jnp.where(own, extra, 0.0), axis=1, keepdims=True)
+        coefficient = jnp.sum(extra * own, axis=1, keepdims=True)
         scaled_ref[...] = (hidden * coefficient).astype(jnp.bfloat16)
-        send_ref[half:, :] = w_ref[:, 256:]
-        keep_ref[half:, :] = w_ref[:, 256:]
-
-        def rows_of(k):
-            pick = jnp.where(away == k * (column * each), 1.0, 0.0).astype(jnp.bfloat16)
-            return jnp.dot(pick, scaled_ref[...], preferred_element_type=jnp.float32).astype(jnp.bfloat16)
-
-        send_ref[:half, :] = rows_of(1 - core)
-        keep_ref[:half, :] = rows_of(core)
+        picked = jnp.dot(pick_ref[...], scaled_ref[...], preferred_element_type=jnp.float32)
+        picked = picked.astype(jnp.bfloat16)
+        send_ref[:half, :] = picked[:half]
+        keep_ref[:half, :] = picked[half:]
         slab_copy.wait()
 
     return pl.pallas_call(
@@ -92,18 +77,18 @@
         + (jax.ShapeDtypeStruct(weights.shape, jnp.bfloat16),),
         in_specs=[
             pl.BlockSpec(memory_space=pltpu.SMEM),
+            pl.BlockSpec(memory_space=pltpu.VMEM),
             pl.BlockSpec(memory_space=pltpu.HBM),
-            pl.BlockSpec(memory_space=pltpu.HBM),
+            pl.BlockSpec(memory_space=pltpu.VMEM),
         ],
         out_specs=(pl.BlockSpec(memory_space=pltpu.VMEM),) * 2 + (pl.BlockSpec(memory_space=pltpu.HBM),),
         scratch_shapes=[
             pltpu.VMEM(rows_ext.shape, jnp.bfloat16),
-            pltpu.VMEM(weights.shape, jnp.bfloat16),
             pltpu.VMEM((row_count, 128), jnp.bfloat16),
-            pltpu.SemaphoreType.DMA((3,)),
+            pltpu.SemaphoreType.DMA((2,)),
         ],
-        compiler_params=pltpu.CompilerParams(vmem_limit_bytes=52 * 2**20),
-    )(numbers, rows_ext, weights)
+        compiler_params=pltpu.CompilerParams(vmem_limit_bytes=50 * 2**20),
+    )(expert_id, pick, rows_ext, weights)
 
 
 def pair_outputs(kept, received):
@@ -181,7 +166,16 @@
     core = lax.axis_index("c")
     place = lax.axis_index(ALONG)
     row_count, depth = tokens.shape[1:]
-
+    width = depth + EXTRA
+
+    experts = jnp.arange(EXPERT_COUNT, dtype=jnp.int32)
+    named = routed_expert_index[0][:, :, None] == experts[None, None, :]
+    coefficient = jnp.sum(jnp.where(named, gate_weights[0][:, :, None], 0.0), axis=1)
+    high = coefficient.astype(jnp.bfloat16)
+    low = (coefficient - high.astype(jnp.float32)).astype(jnp.bfloat16)
+    fill = jnp.zeros((row_count, EXTRA - 2 * EXPERT_COUNT), jnp.bfloat16)
+    own_rows = jnp.concatenate([tokens[0], high, low, fill], axis=1)
+    other_rows = lax.ppermute(own_rows, "zh", [(0, 1), (1, 0)])
     grad_float = gradient.astype(jnp.float32)
     first_new = beta_one * first_moment + (1.0 - beta_one) * grad_float
     second_new = beta_two * second_moment + (1.0 - beta_two) * grad_float * grad_float
@@ -193,25 +187,21 @@
     master_out = master_weights - learn_rate * (update + weight_decay * master_weights)
     rounded = master_out.astype(jnp.bfloat16)
 
+    other_rows, _ = lax.optimization_barrier((other_rows, rounded))
+    first = lax.axis_index("zh") == 0
+    pair = jnp.concatenate(
+        [jnp.where(first, own_rows, other_rows), jnp.where(first, other_rows, own_rows)], axis=0
+    )
+    column = lax.all_gather(jnp.pad(pair, ((0, ROOM - ZHS * row_count), (0, 0))), "y", axis=0, tiled=True)
+
     parts = [rounded] + [
         lax.ppermute(rounded, "g", [(i, (i + s) % GROUPS) for i in range(GROUPS)])
         for s in range(1, GROUPS)
     ]
-
-    parts[1], tokens, routed_expert_index, gate_weights = lax.optimization_barrier(
-        (parts[1], tokens, routed_expert_index, gate_weights)
-    )
-    experts = jnp.arange(EXPERT_COUNT, dtype=jnp.int32)
-    named = routed_expert_index[0][:, :, None] == experts[None, None, :]
-    coefficient = jnp.sum(jnp.where(named, gate_weights[0][:, :, None], 0.0), axis=1)
-    high = coefficient.astype(jnp.bfloat16)
-    low = (coefficient - high.astype(jnp.float32)).astype(jnp.bfloat16)
-    fill = jnp.zeros((row_count, EXTRA - 2 * EXPERT_COUNT), jnp.bfloat16)
-    own_rows = jnp.concatenate([tokens[0], high, low, fill], axis=1)
-    spread = jnp.broadcast_to(own_rows[None], (YS * ZHS,) + own_rows.shape)
-    some_rows = lax.all_to_all(spread, ("y", "zh"), split_axis=0, concat_axis=0, tiled=True)
-    some_rows = some_rows.reshape(-1, depth + EXTRA)
-    parts, _ = lax.optimization_barrier((parts, some_rows))
+    parts, column = lax.optimization_barrier((parts, column))
+
+    column = column.reshape(YS, ROOM, width)[:, : ZHS * row_count].reshape(-1, width)
+    all_rows = lax.all_gather(column, ("x", "c"), axis=0, tiled=True)
 
     unit_count = placement.shape[1]
     unit_ids = jnp.arange(unit_count, dtype=jnp.int32)
@@ -222,12 +212,14 @@
     own_slab = lax.all_to_all(ordered, ALONG, split_axis=0, concat_axis=0, tiled=True)
     weights = own_slab.reshape(depth, -1)
 
-    all_rows = lax.all_gather(some_rows, ("x", "c"), axis=0, tiled=True)
+    by_place = jnp.arange(all_rows.shape[0], dtype=jnp.int32).reshape(XS, CORES, YS * ZHS, row_count)
+    by_place = by_place.transpose(1, 2, 0, 3).reshape(CORES, -1)
+    source = jnp.where(core == 0, by_place[::-1], by_place).reshape(-1)
+    pick = (source[:, None] == jnp.arange(all_rows.shape[0], dtype=jnp.int32)[None, :]).astype(jnp.bfloat16)
 
     slabs_each = unit_count // EXPERT_COUNT
-    expert_id = jnp.sum(jnp.where(own_row == place, unit_ids, 0)) // slabs_each
-    numbers = jnp.stack([expert_id, core]).astype(jnp.int32)
-    sent, kept, slab = hidden_units(numbers, all_rows, weights)
+    expert_id = jnp.sum(jnp.where(own_row == place, unit_ids, 0), keepdims=True) // slabs_each
+    sent, kept, slab = hidden_units(expert_id, pick, all_rows, weights)
     received = lax.ppermute(sent, "c", [(0, 1), (1, 0)])
     chunks = pair_outputs(kept, received)
     chunks = lax.all_to_all(chunks, ("y", "zh", "x"), split_axis=0, concat_axis=0, tiled=True)

time: 194 us -> 183 us (0.943)
  blocking collectives: 67.6 us -> 39.1 us
  starting transfers between devices: 20.2 us -> 37.6 us
    all_to_all x1 -> x0, blocking collectives: 28.5 us -> none  [per_device(): lax.all_to_all(spread, ('y', 'zh'), split_axis=0, concat_axis=0, tiled=True)]
    ppermute x0 -> x1, starting transfers between devices: none -> 11 us  [per_device(): other_rows = lax.ppermute(own_rows, 'zh', [(0, 1), (1, 0)])]
    all_to_all x1, starting transfers between devices: 8.54 us -> 14.4 us  [per_device(): lax.all_to_all(ordered, ALONG, split_axis=0, concat_axis=0, tiled=True)]
    ppermute x3, waiting for transfers between devices: 32.5 us -> 28.5 us  [per_device(): lax.ppermute(rounded, 'g', [(i, (i + s) % GROUPS) for i in range(GROUPS)])]
    all_gather x1 -> x2, waiting for transfers between devices: 0.01 us -> 2.65 us  [the longest x1 2.65 us: per_device(): lax.all_gather(jnp.pad(pair, ((0, ROOM - ZHS * row_count), (0, 0))), 'y',...]
  transfers between devices with their start and end apart: 6 -> 8, of which waited for: 5 -> 5; matrix products, arithmetic and copies ran while one was open for 1% -> 3% of each run, Pallas kernels for 1% -> 1%
where the time goes in v4:
time: 183 us; the launch traced here: 182 us
  waiting for transfers between devices  72.3 us (40%)
  blocking collectives  39.1 us (21%)
  starting transfers between devices  37.6 us (21%)
  between operations  16.8 us (9%)
  Pallas kernels  6.91 us (4%)
  other arithmetic  5.65 us (3%)
  local copies, waits for them, and re-layouts  3.56 us (2%)
    all_to_all x1, waiting for transfers between devices, per_device(): lax.all_to_all(ordered, ALONG, split_axis=0, concat_axis=0, tiled=True)  39.2 us
    all_to_all x1, blocking collectives, per_device(): lax.all_to_all(chunks, ('y', 'zh', 'x'), split_axis=0, concat_axis=0, til...  39.1 us
    ppermute x3, waiting for transfers between devices, per_device(): lax.ppermute(rounded, 'g', [(i, (i + s) % GROUPS) for i in range(GROUPS)])  28.5 us
    all_to_all x1, starting transfers between devices, per_device(): lax.all_to_all(ordered, ALONG, split_axis=0, concat_axis=0, tiled=True)  14.4 us
    ppermute x1, starting transfers between devices, per_device(): other_rows = lax.ppermute(own_rows, 'zh', [(0, 1), (1, 0)])  11 us
    ppermute x3, starting transfers between devices, per_device(): lax.ppermute(rounded, 'g', [(i, (i + s) % GROUPS) for i in range(GROUPS)])  10.1 us
  transfers between devices with their start and end apart: 8, of which 5 were waited for; matrix products, arithmetic and copies ran while one was open for 3% of the time, Pallas kernels for 1%

profile of v4, /device:TPU:6, one launch (start us, length us, event | category | flops | bytes accessed | tf_op | source)
XLA Modules:
  0.0 182.0 jit_solution(13679149285656676537)
XLA Ops:
  7.2 0.0 all-gather.3.cloned.1.call-start
  7.2 0.8 select_reduce_fusion
  8.0 0.8 concatenate.6
  8.8 0.0 copy-start
  8.8 11.0 %collective-permute-start.3 = (bf16[4,2176]{1,0:T(4,128)(2,1)S(1)}, bf16[4,2176]{1,0:T(4,128)(2,1)S(1)}, u32[]{:S(2)}, u32[]{:S(2)}) collective-permute-start(bf16[4,2176]{1,0:T(4,128)(2,1)S(1)} %concatenate.6), channel_id=1, source_target_pairs={{0,8},{8,0},{1,9},{9,1},{2,10},{10,2},{3,11},{11,3},{4,12},{12,4},... | collective-permute-start | bytes 52232 | tf_op jit(solution)/shard_map/ppermute | solution.py:178
  19.9 3.2 %fusion.18 = (bf16[32,16,384]{2,1,0:T(8,128)(2,1)S(1)}, f32[32,16,384]{2,1,0:T(8,128)}) fusion(f32[32,16,384]{2,1,0:T(8,128)} %param.8, f32[32,16,384]{2,1,0:T(8,128)} %param.10, bf16[32,16,384]{2,1,0:T(8,128)(2,1)} %param.11, f32[32,16,384]{2,1,0:T(8,128)} %param.9), kind=kLoop, calls=%fused_computation.46 | loop fusion | flops 3145728 | bytes 3932160 | tf_op jit(solution)/shard_map/convert_element_type | solution.py:188
  23.1 0.0 collective-permute-done.3
  23.1 0.7 fusion.12
  23.8 0.0 all-gather.3.cloned.1.call-update
  23.8 0.0 all-gather.5.cloned.1.call-start
  23.9 5.2 %collective-permute-start.2 = (bf16[32,16,384]{2,1,0:T(8,128)(2,1)S(1)}, bf16[32,16,384]{2,1,0:T(8,128)(2,1)S(1)}, u32[]{:S(2)}, u32[]{:S(2)}) collective-permute-start(bf16[32,16,384]{2,1,0:T(8,128)(2,1)S(1)} %get-tuple-element.14.a), channel_id=1, source_target_pairs={{0,384},{128,0},{256,128},{384,256},{1,385},{129,1},{257,129},{385... | collective-permute-start | bytes 1179656 | tf_op jit(solution)/shard_map/ppermute | solution.py:198
  29.1 1.9 %collective-permute-start.1 = (bf16[32,16,384]{2,1,0:T(8,128)(2,1)S(1)}, bf16[32,16,384]{2,1,0:T(8,128)(2,1)S(1)}, u32[]{:S(2)}, u32[]{:S(2)}) collective-permute-start(bf16[32,16,384]{2,1,0:T(8,128)(2,1)S(1)} %get-tuple-element.14.a), channel_id=1, source_target_pairs={{0,256},{128,384},{256,0},{384,128},{1,257},{129,385},{257,1},{385... | collective-permute-start | bytes 1179656 | tf_op jit(solution)/shard_map/ppermute | solution.py:198
  31.0 3.0 %collective-permute-start = (bf16[32,16,384]{2,1,0:T(8,128)(2,1)S(1)}, bf16[32,16,384]{2,1,0:T(8,128)(2,1)S(1)}, u32[]{:S(2)}, u32[]{:S(2)}) collective-permute-start(bf16[32,16,384]{2,1,0:T(8,128)(2,1)S(1)} %get-tuple-element.14.a), channel_id=1, source_target_pairs={{0,128},{128,256},{256,384},{384,0},{1,129},{129,257},{257,385},{3... | collective-permute-start | bytes 1179656 | tf_op jit(solution)/shard_map/ppermute | solution.py:198
  34.0 4.7 %collective-permute-done.2.d = bf16[32,16,384]{2,1,0:T(8,128)(2,1)S(1)} collective-permute-done((bf16[32,16,384]{2,1,0:T(8,128)(2,1)S(1)}, bf16[32,16,384]{2,1,0:T(8,128)(2,1)S(1)}, u32[]{:S(2)}, u32[]{:S(2)}) %collective-permute-start.2) | collective-permute-done | bytes 393248 | tf_op jit(solution)/shard_map/ppermute | solution.py:198
  38.7 23.8 %collective-permute-done.1.c = bf16[32,16,384]{2,1,0:T(8,128)(2,1)S(1)} collective-permute-done((bf16[32,16,384]{2,1,0:T(8,128)(2,1)S(1)}, bf16[32,16,384]{2,1,0:T(8,128)(2,1)S(1)}, u32[]{:S(2)}, u32[]{:S(2)}) %collective-permute-start.1) | collective-permute-done | bytes 393248 | tf_op jit(solution)/shard_map/ppermute | solution.py:198
  62.5 0.0 collective-permute-done.b
  62.5 2.7 %all-gather.3.cloned.1.call-done = bf16[256,2176]{1,0:T(8,128)(2,1)} async-done(((bf16[32,2176]{1,0:T(8,128)(2,1)}), bf16[256,2176]{1,0:T(8,128)(2,1)}) %all-gather.3.cloned.1.call-update) | async-done | bytes 1114128 | tf_op jit(solution)/shard_map/all_gather | solution.py:195
  65.2 1.7 slice_bitcast_fusion
  66.9 0.0 all-gather.5.cloned.1.call-update
  66.9 0.0 copy-done
  66.9 0.1 reshape.152
  67.1 0.6 gather_fusion
  67.6 0.1 broadcast_select_fusion.2
  67.7 0.1 select_n.93.places_ref
  67.8 2.0 %shard_map.103 = bf16[128,16,384]{2,1,0:T(8,128)(2,1)} custom-call(s32[128]{0:T(128)S(1)} %select_n.93.places_ref, bf16[32,16,384]{2,1,0:T(8,128)(2,1)S(1)} %get-tuple-element.14.a, bf16[32,16,384]{2,1,0:T(8,128)(2,1)S(1)} %collective-permute-done.b, bf16[32,16,384]{2,1,0:T(8,128)(2,1)S(1)} %collective-permute-done.1.c, ...), custom_call_target="tpu_custom_call" | custom-call | tf_op jit(solution)/shard_map/pallas_call | solution.py:35
  69.8 14.4 %all-to-all-start = ((bf16[128,16,384]{2,1,0:T(8,128)(2,1)}), bf16[128,16,384]{2,1,0:T(8,128)(2,1)S(1)}, u32[]{:S(2)}, u32[]{:S(2)}) async-start(bf16[128,16,384]{2,1,0:T(8,128)(2,1)} %shard_map.103), calls=%async_computation | async-start | bytes 3145728 | tf_op jit(solution)/shard_map/all_to_all | solution.py:212
  84.2 0.6 fusion.13
  87.5 0.1 reshape.142
  87.6 0.1 reshape.148
  87.7 0.1 rev.3
  87.8 0.2 fusion.pick_ref
  88.0 39.2 %all-to-all-done = bf16[128,16,384]{2,1,0:T(8,128)(2,1)S(1)} async-done(((bf16[128,16,384]{2,1,0:T(8,128)(2,1)}), bf16[128,16,384]{2,1,0:T(8,128)(2,1)S(1)}, u32[]{:S(2)}, u32[]{:S(2)}) %all-to-all-start) | async-done | bytes 1572896 | tf_op jit(solution)/shard_map/all_to_all | solution.py:212
  127.2 0.0 all-gather.5.cloned.1.call-done.rows_hbm
  127.2 3.4 %shard_map.104 = (bf16[2304,128]{1,0:T(8,128)(2,1)S(1)}, bf16[2304,128]{1,0:T(8,128)(2,1)S(1)}, bf16[2048,384]{1,0:T(8,128)(2,1)}) custom-call(s32[1]{0:T(128)S(6)} %select_n.81.expert_ref, bf16[512,512]{1,0:T(8,128)(2,1)S(1)} %fusion.pick_ref, bf16[512,2176]{1,0:T(8,128)(2,1)} %all-gather.5.cloned.1.call-done.rows_hbm, bf16[2048,384]{1,0:T(8,128)(2,1)S(1)} %bitcast.20), custom_call_target="tpu_custom_call" | custom-call | tf_op jit(solution)/shard_map/pallas_call | solution.py:74
  130.7 1.9 %collective-permute-start.4 = (bf16[2304,128]{1,0:T(8,128)(2,1)S(1)}, bf16[2304,128]{1,0:T(8,128)(2,1)S(1)}, u32[]{:S(2)}, u32[]{:S(2)}) collective-permute-start(bf16[2304,128]{1,0:T(8,128)(2,1)S(1)} %get-tuple-element.20), channel_id=1, source_target_pairs={{0,1},{1,0},{2,3},{3,2},{4,5},{5,4},{6,7},{7,6},{8,9},{9,8},{10,11... | collective-permute-start | bytes 1769480 | tf_op jit(solution)/shard_map/ppermute | solution.py:223
  132.6 1.9 %collective-permute-done.4.recv_ref = bf16[2304,128]{1,0:T(8,128)(2,1)S(1)} collective-permute-done((bf16[2304,128]{1,0:T(8,128)(2,1)S(1)}, bf16[2304,128]{1,0:T(8,128)(2,1)S(1)}, u32[]{:S(2)}, u32[]{:S(2)}) %collective-permute-start.4) | collective-permute-done | bytes 589856 | tf_op jit(solution)/shard_map/ppermute | solution.py:223
  134.6 0.7 shard_map.105
  135.3 39.1 %all_to_all.10.ref = bf16[64,64,128]{2,1,0:T(8,128)(2,1)S(1)} all-to-all(bf16[64,64,128]{2,1,0:T(8,128)(2,1)S(1)} %bitcast.21), channel_id=1, replica_groups=mesh['g'=4,'y'=8,'zh'=2,'x'=4,'c'=2] {'y','zh','x'}, dimensions={0} | all-to-all | bytes 2097152 | tf_op jit(solution)/shard_map/all_to_all | solution.py:225
  174.4 0.8 shard_map.106
  (12 shorter events, 0.1 us)
Async XLA Ops:
  7.2 58.0 %all-gather.3.cloned.1.call-start = ((), (), s32[]{:S(2)}) async-start(), calls=%async_computation.2 | async-start | bytes 1253376 | tf_op jit(solution)/shard_map/all_gather | solution.py:195
  8.8 58.1 %copy-start = (s32[4,128]{1,0:T(4,128)S(1)}, s32[4,128]{1,0:T(4,128)}, u32[]{:S(2)}) copy-start(s32[4,128]{1,0:T(4,128)} %param.12) | copy-start | bytes 6148
  8.8 14.3 %collective-permute-start.3 = (bf16[4,2176]{1,0:T(4,128)(2,1)S(1)}, bf16[4,2176]{1,0:T(4,128)(2,1)S(1)}, u32[]{:S(2)}, u32[]{:S(2)}) collective-permute-start(bf16[4,2176]{1,0:T(4,128)(2,1)S(1)} %concatenate.6), channel_id=1, source_target_pairs={{0,8},{8,0},{1,9},{9,1},{2,10},{10,2},{3,11},{11,3},{4,12},{12,4},... | collective-permute-start | bytes 52232 | tf_op jit(solution)/shard_map/ppermute | solution.py:178
  23.8 103.4 %all-gather.5.cloned.1.call-start = ((), (), s32[]{:S(2)}) async-start(), calls=%async_computation.3 | async-start | bytes 2506752 | tf_op jit(solution)/shard_map/all_gather | solution.py:204
  23.9 14.8 %collective-permute-start.2 = (bf16[32,16,384]{2,1,0:T(8,128)(2,1)S(1)}, bf16[32,16,384]{2,1,0:T(8,128)(2,1)S(1)}, u32[]{:S(2)}, u32[]{:S(2)}) collective-permute-start(bf16[32,16,384]{2,1,0:T(8,128)(2,1)S(1)} %get-tuple-element.14.a), channel_id=1, source_target_pairs={{0,384},{128,0},{256,128},{384,256},{1,385},{129,1},{257,129},{385... | collective-permute-start | bytes 1179656 | tf_op jit(solution)/shard_map/ppermute | solution.py:198
  29.1 33.4 %collective-permute-start.1 = (bf16[32,16,384]{2,1,0:T(8,128)(2,1)S(1)}, bf16[32,16,384]{2,1,0:T(8,128)(2,1)S(1)}, u32[]{:S(2)}, u32[]{:S(2)}) collective-permute-start(bf16[32,16,384]{2,1,0:T(8,128)(2,1)S(1)} %get-tuple-element.14.a), channel_id=1, source_target_pairs={{0,256},{128,384},{256,0},{384,128},{1,257},{129,385},{257,1},{385... | collective-permute-start | bytes 1179656 | tf_op jit(solution)/shard_map/ppermute | solution.py:198
  31.0 31.5 %collective-permute-start = (bf16[32,16,384]{2,1,0:T(8,128)(2,1)S(1)}, bf16[32,16,384]{2,1,0:T(8,128)(2,1)S(1)}, u32[]{:S(2)}, u32[]{:S(2)}) collective-permute-start(bf16[32,16,384]{2,1,0:T(8,128)(2,1)S(1)} %get-tuple-element.14.a), channel_id=1, source_target_pairs={{0,128},{128,256},{256,384},{384,0},{1,129},{129,257},{257,385},{3... | collective-permute-start | bytes 1179656 | tf_op jit(solution)/shard_map/ppermute | solution.py:198
  69.8 57.5 %all-to-all-start = ((bf16[128,16,384]{2,1,0:T(8,128)(2,1)}), bf16[128,16,384]{2,1,0:T(8,128)(2,1)S(1)}, u32[]{:S(2)}, u32[]{:S(2)}) async-start(bf16[128,16,384]{2,1,0:T(8,128)(2,1)} %shard_map.103), calls=%async_computation | async-start | bytes 3145728 | tf_op jit(solution)/shard_map/all_to_all | solution.py:212
  130.7 3.9 %collective-permute-start.4 = (bf16[2304,128]{1,0:T(8,128)(2,1)S(1)}, bf16[2304,128]{1,0:T(8,128)(2,1)S(1)}, u32[]{:S(2)}, u32[]{:S(2)}) collective-permute-start(bf16[2304,128]{1,0:T(8,128)(2,1)S(1)} %get-tuple-element.20), channel_id=1, source_target_pairs={{0,1},{1,0},{2,3},{3,2},{4,5},{5,4},{6,7},{7,6},{8,9},{9,8},{10,11... | collective-permute-start | bytes 1769480 | tf_op jit(solution)/shard_map/ppermute | solution.py:223
Sparse Core Ops, SparseCore 0:
  24.0 41.1 all-gather.2
  67.3 34.6 all-gather.4

commit v5 on v4

--- a/solution.py
+++ b/solution.py
@@ -16,18 +16,44 @@
 ALONG = ("y", "zh", "x", "c")
 EXPERT_COUNT = 16
 EXTRA = 128
-ROOM = 32
-
-
-def place_slabs(places, parts):
+
+
+def extend_rows(tokens, routed, gates):
+    _, row_count, depth = tokens.shape
+    top = routed.shape[2]
+
+    def kernel(tokens_ref, routed_ref, gates_ref, out_ref):
+        lane = lax.broadcasted_iota(jnp.int32, (row_count, EXTRA), 1)
+        expert = jnp.where(lane < EXPERT_COUNT, lane, lane - EXPERT_COUNT)
+        routed_here, gates_here = routed_ref[0], gates_ref[0]
+        coefficient = jnp.zeros((row_count, EXTRA), jnp.float32)
+        for k in range(top):
+            named = routed_here[:, k : k + 1] == expert
+            coefficient += jnp.where(named, gates_here[:, k : k + 1], 0.0)
+        high = coefficient.astype(jnp.bfloat16).astype(jnp.float32)
+        extra = jnp.where(lane < EXPERT_COUNT, high, coefficient - high)
+        out_ref[:, :depth] = tokens_ref[0]
+        out_ref[:, depth:] = jnp.where(lane < 2 * EXPERT_COUNT, extra, 0.0).astype(jnp.bfloat16)
+
+    return pl.pallas_call(
+        kernel,
+        out_shape=jax.ShapeDtypeStruct((row_count, depth + EXTRA), jnp.bfloat16),
+        in_specs=[pl.BlockSpec(memory_space=pltpu.VMEM)] * 3,
+        out_specs=pl.BlockSpec(memory_space=pltpu.VMEM),
+    )(tokens, routed, gates)
+
+
+def place_slabs(group, placement, parts):
     count, rows, cols = parts[0].shape
     total = count * len(parts)
 
-    def kernel(places_ref, a, b, c, d, out_ref):
+    def kernel(group_ref, placement_ref, a, b, c, d, out_ref):
+        own = group_ref[0]
         for k, ref in enumerate((a, b, c, d)):
-
-            def body(i, _, k=k, ref=ref):
-                out_ref[places_ref[k * count + i]] = ref[i]
+            base = ((own + len(parts) - k) % len(parts)) * count
+
+            def body(i, _, ref=ref, base=base):
+                out_ref[placement_ref[own, base + i]] = ref[i]
                 return 0
 
             lax.fori_loop(0, count, body, 0, unroll=8)
@@ -35,28 +61,41 @@
     return pl.pallas_call(
         kernel,
         out_shape=jax.ShapeDtypeStruct((total, rows, cols), parts[0].dtype),
-        in_specs=[pl.BlockSpec(memory_space=pltpu.SMEM)] + [pl.BlockSpec(memory_space=pltpu.VMEM)] * 4,
+        in_specs=[pl.BlockSpec(memory_space=pltpu.SMEM)] * 2 + [pl.BlockSpec(memory_space=pltpu.VMEM)] * 4,
         out_specs=pl.BlockSpec(memory_space=pltpu.VMEM),
         compiler_params=pltpu.CompilerParams(vmem_limit_bytes=16 * 2**20),
-    )(places, *parts)
+    )(group, placement, *parts)
 
 
 def hidden_units(expert_id, pick, rows_ext, weights):
     row_count = rows_ext.shape[0]
     depth = weights.shape[0]
     half = row_count // CORES
+    blocks = 8
+    block, piece = row_count // blocks, depth // blocks
 
     def kernel(expert_ref, pick_ref, rows_hbm, w_ref, send_ref, keep_ref, slab_hbm, rows_ref, scaled_ref, sems):
-        rows_copy = pltpu.make_async_copy(rows_hbm, rows_ref, sems.at[0])
-        rows_copy.start()
-        slab_copy = pltpu.make_async_copy(w_ref, slab_hbm, sems.at[1])
-        slab_copy.start()
+        rows_copies = [
+            pltpu.make_async_copy(
+                rows_hbm.at[pl.ds(k * block, block)], rows_ref.at[pl.ds(k * block, block)], sems.at[k]
+            )
+            for k in range(blocks)
+        ]
+        slab_copies = [
+            pltpu.make_async_copy(
+                w_ref.at[pl.ds(k * piece, piece)], slab_hbm.at[pl.ds(k * piece, piece)], sems.at[blocks + k]
+            )
+            for k in range(blocks)
+        ]
+        for copy in rows_copies + slab_copies:
+            copy.start()
         send_ref[half:, :] = w_ref[:, 256:]
         keep_ref[half:, :] = w_ref[:, 256:]
         expert = expert_ref[0]
         lane = lax.broadcasted_iota(jnp.int32, (1, EXTRA), 1)
         own = jnp.where((lane == expert) | (lane == expert + EXPERT_COUNT), 1.0, 0.0)
-        rows_copy.wait()
+        for copy in rows_copies:
+            copy.wait()
         gate_up = jnp.dot(
             rows_ref[:, :depth], w_ref[:, :256], preferred_element_type=jnp.float32
         )
@@ -69,7 +108,8 @@
         picked = picked.astype(jnp.bfloat16)
         send_ref[:half, :] = picked[:half]
         keep_ref[:half, :] = picked[half:]
-        slab_copy.wait()
+        for copy in slab_copies:
+            copy.wait()
 
     return pl.pallas_call(
         kernel,
@@ -85,7 +125,7 @@
         scratch_shapes=[
             pltpu.VMEM(rows_ext.shape, jnp.bfloat16),
             pltpu.VMEM((row_count, 128), jnp.bfloat16),
-            pltpu.SemaphoreType.DMA((2,)),
+            pltpu.SemaphoreType.DMA((2 * blocks,)),
         ],
         compiler_params=pltpu.CompilerParams(vmem_limit_bytes=50 * 2**20),
     )(expert_id, pick, rows_ext, weights)
@@ -166,16 +206,10 @@
     core = lax.axis_index("c")
     place = lax.axis_index(ALONG)
     row_count, depth = tokens.shape[1:]
-    width = depth + EXTRA
-
-    experts = jnp.arange(EXPERT_COUNT, dtype=jnp.int32)
-    named = routed_expert_index[0][:, :, None] == experts[None, None, :]
-    coefficient = jnp.sum(jnp.where(named, gate_weights[0][:, :, None], 0.0), axis=1)
-    high = coefficient.astype(jnp.bfloat16)
-    low = (coefficient - high.astype(jnp.float32)).astype(jnp.bfloat16)
-    fill = jnp.zeros((row_count, EXTRA - 2 * EXPERT_COUNT), jnp.bfloat16)
-    own_rows = jnp.concatenate([tokens[0], high, low, fill], axis=1)
+
+    own_rows = extend_rows(tokens, routed_expert_index, gate_weights)
     other_rows = lax.ppermute(own_rows, "zh", [(0, 1), (1, 0)])
+
     grad_float = gradient.astype(jnp.float32)
     first_new = beta_one * first_moment + (1.0 - beta_one) * grad_float
     second_new = beta_two * second_moment + (1.0 - beta_two) * grad_float * grad_float
@@ -188,11 +222,8 @@
     rounded = master_out.astype(jnp.bfloat16)
 
     other_rows, _ = lax.optimization_barrier((other_rows, rounded))
-    first = lax.axis_index("zh") == 0
-    pair = jnp.concatenate(
-        [jnp.where(first, own_rows, other_rows), jnp.where(first, other_rows, own_rows)], axis=0
-    )
-    column = lax.all_gather(jnp.pad(pair, ((0, ROOM - ZHS * row_count), (0, 0))), "y", axis=0, tiled=True)
+    pair = jnp.concatenate([own_rows, other_rows], axis=0)
+    column = lax.all_gather(pair, "y", axis=0, tiled=True)
 
     parts = [rounded] + [
         lax.ppermute(rounded, "g", [(i, (i + s) % GROUPS) for i in range(GROUPS)])
@@ -200,22 +231,22 @@
     ]
     parts, column = lax.optimization_barrier((parts, column))
 
-    column = column.reshape(YS, ROOM, width)[:, : ZHS * row_count].reshape(-1, width)
     all_rows = lax.all_gather(column, ("x", "c"), axis=0, tiled=True)
 
     unit_count = placement.shape[1]
     unit_ids = jnp.arange(unit_count, dtype=jnp.int32)
     own_row = lax.dynamic_index_in_dim(placement, group, 0, keepdims=False)
-    by_group = own_row.reshape(GROUPS, -1)
-    places = jnp.take(by_group, (group - jnp.arange(GROUPS)) % GROUPS, axis=0).reshape(-1)
-    ordered = place_slabs(places, parts)
+    ordered = place_slabs(jnp.full((1,), group, jnp.int32), placement, parts)
     own_slab = lax.all_to_all(ordered, ALONG, split_axis=0, concat_axis=0, tiled=True)
     weights = own_slab.reshape(depth, -1)
 
-    by_place = jnp.arange(all_rows.shape[0], dtype=jnp.int32).reshape(XS, CORES, YS * ZHS, row_count)
-    by_place = by_place.transpose(1, 2, 0, 3).reshape(CORES, -1)
-    source = jnp.where(core == 0, by_place[::-1], by_place).reshape(-1)
-    pick = (source[:, None] == jnp.arange(all_rows.shape[0], dtype=jnp.int32)[None, :]).astype(jnp.bfloat16)
+    row_ids = jnp.arange(all_rows.shape[0], dtype=jnp.int32)
+    half = all_rows.shape[0] // CORES
+    i, x, y_zh = row_ids % row_count, row_ids // row_count % XS, row_ids % half // (row_count * XS)
+    of_core = jnp.where(row_ids < half, 1 - core, core)
+    here = lax.axis_index("zh")
+    source = ((x * CORES + of_core) * (YS * ZHS) + (y_zh ^ here)) * row_count + i
+    pick = (source[:, None] == row_ids[None, :]).astype(jnp.bfloat16)
 
     slabs_each = unit_count // EXPERT_COUNT
     expert_id = jnp.sum(jnp.where(own_row == place, unit_ids, 0), keepdims=True) // slabs_each

time: 183 us -> 174 us (0.951)
  waiting for transfers between devices: 72.3 us -> 41.6 us
  blocking collectives: 39.1 us -> 67.6 us
  local copies, waits for them, and re-layouts: 3.56 us -> 0.01 us
  starting transfers between devices: 37.6 us -> 34.5 us
    ppermute x3, waiting for transfers between devices: 28.5 us -> 0.04 us  [per_device(): lax.ppermute(rounded, 'g', [(i, (i + s) % GROUPS) for i in range(GROUPS)])]
    all_gather x0 -> x1, blocking collectives: none -> 28.4 us  [per_device(): column = lax.all_gather(pair, 'y', axis=0, tiled=True)]
    all_to_all x1, starting transfers between devices: 14.4 us -> 11.4 us  [per_device(): lax.all_to_all(ordered, ALONG, split_axis=0, concat_axis=0, tiled=True)]
    all_gather x1 -> x0, waiting for transfers between devices: 2.65 us -> none  [per_device(): lax.all_gather(jnp.pad(pair, ((0, ROOM - ZHS * row_count), (0, 0))), 'y',...]
    reshape x4 -> x0, local copies, waits for them, and re-layouts: 1.99 us -> none  [the longest x1 1.68 us: per_device(): column.reshape(YS, ROOM, width)[:, :ZHS * row_count].reshape(-1, width)]
  transfers between devices with their start and end apart: 8 -> 7, of which waited for: 5 -> 2; matrix products, arithmetic and copies ran while one was open for 3% -> 2% of each run, Pallas kernels for 1% -> 1%
where the time goes in v5:
time: 174 us; the launch traced here: 173 us
  blocking collectives  67.6 us (39%)
  waiting for transfers between devices  41.6 us (24%)
  starting transfers between devices  34.5 us (20%)
  between operations  16.8 us (10%)
  Pallas kernels  8.62 us (5%)
  other arithmetic  4.04 us (2%)
    all_to_all x1, waiting for transfers between devices, per_device(): lax.all_to_all(ordered, ALONG, split_axis=0, concat_axis=0, tiled=True)  39.6 us
    all_to_all x1, blocking collectives, per_device(): lax.all_to_all(chunks, ('y', 'zh', 'x'), split_axis=0, concat_axis=0, til...  39.2 us
    all_gather x1, blocking collectives, per_device(): column = lax.all_gather(pair, 'y', axis=0, tiled=True)  28.4 us
    all_to_all x1, starting transfers between devices, per_device(): lax.all_to_all(ordered, ALONG, split_axis=0, concat_axis=0, tiled=True)  11.4 us
    ppermute x1, starting transfers between devices, per_device(): other_rows = lax.ppermute(own_rows, 'zh', [(0, 1), (1, 0)])  11 us
    ppermute x3, starting transfers between devices, per_device(): lax.ppermute(rounded, 'g', [(i, (i + s) % GROUPS) for i in range(GROUPS)])  10.1 us
    pallas_call x1, Pallas kernels, hidden_units(): pl.pallas_call(kernel, out_shape=(jax.ShapeDtypeStruct((half + depth, 128...  3.51 us
  transfers between devices with their start and end apart: 7, of which 2 were waited for; matrix products, arithmetic and copies ran while one was open for 2% of the time, Pallas kernels for 1%

profile of v5, /device:TPU:6, one launch (start us, length us, event | category | flops | bytes accessed | tf_op | source)
XLA Modules:
  0.0 173.2 jit_solution(7392850170065412223)
XLA Ops:
  7.2 0.0 all-gather.2.cloned.1.call-start
  7.2 1.4 shard_map.103
  8.7 0.0 copy-start.1
  8.7 0.0 copy-start
  8.7 11.0 %collective-permute-start.3 = (bf16[4,2176]{1,0:T(4,128)(2,1)}, bf16[4,2176]{1,0:T(4,128)(2,1)S(1)}, u32[]{:S(2)}, u32[]{:S(2)}) collective-permute-start(bf16[4,2176]{1,0:T(4,128)(2,1)} %shard_map.103), channel_id=1, source_target_pairs={{0,8},{8,0},{1,9},{9,1},{2,10},{10,2},{3,11},{11,3},{4,12},{12,4},... | collective-permute-start | bytes 52232 | tf_op jit(solution)/shard_map/ppermute | solution.py:211
  19.7 3.2 %fusion.32 = (bf16[32,16,384]{2,1,0:T(8,128)(2,1)S(1)}, f32[32,16,384]{2,1,0:T(8,128)}) fusion(f32[32,16,384]{2,1,0:T(8,128)} %param.8, f32[32,16,384]{2,1,0:T(8,128)} %param.10, bf16[32,16,384]{2,1,0:T(8,128)(2,1)} %param.11, f32[32,16,384]{2,1,0:T(8,128)} %param.9), kind=kLoop, calls=%fused_computation.52 | loop fusion | flops 3145728 | bytes 3932160 | tf_op jit(solution)/shard_map/convert_element_type | solution.py:222
  22.9 5.2 %collective-permute-start.2 = (bf16[32,16,384]{2,1,0:T(8,128)(2,1)S(1)}, bf16[32,16,384]{2,1,0:T(8,128)(2,1)S(1)}, u32[]{:S(2)}, u32[]{:S(2)}) collective-permute-start(bf16[32,16,384]{2,1,0:T(8,128)(2,1)S(1)} %get-tuple-element.14.a), channel_id=1, source_target_pairs={{0,384},{128,0},{256,128},{384,256},{1,385},{129,1},{257,129},{385... | collective-permute-start | bytes 1179656 | tf_op jit(solution)/shard_map/ppermute | solution.py:229
  28.1 1.9 %collective-permute-start.1 = (bf16[32,16,384]{2,1,0:T(8,128)(2,1)S(1)}, bf16[32,16,384]{2,1,0:T(8,128)(2,1)S(1)}, u32[]{:S(2)}, u32[]{:S(2)}) collective-permute-start(bf16[32,16,384]{2,1,0:T(8,128)(2,1)S(1)} %get-tuple-element.14.a), channel_id=1, source_target_pairs={{0,256},{128,384},{256,0},{384,128},{1,257},{129,385},{257,1},{385... | collective-permute-start | bytes 1179656 | tf_op jit(solution)/shard_map/ppermute | solution.py:229
  30.0 3.0 %collective-permute-start = (bf16[32,16,384]{2,1,0:T(8,128)(2,1)S(1)}, bf16[32,16,384]{2,1,0:T(8,128)(2,1)S(1)}, u32[]{:S(2)}, u32[]{:S(2)}) collective-permute-start(bf16[32,16,384]{2,1,0:T(8,128)(2,1)S(1)} %get-tuple-element.14.a), channel_id=1, source_target_pairs={{0,128},{128,256},{256,384},{384,0},{1,129},{129,257},{257,385},{3... | collective-permute-start | bytes 1179656 | tf_op jit(solution)/shard_map/ppermute | solution.py:229
  33.1 0.0 collective-permute-done.3
  33.1 0.0 copy-done.1
  33.1 28.4 %all_gather.6 = bf16[64,2176]{1,0:T(8,128)(2,1)} all-gather(bf16[8,2176]{1,0:T(8,128)(2,1)S(1)} %pad_maximum_fusion), channel_id=1, replica_groups=mesh['g'=4,'y'=8,'zh'=2,'x'=4,'c'=2] {'y'}, dimensions={0}, use_global_device_ids=true | all-gather | bytes 313344 | tf_op jit(solution)/shard_map/all_gather | solution.py:226
  61.5 0.0 collective-permute-done.2.d
  61.5 0.0 collective-permute-done.1.c
  61.6 0.0 collective-permute-done.b
  61.6 0.0 all-gather.2.cloned.1.call-update
  61.6 0.0 copy-done
  61.6 2.2 %shard_map.104 = bf16[128,16,384]{2,1,0:T(8,128)(2,1)} custom-call(s32[1]{0:T(128)} %bitcast.2.group_ref, s32[4,128]{1,0:T(4,128)S(1)} %copy-done, bf16[32,16,384]{2,1,0:T(8,128)(2,1)S(1)} %get-tuple-element.14.a, bf16[32,16,384]{2,1,0:T(8,128)(2,1)S(1)} %collective-permute-done.b, bf16[32,16,384]{2,1,0:T(8,128)(2,1)S(1)} %collective-permute-done.1.c, ...), custom_call_target="tpu_custom_call" | custom-call | tf_op jit(solution)/shard_map/pallas_call | solution.py:61
  63.8 11.4 %all-to-all-start = ((bf16[128,16,384]{2,1,0:T(8,128)(2,1)}), bf16[128,16,384]{2,1,0:T(8,128)(2,1)S(1)}, u32[]{:S(2)}, u32[]{:S(2)}) async-start(bf16[128,16,384]{2,1,0:T(8,128)(2,1)} %shard_map.104), calls=%async_computation | async-start | bytes 3145728 | tf_op jit(solution)/shard_map/all_to_all | solution.py:240
  75.2 0.6 fusion.31
  78.5 0.2 fusion.pick_ref
  78.6 39.6 %all-to-all-done = bf16[128,16,384]{2,1,0:T(8,128)(2,1)S(1)} async-done(((bf16[128,16,384]{2,1,0:T(8,128)(2,1)}), bf16[128,16,384]{2,1,0:T(8,128)(2,1)S(1)}, u32[]{:S(2)}, u32[]{:S(2)}) %all-to-all-start) | async-done | bytes 1572896 | tf_op jit(solution)/shard_map/all_to_all | solution.py:240
  118.2 0.0 all-gather.2.cloned.1.call-done.rows_hbm
  118.2 3.5 %shard_map.105 = (bf16[2304,128]{1,0:T(8,128)(2,1)S(1)}, bf16[2304,128]{1,0:T(8,128)(2,1)S(1)}, bf16[2048,384]{1,0:T(8,128)(2,1)}) custom-call(s32[1]{0:T(128)S(6)} %select_n.66.expert_ref, bf16[512,512]{1,0:T(8,128)(2,1)S(1)} %fusion.pick_ref, bf16[512,2176]{1,0:T(8,128)(2,1)} %all-gather.2.cloned.1.call-done.rows_hbm, bf16[2048,384]{1,0:T(8,128)(2,1)S(1)} %bitcast.10), custom_call_target="tpu_custom_call" | custom-call | tf_op jit(solution)/shard_map/pallas_call | solution.py:114
  121.8 1.9 %collective-permute-start.4 = (bf16[2304,128]{1,0:T(8,128)(2,1)S(1)}, bf16[2304,128]{1,0:T(8,128)(2,1)S(1)}, u32[]{:S(2)}, u32[]{:S(2)}) collective-permute-start(bf16[2304,128]{1,0:T(8,128)(2,1)S(1)} %get-tuple-element.20), channel_id=1, source_target_pairs={{0,1},{1,0},{2,3},{3,2},{4,5},{5,4},{6,7},{7,6},{8,9},{9,8},{10,11... | collective-permute-start | bytes 1769480 | tf_op jit(solution)/shard_map/ppermute | solution.py:254
  123.7 2.0 %collective-permute-done.4.recv_ref = bf16[2304,128]{1,0:T(8,128)(2,1)S(1)} collective-permute-done((bf16[2304,128]{1,0:T(8,128)(2,1)S(1)}, bf16[2304,128]{1,0:T(8,128)(2,1)S(1)}, u32[]{:S(2)}, u32[]{:S(2)}) %collective-permute-start.4) | collective-permute-done | bytes 589856 | tf_op jit(solution)/shard_map/ppermute | solution.py:254
  125.7 0.7 shard_map.106
  126.4 39.2 %all_to_all.10.ref = bf16[64,64,128]{2,1,0:T(8,128)(2,1)S(1)} all-to-all(bf16[64,64,128]{2,1,0:T(8,128)(2,1)S(1)} %bitcast.11), channel_id=1, replica_groups=mesh['g'=4,'y'=8,'zh'=2,'x'=4,'c'=2] {'y','zh','x'}, dimensions={0} | all-to-all | bytes 2097152 | tf_op jit(solution)/shard_map/all_to_all | solution.py:256
  165.5 0.8 shard_map.107
  (2 shorter events, 0.0 us)
Async XLA Ops:
  7.2 111.1 %all-gather.2.cloned.1.call-start = ((), (), s32[]{:S(2)}) async-start(), calls=%async_computation.2 | async-start | bytes 2506752 | tf_op jit(solution)/shard_map/all_gather | solution.py:234
  8.7 24.4 %copy-start.1 = (bf16[4,2176]{1,0:T(4,128)(2,1)S(1)}, bf16[4,2176]{1,0:T(4,128)(2,1)}, u32[]{:S(2)}) copy-start(bf16[4,2176]{1,0:T(4,128)(2,1)} %shard_map.103) | copy-start | bytes 52228
  8.7 52.9 %copy-start = (s32[4,128]{1,0:T(4,128)S(1)}, s32[4,128]{1,0:T(4,128)}, u32[]{:S(2)}) copy-start(s32[4,128]{1,0:T(4,128)} %placement_ref.1) | copy-start | bytes 6148
  8.7 24.4 %collective-permute-start.3 = (bf16[4,2176]{1,0:T(4,128)(2,1)}, bf16[4,2176]{1,0:T(4,128)(2,1)S(1)}, u32[]{:S(2)}, u32[]{:S(2)}) collective-permute-start(bf16[4,2176]{1,0:T(4,128)(2,1)} %shard_map.103), channel_id=1, source_target_pairs={{0,8},{8,0},{1,9},{9,1},{2,10},{10,2},{3,11},{11,3},{4,12},{12,4},... | collective-permute-start | bytes 52232 | tf_op jit(solution)/shard_map/ppermute | solution.py:211
  22.9 38.6 %collective-permute-start.2 = (bf16[32,16,384]{2,1,0:T(8,128)(2,1)S(1)}, bf16[32,16,384]{2,1,0:T(8,128)(2,1)S(1)}, u32[]{:S(2)}, u32[]{:S(2)}) collective-permute-start(bf16[32,16,384]{2,1,0:T(8,128)(2,1)S(1)} %get-tuple-element.14.a), channel_id=1, source_target_pairs={{0,384},{128,0},{256,128},{384,256},{1,385},{129,1},{257,129},{385... | collective-permute-start | bytes 1179656 | tf_op jit(solution)/shard_map/ppermute | solution.py:229
  28.1 33.4 %collective-permute-start.1 = (bf16[32,16,384]{2,1,0:T(8,128)(2,1)S(1)}, bf16[32,16,384]{2,1,0:T(8,128)(2,1)S(1)}, u32[]{:S(2)}, u32[]{:S(2)}) collective-permute-start(bf16[32,16,384]{2,1,0:T(8,128)(2,1)S(1)} %get-tuple-element.14.a), channel_id=1, source_target_pairs={{0,256},{128,384},{256,0},{384,128},{1,257},{129,385},{257,1},{385... | collective-permute-start | bytes 1179656 | tf_op jit(solution)/shard_map/ppermute | solution.py:229
  30.0 31.5 %collective-permute-start = (bf16[32,16,384]{2,1,0:T(8,128)(2,1)S(1)}, bf16[32,16,384]{2,1,0:T(8,128)(2,1)S(1)}, u32[]{:S(2)}, u32[]{:S(2)}) collective-permute-start(bf16[32,16,384]{2,1,0:T(8,128)(2,1)S(1)} %get-tuple-element.14.a), channel_id=1, source_target_pairs={{0,128},{128,256},{256,384},{384,0},{1,129},{129,257},{257,385},{3... | collective-permute-start | bytes 1179656 | tf_op jit(solution)/shard_map/ppermute | solution.py:229
  63.8 54.4 %all-to-all-start = ((bf16[128,16,384]{2,1,0:T(8,128)(2,1)}), bf16[128,16,384]{2,1,0:T(8,128)(2,1)S(1)}, u32[]{:S(2)}, u32[]{:S(2)}) async-start(bf16[128,16,384]{2,1,0:T(8,128)(2,1)} %shard_map.104), calls=%async_computation | async-start | bytes 3145728 | tf_op jit(solution)/shard_map/all_to_all | solution.py:240
  121.8 3.9 %collective-permute-start.4 = (bf16[2304,128]{1,0:T(8,128)(2,1)S(1)}, bf16[2304,128]{1,0:T(8,128)(2,1)S(1)}, u32[]{:S(2)}, u32[]{:S(2)}) collective-permute-start(bf16[2304,128]{1,0:T(8,128)(2,1)S(1)} %get-tuple-element.20), channel_id=1, source_target_pairs={{0,1},{1,0},{2,3},{3,2},{4,5},{5,4},{6,7},{7,6},{8,9},{9,8},{10,11... | collective-permute-start | bytes 1769480 | tf_op jit(solution)/shard_map/ppermute | solution.py:254
Sparse Core Ops, SparseCore 0:
  61.7 34.9 all-gather.1

commit v6 on v5

--- a/solution.py
+++ b/solution.py
@@ -18,7 +18,7 @@
 EXTRA = 128
 
 
-def extend_rows(tokens, routed, gates):
+def extend_rows(copies, tokens, routed, gates):
     _, row_count, depth = tokens.shape
     top = routed.shape[2]
 
@@ -32,12 +32,14 @@
             coefficient += jnp.where(named, gates_here[:, k : k + 1], 0.0)
         high = coefficient.astype(jnp.bfloat16).astype(jnp.float32)
         extra = jnp.where(lane < EXPERT_COUNT, high, coefficient - high)
-        out_ref[:, :depth] = tokens_ref[0]
-        out_ref[:, depth:] = jnp.where(lane < 2 * EXPERT_COUNT, extra, 0.0).astype(jnp.bfloat16)
-
-    return pl.pallas_call(
-        kernel,
-        out_shape=jax.ShapeDtypeStruct((row_count, depth + EXTRA), jnp.bfloat16),
+        extra = jnp.where(lane < 2 * EXPERT_COUNT, extra, 0.0).astype(jnp.bfloat16)
+        for k in range(copies):
+            out_ref[k, :, :depth] = tokens_ref[0]
+            out_ref[k, :, depth:] = extra
+
+    return pl.pallas_call(
+        kernel,
+        out_shape=jax.ShapeDtypeStruct((copies, row_count, depth + EXTRA), jnp.bfloat16),
         in_specs=[pl.BlockSpec(memory_space=pltpu.VMEM)] * 3,
         out_specs=pl.BlockSpec(memory_space=pltpu.VMEM),
     )(tokens, routed, gates)
@@ -67,47 +69,34 @@
     )(group, placement, *parts)
 
 
-def hidden_units(expert_id, pick, rows_ext, weights):
-    row_count = rows_ext.shape[0]
+def hidden_units(expert_id, pick, own_rows, other_rows, weights):
+    half = own_rows.shape[0]
     depth = weights.shape[0]
-    half = row_count // CORES
-    blocks = 8
-    block, piece = row_count // blocks, depth // blocks
-
-    def kernel(expert_ref, pick_ref, rows_hbm, w_ref, send_ref, keep_ref, slab_hbm, rows_ref, scaled_ref, sems):
-        rows_copies = [
+    blocks = 4
+    piece = depth // blocks
+
+    def kernel(expert_ref, pick_ref, own_ref, other_ref, w_ref, send_ref, keep_ref, slab_hbm, sems):
+        slab_copies = [
             pltpu.make_async_copy(
-                rows_hbm.at[pl.ds(k * block, block)], rows_ref.at[pl.ds(k * block, block)], sems.at[k]
+                w_ref.at[pl.ds(k * piece, piece)], slab_hbm.at[pl.ds(k * piece, piece)], sems.at[k]
             )
             for k in range(blocks)
         ]
-        slab_copies = [
-            pltpu.make_async_copy(
-                w_ref.at[pl.ds(k * piece, piece)], slab_hbm.at[pl.ds(k * piece, piece)], sems.at[blocks + k]
-            )
-            for k in range(blocks)
-        ]
-        for copy in rows_copies + slab_copies:
+        for copy in slab_copies:
             copy.start()
-        send_ref[half:, :] = w_ref[:, 256:]
-        keep_ref[half:, :] = w_ref[:, 256:]
         expert = expert_ref[0]
         lane = lax.broadcasted_iota(jnp.int32, (1, EXTRA), 1)
         own = jnp.where((lane == expert) | (lane == expert + EXPERT_COUNT), 1.0, 0.0)
-        for copy in rows_copies:
-            copy.wait()
-        gate_up = jnp.dot(
-            rows_ref[:, :depth], w_ref[:, :256], preferred_element_type=jnp.float32
-        )
-        gate, up = gate_up[:, :128], gate_up[:, 128:]
-        hidden = (gate / (1.0 + jnp.exp(-gate)) * up).astype(jnp.bfloat16).astype(jnp.float32)
-        extra = rows_ref[:, depth:].astype(jnp.float32)
-        coefficient = jnp.sum(extra * own, axis=1, keepdims=True)
-        scaled_ref[...] = (hidden * coefficient).astype(jnp.bfloat16)
-        picked = jnp.dot(pick_ref[...], scaled_ref[...], preferred_element_type=jnp.float32)
-        picked = picked.astype(jnp.bfloat16)
-        send_ref[:half, :] = picked[:half]
-        keep_ref[:half, :] = picked[half:]
+        for rows_ref, out_ref in ((other_ref, send_ref), (own_ref, keep_ref)):
+            gate_up = jnp.dot(rows_ref[:, :depth], w_ref[:, :256], preferred_element_type=jnp.float32)
+            gate, up = gate_up[:, :128], gate_up[:, 128:]
+            hidden = (gate / (1.0 + jnp.exp(-gate)) * up).astype(jnp.bfloat16).astype(jnp.float32)
+            extra = rows_ref[:, depth:].astype(jnp.float32)
+            coefficient = jnp.sum(extra * own, axis=1, keepdims=True)
+            scaled = (hidden * coefficient).astype(jnp.bfloat16)
+            ordered = jnp.dot(pick_ref[...], scaled, preferred_element_type=jnp.float32)
+            out_ref[:half, :] = ordered.astype(jnp.bfloat16)
+            out_ref[half:, :] = w_ref[:, 256:]
         for copy in slab_copies:
             copy.wait()
 
@@ -115,20 +104,11 @@
         kernel,
         out_shape=(jax.ShapeDtypeStruct((half + depth, 128), jnp.bfloat16),) * 2
         + (jax.ShapeDtypeStruct(weights.shape, jnp.bfloat16),),
-        in_specs=[
-            pl.BlockSpec(memory_space=pltpu.SMEM),
-            pl.BlockSpec(memory_space=pltpu.VMEM),
-            pl.BlockSpec(memory_space=pltpu.HBM),
-            pl.BlockSpec(memory_space=pltpu.VMEM),
-        ],
+        in_specs=[pl.BlockSpec(memory_space=pltpu.SMEM)] + [pl.BlockSpec(memory_space=pltpu.VMEM)] * 4,
         out_specs=(pl.BlockSpec(memory_space=pltpu.VMEM),) * 2 + (pl.BlockSpec(memory_space=pltpu.HBM),),
-        scratch_shapes=[
-            pltpu.VMEM(rows_ext.shape, jnp.bfloat16),
-            pltpu.VMEM((row_count, 128), jnp.bfloat16),
-            pltpu.SemaphoreType.DMA((2 * blocks,)),
-        ],
-        compiler_params=pltpu.CompilerParams(vmem_limit_bytes=50 * 2**20),
-    )(expert_id, pick, rows_ext, weights)
+        scratch_shapes=[pltpu.SemaphoreType.DMA((blocks,))],
+        compiler_params=pltpu.CompilerParams(vmem_limit_bytes=24 * 2**20),
+    )(expert_id, pick, own_rows, other_rows, weights)
 
 
 def pair_outputs(kept, received):
@@ -203,11 +183,10 @@
     gate_weights,
 ):
     group = lax.axis_index("g")
-    core = lax.axis_index("c")
     place = lax.axis_index(ALONG)
     row_count, depth = tokens.shape[1:]
 
-    own_rows = extend_rows(tokens, routed_expert_index, gate_weights)
+    own_rows = extend_rows(1, tokens, routed_expert_index, gate_weights)[0]
     other_rows = lax.ppermute(own_rows, "zh", [(0, 1), (1, 0)])
 
     grad_float = gradient.astype(jnp.float32)
@@ -220,18 +199,20 @@
     )
     master_out = master_weights - learn_rate * (update + weight_decay * master_weights)
     rounded = master_out.astype(jnp.bfloat16)
-
     other_rows, _ = lax.optimization_barrier((other_rows, rounded))
-    pair = jnp.concatenate([own_rows, other_rows], axis=0)
-    column = lax.all_gather(pair, "y", axis=0, tiled=True)
 
     parts = [rounded] + [
         lax.ppermute(rounded, "g", [(i, (i + s) % GROUPS) for i in range(GROUPS)])
         for s in range(1, GROUPS)
     ]
+
+    pair = jnp.concatenate([own_rows, other_rows], axis=0)
+    column = lax.all_gather(pair, "y", axis=0, tiled=True)
     parts, column = lax.optimization_barrier((parts, column))
 
-    all_rows = lax.all_gather(column, ("x", "c"), axis=0, tiled=True)
+    others = [lax.ppermute(column, "x", [(k, (k + t) % XS) for k in range(XS)]) for t in range(1, XS)]
+    own_rows = jnp.concatenate([column] + others, axis=0)
+    other_rows = lax.ppermute(own_rows, "c", [(0, 1), (1, 0)])
 
     unit_count = placement.shape[1]
     unit_ids = jnp.arange(unit_count, dtype=jnp.int32)
@@ -240,17 +221,15 @@
     own_slab = lax.all_to_all(ordered, ALONG, split_axis=0, concat_axis=0, tiled=True)
     weights = own_slab.reshape(depth, -1)
 
-    row_ids = jnp.arange(all_rows.shape[0], dtype=jnp.int32)
-    half = all_rows.shape[0] // CORES
-    i, x, y_zh = row_ids % row_count, row_ids // row_count % XS, row_ids % half // (row_count * XS)
-    of_core = jnp.where(row_ids < half, 1 - core, core)
-    here = lax.axis_index("zh")
-    source = ((x * CORES + of_core) * (YS * ZHS) + (y_zh ^ here)) * row_count + i
+    row_ids = jnp.arange(own_rows.shape[0], dtype=jnp.int32)
+    i, x, y_zh = row_ids % row_count, row_ids // row_count % XS, row_ids // (row_count * XS)
+    away = (lax.axis_index("x") + XS - x) % XS
+    source = (away * (YS * ZHS) + (y_zh ^ lax.axis_index("zh"))) * row_count + i
     pick = (source[:, None] == row_ids[None, :]).astype(jnp.bfloat16)
 
     slabs_each = unit_count // EXPERT_COUNT
     expert_id = jnp.sum(jnp.where(own_row == place, unit_ids, 0), keepdims=True) // slabs_each
-    sent, kept, slab = hidden_units(expert_id, pick, all_rows, weights)
+    sent, kept, slab = hidden_units(expert_id, pick, own_rows, other_rows, weights)
     received = lax.ppermute(sent, "c", [(0, 1), (1, 0)])
     chunks = pair_outputs(kept, received)
     chunks = lax.all_to_all(chunks, ("y", "zh", "x"), split_axis=0, concat_axis=0, tiled=True)

time: 174 us -> 162 us (0.931)
  between operations: 16.8 us -> 3.43 us
  starting transfers between devices: 34.5 us -> 46.2 us
  waiting for transfers between devices: 41.6 us -> 31.7 us
    all_to_all x1, waiting for transfers between devices: 39.6 us -> 7.45 us  [per_device(): lax.all_to_all(ordered, ALONG, split_axis=0, concat_axis=0, tiled=True)]
    ppermute x0 -> x4, waiting for transfers between devices: none -> 20.3 us  [the longest x3 20.3 us: per_device(): lax.ppermute(column, 'x', [(k, (k + t) % XS) for k in range(XS)])]
    ppermute x0 -> x4, starting transfers between devices: none -> 11.7 us  [the longest x3 9.82 us: per_device(): lax.ppermute(column, 'x', [(k, (k + t) % XS) for k in range(XS)])]
    all_gather x1, blocking collectives: 28.4 us -> 26.4 us  [per_device(): column = lax.all_gather(pair, 'y', axis=0, tiled=True)]
    ppermute x3, waiting for transfers between devices: 0.04 us -> 2.03 us  [per_device(): lax.ppermute(rounded, 'g', [(i, (i + s) % GROUPS) for i in range(GROUPS)])]
  transfers between devices with their start and end apart: 7 -> 10, of which waited for: 2 -> 4; matrix products, arithmetic and copies ran while one was open for 2% -> 3% of each run, Pallas kernels for 1% -> 0%
where the time goes in v6:
time: 162 us; the launch traced here: 161 us
  blocking collectives  67 us (41%)
  starting transfers between devices  46.2 us (29%)
  waiting for transfers between devices  31.7 us (20%)
  Pallas kernels  8.66 us (5%)
  other arithmetic  4 us (2%)
  between operations  3.43 us (2%)
    all_to_all x1, blocking collectives, per_device(): lax.all_to_all(chunks, ('y', 'zh', 'x'), split_axis=0, concat_axis=0, til...  40.6 us
    all_gather x1, blocking collectives, per_device(): column = lax.all_gather(pair, 'y', axis=0, tiled=True)  26.4 us
    ppermute x3, waiting for transfers between devices, per_device(): lax.ppermute(column, 'x', [(k, (k + t) % XS) for k in range(XS)])  20.3 us
    all_to_all x1, starting transfers between devices, per_device(): lax.all_to_all(ordered, ALONG, split_axis=0, concat_axis=0, tiled=True)  11.4 us
    ppermute x1, starting transfers between devices, per_device(): other_rows = lax.ppermute(own_rows, 'zh', [(0, 1), (1, 0)])  11 us
    ppermute x3, starting transfers between devices, per_device(): lax.ppermute(rounded, 'g', [(i, (i + s) % GROUPS) for i in range(GROUPS)])  10.1 us
    ppermute x3, starting transfers between devices, per_device(): lax.ppermute(column, 'x', [(k, (k + t) % XS) for k in range(XS)])  9.82 us
    all_to_all x1, waiting for transfers between devices, per_device(): lax.all_to_all(ordered, ALONG, split_axis=0, concat_axis=0, tiled=True)  7.45 us
  transfers between devices with their start and end apart: 10, of which 4 were waited for; matrix products, arithmetic and copies ran while one was open for 3% of the time, Pallas kernels for 0%

profile of v6, /device:TPU:6, one launch (start us, length us, event | category | flops | bytes accessed | tf_op | source)
XLA Modules:
  0.0 161.2 jit_solution(8380099669986064331)
XLA Ops:
  0.6 1.4 shard_map.103
  2.1 0.0 copy-start.1
  2.1 0.0 copy-start
  2.1 11.0 %collective-permute-start.3 = (bf16[4,2176]{1,0:T(4,128)(2,1)}, bf16[4,2176]{1,0:T(4,128)(2,1)S(1)}, u32[]{:S(2)}, u32[]{:S(2)}) collective-permute-start(bf16[4,2176]{1,0:T(4,128)(2,1)} %bitcast.13), channel_id=1, source_target_pairs={{0,8},{8,0},{1,9},{9,1},{2,10},{10,2},{3,11},{11,3},{4,12},{12,4},... | collective-permute-start | bytes 52232 | tf_op jit(solution)/shard_map/ppermute | solution.py:190
  13.1 3.2 %fusion.22 = (bf16[32,16,384]{2,1,0:T(8,128)(2,1)S(1)}, f32[32,16,384]{2,1,0:T(8,128)}) fusion(f32[32,16,384]{2,1,0:T(8,128)} %param.8, f32[32,16,384]{2,1,0:T(8,128)} %param.10, bf16[32,16,384]{2,1,0:T(8,128)(2,1)} %param.11, f32[32,16,384]{2,1,0:T(8,128)} %param.9), kind=kLoop, calls=%fused_computation.45 | loop fusion | flops 3145728 | bytes 3932160 | tf_op jit(solution)/shard_map/convert_element_type | solution.py:201
  16.3 5.2 %collective-permute-start.2 = (bf16[32,16,384]{2,1,0:T(8,128)(2,1)S(1)}, bf16[32,16,384]{2,1,0:T(8,128)(2,1)S(1)}, u32[]{:S(2)}, u32[]{:S(2)}) collective-permute-start(bf16[32,16,384]{2,1,0:T(8,128)(2,1)S(1)} %get-tuple-element.14.a), channel_id=1, source_target_pairs={{0,384},{128,0},{256,128},{384,256},{1,385},{129,1},{257,129},{385... | collective-permute-start | bytes 1179656 | tf_op jit(solution)/shard_map/ppermute | solution.py:205
  21.5 1.9 %collective-permute-start.1 = (bf16[32,16,384]{2,1,0:T(8,128)(2,1)S(1)}, bf16[32,16,384]{2,1,0:T(8,128)(2,1)S(1)}, u32[]{:S(2)}, u32[]{:S(2)}) collective-permute-start(bf16[32,16,384]{2,1,0:T(8,128)(2,1)S(1)} %get-tuple-element.14.a), channel_id=1, source_target_pairs={{0,256},{128,384},{256,0},{384,128},{1,257},{129,385},{257,1},{385... | collective-permute-start | bytes 1179656 | tf_op jit(solution)/shard_map/ppermute | solution.py:205
  23.5 3.0 %collective-permute-start = (bf16[32,16,384]{2,1,0:T(8,128)(2,1)S(1)}, bf16[32,16,384]{2,1,0:T(8,128)(2,1)S(1)}, u32[]{:S(2)}, u32[]{:S(2)}) collective-permute-start(bf16[32,16,384]{2,1,0:T(8,128)(2,1)S(1)} %get-tuple-element.14.a), channel_id=1, source_target_pairs={{0,128},{128,256},{256,384},{384,0},{1,129},{129,257},{257,385},{3... | collective-permute-start | bytes 1179656 | tf_op jit(solution)/shard_map/ppermute | solution.py:205
  26.5 0.0 collective-permute-done.3
  26.5 0.0 copy-done.1
  26.5 26.4 %all_gather.3 = bf16[64,2176]{1,0:T(8,128)(2,1)S(1)} all-gather(bf16[8,2176]{1,0:T(8,128)(2,1)S(1)} %pad_maximum_fusion), channel_id=1, replica_groups=mesh['g'=4,'y'=8,'zh'=2,'x'=4,'c'=2] {'y'}, dimensions={0}, use_global_device_ids=true | all-gather | bytes 313344 | tf_op jit(solution)/shard_map/all_gather | solution.py:210
  53.0 0.0 collective-permute-done.2.d
  53.0 2.0 %collective-permute-done.1.c = bf16[32,16,384]{2,1,0:T(8,128)(2,1)S(1)} collective-permute-done((bf16[32,16,384]{2,1,0:T(8,128)(2,1)S(1)}, bf16[32,16,384]{2,1,0:T(8,128)(2,1)S(1)}, u32[]{:S(2)}, u32[]{:S(2)}) %collective-permute-start.1) | collective-permute-done | bytes 393248 | tf_op jit(solution)/shard_map/ppermute | solution.py:205
  55.0 0.0 collective-permute-done.b
  55.0 0.0 copy-done
  55.0 2.2 %shard_map.104 = bf16[128,16,384]{2,1,0:T(8,128)(2,1)} custom-call(s32[1]{0:T(128)} %bitcast.3.group_ref, s32[4,128]{1,0:T(4,128)S(1)} %copy-done, bf16[32,16,384]{2,1,0:T(8,128)(2,1)S(1)} %get-tuple-element.14.a, bf16[32,16,384]{2,1,0:T(8,128)(2,1)S(1)} %collective-permute-done.b, bf16[32,16,384]{2,1,0:T(8,128)(2,1)S(1)} %collective-permute-done.1.c, ...), custom_call_target="tpu_custom_call" | custom-call | tf_op jit(solution)/shard_map/pallas_call | solution.py:63
  57.2 11.4 %all-to-all-start = ((bf16[128,16,384]{2,1,0:T(8,128)(2,1)}), bf16[128,16,384]{2,1,0:T(8,128)(2,1)S(1)}, u32[]{:S(2)}, u32[]{:S(2)}) async-start(bf16[128,16,384]{2,1,0:T(8,128)(2,1)} %shard_map.104), calls=%async_computation | async-start | bytes 3145728 | tf_op jit(solution)/shard_map/all_to_all | solution.py:221
  68.6 2.8 %collective-permute-start.6 = (bf16[64,2176]{1,0:T(8,128)(2,1)S(1)}, bf16[64,2176]{1,0:T(8,128)(2,1)S(1)}, u32[]{:S(2)}, u32[]{:S(2)}) collective-permute-start(bf16[64,2176]{1,0:T(8,128)(2,1)S(1)} %all_gather.3), channel_id=1, source_target_pairs={{0,6},{2,0},{4,2},{6,4},{1,7},{3,1},{5,3},{7,5},{8,14},{10,8},{12,... | collective-permute-start | bytes 835592 | tf_op jit(solution)/shard_map/ppermute | solution.py:213
  71.3 3.4 %collective-permute-start.5 = (bf16[64,2176]{1,0:T(8,128)(2,1)S(1)}, bf16[64,2176]{1,0:T(8,128)(2,1)S(1)}, u32[]{:S(2)}, u32[]{:S(2)}) collective-permute-start(bf16[64,2176]{1,0:T(8,128)(2,1)S(1)} %all_gather.3), channel_id=1, source_target_pairs={{0,4},{2,6},{4,0},{6,2},{1,5},{3,7},{5,1},{7,3},{8,12},{10,14},{12... | collective-permute-start | bytes 835592 | tf_op jit(solution)/shard_map/ppermute | solution.py:213
  74.7 3.6 %collective-permute-start.4 = (bf16[64,2176]{1,0:T(8,128)(2,1)S(1)}, bf16[64,2176]{1,0:T(8,128)(2,1)S(1)}, u32[]{:S(2)}, u32[]{:S(2)}) collective-permute-start(bf16[64,2176]{1,0:T(8,128)(2,1)S(1)} %all_gather.3), channel_id=1, source_target_pairs={{0,2},{2,4},{4,6},{6,0},{1,3},{3,5},{5,7},{7,1},{8,10},{10,12},{12... | collective-permute-start | bytes 835592 | tf_op jit(solution)/shard_map/ppermute | solution.py:213
  78.4 20.3 %collective-permute-done.4 = bf16[64,2176]{1,0:T(8,128)(2,1)S(1)} collective-permute-done((bf16[64,2176]{1,0:T(8,128)(2,1)S(1)}, bf16[64,2176]{1,0:T(8,128)(2,1)S(1)}, u32[]{:S(2)}, u32[]{:S(2)}) %collective-permute-start.4) | collective-permute-done | bytes 278560 | tf_op jit(solution)/shard_map/ppermute | solution.py:213
  98.8 0.0 collective-permute-done.5
  98.8 0.0 collective-permute-done.6
  98.8 1.9 %collective-permute-start.7 = (bf16[256,2176]{1,0:T(8,128)(2,1)S(1)}, bf16[256,2176]{1,0:T(8,128)(2,1)}, u32[]{:S(2)}, u32[]{:S(2)}) collective-permute-start(bf16[256,2176]{1,0:T(8,128)(2,1)S(1)} %constant_dynamic-update-slice_fusion.own_ref), channel_id=1, source_target_pairs={{0,1},{1,0},{2,3},{3,2},{4,5},{5,4},{6,7},{7,6},{8,9},{9,8},{10,11... | collective-permute-start | bytes 3342344 | tf_op jit(solution)/shard_map/ppermute | solution.py:215
  100.8 0.6 fusion.21
  104.0 0.1 fusion.9.pick_ref
  104.2 0.0 collective-permute-done.7.other_ref
  104.2 7.4 %all-to-all-done = bf16[128,16,384]{2,1,0:T(8,128)(2,1)S(1)} async-done(((bf16[128,16,384]{2,1,0:T(8,128)(2,1)}), bf16[128,16,384]{2,1,0:T(8,128)(2,1)S(1)}, u32[]{:S(2)}, u32[]{:S(2)}) %all-to-all-start) | async-done | bytes 1572896 | tf_op jit(solution)/shard_map/all_to_all | solution.py:221
  111.6 3.5 %shard_map.105 = (bf16[2304,128]{1,0:T(8,128)(2,1)S(1)}, bf16[2304,128]{1,0:T(8,128)(2,1)S(1)}, bf16[2048,384]{1,0:T(8,128)(2,1)}) custom-call(s32[1]{0:T(128)S(6)} %select_n.58.expert_ref, bf16[256,256]{1,0:T(8,128)(2,1)S(1)} %fusion.9.pick_ref, bf16[256,2176]{1,0:T(8,128)(2,1)S(1)} %constant_dynamic-update-slice_fusion.own_ref, ...), custom_call_target="tpu_custom_call" | custom-call | tf_op jit(solution)/shard_map/pallas_call | solution.py:103
  115.2 1.9 %collective-permute-start.8 = (bf16[2304,128]{1,0:T(8,128)(2,1)S(1)}, bf16[2304,128]{1,0:T(8,128)(2,1)S(1)}, u32[]{:S(2)}, u32[]{:S(2)}) collective-permute-start(bf16[2304,128]{1,0:T(8,128)(2,1)S(1)} %get-tuple-element.20), channel_id=1, source_target_pairs={{0,1},{1,0},{2,3},{3,2},{4,5},{5,4},{6,7},{7,6},{8,9},{9,8},{10,11... | collective-permute-start | bytes 1769480 | tf_op jit(solution)/shard_map/ppermute | solution.py:233
  117.1 2.0 %collective-permute-done.8.recv_ref = bf16[2304,128]{1,0:T(8,128)(2,1)S(1)} collective-permute-done((bf16[2304,128]{1,0:T(8,128)(2,1)S(1)}, bf16[2304,128]{1,0:T(8,128)(2,1)S(1)}, u32[]{:S(2)}, u32[]{:S(2)}) %collective-permute-start.8) | collective-permute-done | bytes 589856 | tf_op jit(solution)/shard_map/ppermute | solution.py:233
  119.1 0.7 shard_map.106
  119.8 40.6 %all_to_all.10.ref = bf16[64,64,128]{2,1,0:T(8,128)(2,1)S(1)} all-to-all(bf16[64,64,128]{2,1,0:T(8,128)(2,1)S(1)} %bitcast.12), channel_id=1, replica_groups=mesh['g'=4,'y'=8,'zh'=2,'x'=4,'c'=2] {'y','zh','x'}, dimensions={0} | all-to-all | bytes 2097152 | tf_op jit(solution)/shard_map/all_to_all | solution.py:235
  160.4 0.8 shard_map.107
  (6 shorter events, 0.1 us)
Async XLA Ops:
  2.1 24.4 %copy-start.1 = (bf16[1,4,2176]{2,1,0:T(4,128)(2,1)S(1)}, bf16[1,4,2176]{2,1,0:T(4,128)(2,1)}, u32[]{:S(2)}) copy-start(bf16[1,4,2176]{2,1,0:T(4,128)(2,1)} %shard_map.103) | copy-start | bytes 52228
  2.1 52.9 %copy-start = (s32[4,128]{1,0:T(4,128)S(1)}, s32[4,128]{1,0:T(4,128)}, u32[]{:S(2)}) copy-start(s32[4,128]{1,0:T(4,128)} %placement_ref.1) | copy-start | bytes 6148
  2.1 24.4 %collective-permute-start.3 = (bf16[4,2176]{1,0:T(4,128)(2,1)}, bf16[4,2176]{1,0:T(4,128)(2,1)S(1)}, u32[]{:S(2)}, u32[]{:S(2)}) collective-permute-start(bf16[4,2176]{1,0:T(4,128)(2,1)} %bitcast.13), channel_id=1, source_target_pairs={{0,8},{8,0},{1,9},{9,1},{2,10},{10,2},{3,11},{11,3},{4,12},{12,4},... | collective-permute-start | bytes 52232 | tf_op jit(solution)/shard_map/ppermute | solution.py:190
  16.3 36.6 %collective-permute-start.2 = (bf16[32,16,384]{2,1,0:T(8,128)(2,1)S(1)}, bf16[32,16,384]{2,1,0:T(8,128)(2,1)S(1)}, u32[]{:S(2)}, u32[]{:S(2)}) collective-permute-start(bf16[32,16,384]{2,1,0:T(8,128)(2,1)S(1)} %get-tuple-element.14.a), channel_id=1, source_target_pairs={{0,384},{128,0},{256,128},{384,256},{1,385},{129,1},{257,129},{385... | collective-permute-start | bytes 1179656 | tf_op jit(solution)/shard_map/ppermute | solution.py:205
  21.5 33.4 %collective-permute-start.1 = (bf16[32,16,384]{2,1,0:T(8,128)(2,1)S(1)}, bf16[32,16,384]{2,1,0:T(8,128)(2,1)S(1)}, u32[]{:S(2)}, u32[]{:S(2)}) collective-permute-start(bf16[32,16,384]{2,1,0:T(8,128)(2,1)S(1)} %get-tuple-element.14.a), channel_id=1, source_target_pairs={{0,256},{128,384},{256,0},{384,128},{1,257},{129,385},{257,1},{385... | collective-permute-start | bytes 1179656 | tf_op jit(solution)/shard_map/ppermute | solution.py:205
  23.5 31.5 %collective-permute-start = (bf16[32,16,384]{2,1,0:T(8,128)(2,1)S(1)}, bf16[32,16,384]{2,1,0:T(8,128)(2,1)S(1)}, u32[]{:S(2)}, u32[]{:S(2)}) collective-permute-start(bf16[32,16,384]{2,1,0:T(8,128)(2,1)S(1)} %get-tuple-element.14.a), channel_id=1, source_target_pairs={{0,128},{128,256},{256,384},{384,0},{1,129},{129,257},{257,385},{3... | collective-permute-start | bytes 1179656 | tf_op jit(solution)/shard_map/ppermute | solution.py:205
  57.2 54.4 %all-to-all-start = ((bf16[128,16,384]{2,1,0:T(8,128)(2,1)}), bf16[128,16,384]{2,1,0:T(8,128)(2,1)S(1)}, u32[]{:S(2)}, u32[]{:S(2)}) async-start(bf16[128,16,384]{2,1,0:T(8,128)(2,1)} %shard_map.104), calls=%async_computation | async-start | bytes 3145728 | tf_op jit(solution)/shard_map/all_to_all | solution.py:221
  68.6 30.2 %collective-permute-start.6 = (bf16[64,2176]{1,0:T(8,128)(2,1)S(1)}, bf16[64,2176]{1,0:T(8,128)(2,1)S(1)}, u32[]{:S(2)}, u32[]{:S(2)}) collective-permute-start(bf16[64,2176]{1,0:T(8,128)(2,1)S(1)} %all_gather.3), channel_id=1, source_target_pairs={{0,6},{2,0},{4,2},{6,4},{1,7},{3,1},{5,3},{7,5},{8,14},{10,8},{12,... | collective-permute-start | bytes 835592 | tf_op jit(solution)/shard_map/ppermute | solution.py:213
  71.3 27.4 %collective-permute-start.5 = (bf16[64,2176]{1,0:T(8,128)(2,1)S(1)}, bf16[64,2176]{1,0:T(8,128)(2,1)S(1)}, u32[]{:S(2)}, u32[]{:S(2)}) collective-permute-start(bf16[64,2176]{1,0:T(8,128)(2,1)S(1)} %all_gather.3), channel_id=1, source_target_pairs={{0,4},{2,6},{4,0},{6,2},{1,5},{3,7},{5,1},{7,3},{8,12},{10,14},{12... | collective-permute-start | bytes 835592 | tf_op jit(solution)/shard_map/ppermute | solution.py:213
  74.7 24.0 %collective-permute-start.4 = (bf16[64,2176]{1,0:T(8,128)(2,1)S(1)}, bf16[64,2176]{1,0:T(8,128)(2,1)S(1)}, u32[]{:S(2)}, u32[]{:S(2)}) collective-permute-start(bf16[64,2176]{1,0:T(8,128)(2,1)S(1)} %all_gather.3), channel_id=1, source_target_pairs={{0,2},{2,4},{4,6},{6,0},{1,3},{3,5},{5,7},{7,1},{8,10},{10,12},{12... | collective-permute-start | bytes 835592 | tf_op jit(solution)/shard_map/ppermute | solution.py:213
  98.8 5.3 %collective-permute-start.7 = (bf16[256,2176]{1,0:T(8,128)(2,1)S(1)}, bf16[256,2176]{1,0:T(8,128)(2,1)}, u32[]{:S(2)}, u32[]{:S(2)}) collective-permute-start(bf16[256,2176]{1,0:T(8,128)(2,1)S(1)} %constant_dynamic-update-slice_fusion.own_ref), channel_id=1, source_target_pairs={{0,1},{1,0},{2,3},{3,2},{4,5},{5,4},{6,7},{7,6},{8,9},{9,8},{10,11... | collective-permute-start | bytes 3342344 | tf_op jit(solution)/shard_map/ppermute | solution.py:215
  115.2 3.9 %collective-permute-start.8 = (bf16[2304,128]{1,0:T(8,128)(2,1)S(1)}, bf16[2304,128]{1,0:T(8,128)(2,1)S(1)}, u32[]{:S(2)}, u32[]{:S(2)}) collective-permute-start(bf16[2304,128]{1,0:T(8,128)(2,1)S(1)} %get-tuple-element.20), channel_id=1, source_target_pairs={{0,1},{1,0},{2,3},{3,2},{4,5},{5,4},{6,7},{7,6},{8,9},{9,8},{10,11... | collective-permute-start | bytes 1769480 | tf_op jit(solution)/shard_map/ppermute | solution.py:233

commit v7 on v6

--- a/solution.py
+++ b/solution.py
@@ -52,7 +52,7 @@
     def kernel(group_ref, placement_ref, a, b, c, d, out_ref):
         own = group_ref[0]
         for k, ref in enumerate((a, b, c, d)):
-            base = ((own + len(parts) - k) % len(parts)) * count
+            base = ((own + k) % len(parts)) * count
 
             def body(i, _, ref=ref, base=base):
                 out_ref[placement_ref[own, base + i]] = ref[i]
@@ -69,46 +69,52 @@
     )(group, placement, *parts)
 
 
-def hidden_units(expert_id, pick, own_rows, other_rows, weights):
-    half = own_rows.shape[0]
+def hidden_units(expert_id, pick, rows, weights, with_slab):
+    half = rows.shape[0]
     depth = weights.shape[0]
     blocks = 4
     piece = depth // blocks
 
-    def kernel(expert_ref, pick_ref, own_ref, other_ref, w_ref, send_ref, keep_ref, slab_hbm, sems):
-        slab_copies = [
-            pltpu.make_async_copy(
-                w_ref.at[pl.ds(k * piece, piece)], slab_hbm.at[pl.ds(k * piece, piece)], sems.at[k]
-            )
-            for k in range(blocks)
-        ]
-        for copy in slab_copies:
+    def kernel(expert_ref, pick_ref, rows_ref, w_ref, out_ref, *slab):
+        copies = []
+        if with_slab:
+            slab_hbm, sems = slab
+            copies = [
+                pltpu.make_async_copy(
+                    w_ref.at[pl.ds(k * piece, piece)], slab_hbm.at[pl.ds(k * piece, piece)], sems.at[k]
+                )
+                for k in range(blocks)
+            ]
+        for copy in copies:
             copy.start()
+        out_ref[half:, :] = w_ref[:, 256:]
         expert = expert_ref[0]
         lane = lax.broadcasted_iota(jnp.int32, (1, EXTRA), 1)
         own = jnp.where((lane == expert) | (lane == expert + EXPERT_COUNT), 1.0, 0.0)
-        for rows_ref, out_ref in ((other_ref, send_ref), (own_ref, keep_ref)):
-            gate_up = jnp.dot(rows_ref[:, :depth], w_ref[:, :256], preferred_element_type=jnp.float32)
-            gate, up = gate_up[:, :128], gate_up[:, 128:]
-            hidden = (gate / (1.0 + jnp.exp(-gate)) * up).astype(jnp.bfloat16).astype(jnp.float32)
-            extra = rows_ref[:, depth:].astype(jnp.float32)
-            coefficient = jnp.sum(extra * own, axis=1, keepdims=True)
-            scaled = (hidden * coefficient).astype(jnp.bfloat16)
-            ordered = jnp.dot(pick_ref[...], scaled, preferred_element_type=jnp.float32)
-            out_ref[:half, :] = ordered.astype(jnp.bfloat16)
-            out_ref[half:, :] = w_ref[:, 256:]
-        for copy in slab_copies:
+        gate_up = jnp.dot(rows_ref[:, :depth], w_ref[:, :256], preferred_element_type=jnp.float32)
+        gate, up = gate_up[:, :128], gate_up[:, 128:]
+        hidden = (gate / (1.0 + jnp.exp(-gate)) * up).astype(jnp.bfloat16).astype(jnp.float32)
+        extra = rows_ref[:, depth:].astype(jnp.float32)
+        coefficient = jnp.sum(extra * own, axis=1, keepdims=True)
+        scaled = (hidden * coefficient).astype(jnp.bfloat16)
+        ordered = jnp.dot(pick_ref[...], scaled, preferred_element_type=jnp.float32)
+        out_ref[:half, :] = ordered.astype(jnp.bfloat16)
+        for copy in copies:
             copy.wait()
 
-    return pl.pallas_call(
-        kernel,
-        out_shape=(jax.ShapeDtypeStruct((half + depth, 128), jnp.bfloat16),) * 2
-        + (jax.ShapeDtypeStruct(weights.shape, jnp.bfloat16),),
-        in_specs=[pl.BlockSpec(memory_space=pltpu.SMEM)] + [pl.BlockSpec(memory_space=pltpu.VMEM)] * 4,
-        out_specs=(pl.BlockSpec(memory_space=pltpu.VMEM),) * 2 + (pl.BlockSpec(memory_space=pltpu.HBM),),
-        scratch_shapes=[pltpu.SemaphoreType.DMA((blocks,))],
+    out_shape = (jax.ShapeDtypeStruct((half + depth, 128), jnp.bfloat16),)
+    out_specs = (pl.BlockSpec(memory_space=pltpu.VMEM),)
+    if with_slab:
+        out_shape += (jax.ShapeDtypeStruct(weights.shape, jnp.bfloat16),)
+        out_specs += (pl.BlockSpec(memory_space=pltpu.HBM),)
+    return pl.pallas_call(
+        kernel,
+        out_shape=out_shape,
+        in_specs=[pl.BlockSpec(memory_space=pltpu.SMEM)] + [pl.BlockSpec(memory_space=pltpu.VMEM)] * 3,
+        out_specs=out_specs,
+        scratch_shapes=[pltpu.SemaphoreType.DMA((blocks,))] if with_slab else [],
         compiler_params=pltpu.CompilerParams(vmem_limit_bytes=24 * 2**20),
-    )(expert_id, pick, own_rows, other_rows, weights)
+    )(expert_id, pick, rows, weights)
 
 
 def pair_outputs(kept, received):
@@ -202,7 +208,7 @@
     other_rows, _ = lax.optimization_barrier((other_rows, rounded))
 
     parts = [rounded] + [
-        lax.ppermute(rounded, "g", [(i, (i + s) % GROUPS) for i in range(GROUPS)])
+        lax.ppermute(rounded, "g", [((i + s) % GROUPS, i) for i in range(GROUPS)])
         for s in range(1, GROUPS)
     ]
 
@@ -229,7 +235,8 @@
 
     slabs_each = unit_count // EXPERT_COUNT
     expert_id = jnp.sum(jnp.where(own_row == place, unit_ids, 0), keepdims=True) // slabs_each
-    sent, kept, slab = hidden_units(expert_id, pick, own_rows, other_rows, weights)
+    kept, slab = hidden_units(expert_id, pick, own_rows, weights, True)
+    (sent,) = hidden_units(expert_id, pick, other_rows, weights, False)
     received = lax.ppermute(sent, "c", [(0, 1), (1, 0)])
     chunks = pair_outputs(kept, received)
     chunks = lax.all_to_all(chunks, ("y", "zh", "x"), split_axis=0, concat_axis=0, tiled=True)

time: 162 us -> 161 us (level)
  the two profiles are of different devices: /device:TPU:6 before, /device:TPU:64 now
where the time goes in v7:
time: 161 us; the launch traced here: 160 us
  blocking collectives  67.5 us (42%)
  starting transfers between devices  45.7 us (28%)
  waiting for transfers between devices  31 us (19%)
  Pallas kernels  8.35 us (5%)
  other arithmetic  4 us (2%)
  between operations  3.44 us (2%)
    all_to_all x1, blocking collectives, per_device(): lax.all_to_all(chunks, ('y', 'zh', 'x'), split_axis=0, concat_axis=0, til...  41.1 us
    all_gather x1, blocking collectives, per_device(): column = lax.all_gather(pair, 'y', axis=0, tiled=True)  26.4 us
    ppermute x3, waiting for transfers between devices, per_device(): lax.ppermute(column, 'x', [(k, (k + t) % XS) for k in range(XS)])  22.1 us
    all_to_all x1, starting transfers between devices, per_device(): lax.all_to_all(ordered, ALONG, split_axis=0, concat_axis=0, tiled=True)  11.8 us
    ppermute x1, starting transfers between devices, per_device(): other_rows = lax.ppermute(own_rows, 'zh', [(0, 1), (1, 0)])  10.1 us
    ppermute x3, starting transfers between devices, per_device(): lax.ppermute(rounded, 'g', [((i + s) % GROUPS, i) for i in range(GROUPS)])  10.1 us
    ppermute x3, starting transfers between devices, per_device(): lax.ppermute(column, 'x', [(k, (k + t) % XS) for k in range(XS)])  9.78 us
    all_to_all x1, waiting for transfers between devices, per_device(): lax.all_to_all(ordered, ALONG, split_axis=0, concat_axis=0, tiled=True)  6.1 us
  transfers between devices with their start and end apart: 10, of which 5 were waited for; matrix products, arithmetic and copies ran while one was open for 3% of the time, Pallas kernels for 1%

profile of v7, /device:TPU:64, one launch (start us, length us, event | category | flops | bytes accessed | tf_op | source)
XLA Modules:
  0.0 160.1 jit_solution(7450538366364103594)
XLA Ops:
  0.6 1.4 shard_map.103
  2.1 0.0 copy-start.1
  2.1 0.0 copy-start
  2.1 10.1 %collective-permute-start.3 = (bf16[4,2176]{1,0:T(4,128)(2,1)}, bf16[4,2176]{1,0:T(4,128)(2,1)S(1)}, u32[]{:S(2)}, u32[]{:S(2)}) collective-permute-start(bf16[4,2176]{1,0:T(4,128)(2,1)} %bitcast.14), channel_id=1, source_target_pairs={{0,8},{8,0},{1,9},{9,1},{2,10},{10,2},{3,11},{11,3},{4,12},{12,4},... | collective-permute-start | bytes 52232 | tf_op jit(solution)/shard_map/ppermute | solution.py:196
  12.2 3.2 %fusion.22 = (bf16[32,16,384]{2,1,0:T(8,128)(2,1)S(1)}, f32[32,16,384]{2,1,0:T(8,128)}) fusion(f32[32,16,384]{2,1,0:T(8,128)} %param.8, f32[32,16,384]{2,1,0:T(8,128)} %param.10, bf16[32,16,384]{2,1,0:T(8,128)(2,1)} %param.11, f32[32,16,384]{2,1,0:T(8,128)} %param.9), kind=kLoop, calls=%fused_computation.45 | loop fusion | flops 3145728 | bytes 3932160 | tf_op jit(solution)/shard_map/convert_element_type | solution.py:207
  15.4 3.4 %collective-permute-start.2 = (bf16[32,16,384]{2,1,0:T(8,128)(2,1)S(1)}, bf16[32,16,384]{2,1,0:T(8,128)(2,1)S(1)}, u32[]{:S(2)}, u32[]{:S(2)}) collective-permute-start(bf16[32,16,384]{2,1,0:T(8,128)(2,1)S(1)} %get-tuple-element.13.a), channel_id=1, source_target_pairs={{384,0},{0,128},{128,256},{256,384},{385,1},{1,129},{129,257},{257... | collective-permute-start | bytes 1179656 | tf_op jit(solution)/shard_map/ppermute | solution.py:211
  18.8 3.3 %collective-permute-start.1 = (bf16[32,16,384]{2,1,0:T(8,128)(2,1)S(1)}, bf16[32,16,384]{2,1,0:T(8,128)(2,1)S(1)}, u32[]{:S(2)}, u32[]{:S(2)}) collective-permute-start(bf16[32,16,384]{2,1,0:T(8,128)(2,1)S(1)} %get-tuple-element.13.a), channel_id=1, source_target_pairs={{256,0},{384,128},{0,256},{128,384},{257,1},{385,129},{1,257},{129... | collective-permute-start | bytes 1179656 | tf_op jit(solution)/shard_map/ppermute | solution.py:211
  22.2 3.4 %collective-permute-start = (bf16[32,16,384]{2,1,0:T(8,128)(2,1)S(1)}, bf16[32,16,384]{2,1,0:T(8,128)(2,1)S(1)}, u32[]{:S(2)}, u32[]{:S(2)}) collective-permute-start(bf16[32,16,384]{2,1,0:T(8,128)(2,1)S(1)} %get-tuple-element.13.a), channel_id=1, source_target_pairs={{128,0},{256,128},{384,256},{0,384},{129,1},{257,129},{385,257},{1... | collective-permute-start | bytes 1179656 | tf_op jit(solution)/shard_map/ppermute | solution.py:211
  25.6 0.0 collective-permute-done.3
  25.6 0.0 copy-done.1
  25.6 26.4 %all_gather.3 = bf16[64,2176]{1,0:T(8,128)(2,1)S(1)} all-gather(bf16[8,2176]{1,0:T(8,128)(2,1)S(1)} %pad_maximum_fusion), channel_id=1, replica_groups=mesh['g'=4,'y'=8,'zh'=2,'x'=4,'c'=2] {'y'}, dimensions={0}, use_global_device_ids=true | all-gather | bytes 313344 | tf_op jit(solution)/shard_map/all_gather | solution.py:216
  52.1 0.0 collective-permute-done.2.d
  52.1 0.1 collective-permute-done.1.c
  52.2 1.9 %collective-permute-done.b = bf16[32,16,384]{2,1,0:T(8,128)(2,1)S(1)} collective-permute-done((bf16[32,16,384]{2,1,0:T(8,128)(2,1)S(1)}, bf16[32,16,384]{2,1,0:T(8,128)(2,1)S(1)}, u32[]{:S(2)}, u32[]{:S(2)}) %collective-permute-start) | collective-permute-done | bytes 393248 | tf_op jit(solution)/shard_map/ppermute | solution.py:211
  54.1 0.0 copy-done
  54.1 2.2 %shard_map.104 = bf16[128,16,384]{2,1,0:T(8,128)(2,1)} custom-call(s32[1]{0:T(128)} %bitcast.3.group_ref, s32[4,128]{1,0:T(4,128)S(1)} %copy-done, bf16[32,16,384]{2,1,0:T(8,128)(2,1)S(1)} %get-tuple-element.13.a, bf16[32,16,384]{2,1,0:T(8,128)(2,1)S(1)} %collective-permute-done.b, bf16[32,16,384]{2,1,0:T(8,128)(2,1)S(1)} %collective-permute-done.1.c, ...), custom_call_target="tpu_custom_call" | custom-call | tf_op jit(solution)/shard_map/pallas_call | solution.py:63
  56.3 11.8 %all-to-all-start = ((bf16[128,16,384]{2,1,0:T(8,128)(2,1)}), bf16[128,16,384]{2,1,0:T(8,128)(2,1)S(1)}, u32[]{:S(2)}, u32[]{:S(2)}) async-start(bf16[128,16,384]{2,1,0:T(8,128)(2,1)} %shard_map.104), calls=%async_computation | async-start | bytes 3145728 | tf_op jit(solution)/shard_map/all_to_all | solution.py:227
  68.1 4.3 %collective-permute-start.6 = (bf16[64,2176]{1,0:T(8,128)(2,1)S(1)}, bf16[64,2176]{1,0:T(8,128)(2,1)S(1)}, u32[]{:S(2)}, u32[]{:S(2)}) collective-permute-start(bf16[64,2176]{1,0:T(8,128)(2,1)S(1)} %all_gather.3), channel_id=1, source_target_pairs={{0,6},{2,0},{4,2},{6,4},{1,7},{3,1},{5,3},{7,5},{8,14},{10,8},{12,... | collective-permute-start | bytes 835592 | tf_op jit(solution)/shard_map/ppermute | solution.py:219
  72.3 2.8 %collective-permute-start.5 = (bf16[64,2176]{1,0:T(8,128)(2,1)S(1)}, bf16[64,2176]{1,0:T(8,128)(2,1)S(1)}, u32[]{:S(2)}, u32[]{:S(2)}) collective-permute-start(bf16[64,2176]{1,0:T(8,128)(2,1)S(1)} %all_gather.3), channel_id=1, source_target_pairs={{0,4},{2,6},{4,0},{6,2},{1,5},{3,7},{5,1},{7,3},{8,12},{10,14},{12... | collective-permute-start | bytes 835592 | tf_op jit(solution)/shard_map/ppermute | solution.py:219
  75.1 2.8 %collective-permute-start.4 = (bf16[64,2176]{1,0:T(8,128)(2,1)S(1)}, bf16[64,2176]{1,0:T(8,128)(2,1)S(1)}, u32[]{:S(2)}, u32[]{:S(2)}) collective-permute-start(bf16[64,2176]{1,0:T(8,128)(2,1)S(1)} %all_gather.3), channel_id=1, source_target_pairs={{0,2},{2,4},{4,6},{6,0},{1,3},{3,5},{5,7},{7,1},{8,10},{10,12},{12... | collective-permute-start | bytes 835592 | tf_op jit(solution)/shard_map/ppermute | solution.py:219
  77.9 22.1 %collective-permute-done.4 = bf16[64,2176]{1,0:T(8,128)(2,1)S(1)} collective-permute-done((bf16[64,2176]{1,0:T(8,128)(2,1)S(1)}, bf16[64,2176]{1,0:T(8,128)(2,1)S(1)}, u32[]{:S(2)}, u32[]{:S(2)}) %collective-permute-start.4) | collective-permute-done | bytes 278560 | tf_op jit(solution)/shard_map/ppermute | solution.py:219
  100.1 0.0 collective-permute-done.5
  100.1 0.0 collective-permute-done.6
  100.2 1.9 %collective-permute-start.7 = (bf16[256,2176]{1,0:T(8,128)(2,1)S(1)}, bf16[256,2176]{1,0:T(8,128)(2,1)}, u32[]{:S(2)}, u32[]{:S(2)}) collective-permute-start(bf16[256,2176]{1,0:T(8,128)(2,1)S(1)} %constant_dynamic-update-slice_fusion.rows_ref), channel_id=1, source_target_pairs={{0,1},{1,0},{2,3},{3,2},{4,5},{5,4},{6,7},{7,6},{8,9},{9,8},{10,11... | collective-permute-start | bytes 3342344 | tf_op jit(solution)/shard_map/ppermute | solution.py:221
  102.1 0.6 fusion.21
  105.4 0.1 fusion.9.pick_ref
  105.5 0.0 collective-permute-done.7.rows_ref
  105.5 6.1 %all-to-all-done = bf16[128,16,384]{2,1,0:T(8,128)(2,1)S(1)} async-done(((bf16[128,16,384]{2,1,0:T(8,128)(2,1)}), bf16[128,16,384]{2,1,0:T(8,128)(2,1)S(1)}, u32[]{:S(2)}, u32[]{:S(2)}) %all-to-all-start) | async-done | bytes 1572896 | tf_op jit(solution)/shard_map/all_to_all | solution.py:227
  111.6 2.0 %shard_map.106 = bf16[2304,128]{1,0:T(8,128)(2,1)S(1)} custom-call(s32[1]{0:T(128)S(6)} %select_n.58.expert_ref, bf16[256,256]{1,0:T(8,128)(2,1)S(1)} %fusion.9.pick_ref, bf16[256,2176]{1,0:T(8,128)(2,1)} %collective-permute-done.7.rows_ref, bf16[2048,384]{1,0:T(8,128)(2,1)S(1)} %bitcast.11), custom_call_target="tpu_custom_call" | custom-call | tf_op jit(solution)/shard_map/pallas_call | solution.py:110
  113.6 1.9 %collective-permute-start.8 = (bf16[2304,128]{1,0:T(8,128)(2,1)S(1)}, bf16[2304,128]{1,0:T(8,128)(2,1)S(1)}, u32[]{:S(2)}, u32[]{:S(2)}) collective-permute-start(bf16[2304,128]{1,0:T(8,128)(2,1)S(1)} %shard_map.106), channel_id=1, source_target_pairs={{0,1},{1,0},{2,3},{3,2},{4,5},{5,4},{6,7},{7,6},{8,9},{9,8},{10,11... | collective-permute-start | bytes 1769480 | tf_op jit(solution)/shard_map/ppermute | solution.py:240
  115.5 1.2 shard_map.105
  116.8 0.7 collective-permute-done.8.recv_ref
  117.5 0.7 shard_map.107
  118.2 41.1 %all_to_all.10.ref = bf16[64,64,128]{2,1,0:T(8,128)(2,1)S(1)} all-to-all(bf16[64,64,128]{2,1,0:T(8,128)(2,1)S(1)} %bitcast.13), channel_id=1, replica_groups=mesh['g'=4,'y'=8,'zh'=2,'x'=4,'c'=2] {'y','zh','x'}, dimensions={0} | all-to-all | bytes 2097152 | tf_op jit(solution)/shard_map/all_to_all | solution.py:242
  159.3 0.8 shard_map.108
  (6 shorter events, 0.1 us)
Async XLA Ops:
  2.1 23.5 %copy-start.1 = (bf16[1,4,2176]{2,1,0:T(4,128)(2,1)S(1)}, bf16[1,4,2176]{2,1,0:T(4,128)(2,1)}, u32[]{:S(2)}) copy-start(bf16[1,4,2176]{2,1,0:T(4,128)(2,1)} %shard_map.103) | copy-start | bytes 52228
  2.1 52.0 %copy-start = (s32[4,128]{1,0:T(4,128)S(1)}, s32[4,128]{1,0:T(4,128)}, u32[]{:S(2)}) copy-start(s32[4,128]{1,0:T(4,128)} %placement_ref.1) | copy-start | bytes 6148
  2.1 23.5 %collective-permute-start.3 = (bf16[4,2176]{1,0:T(4,128)(2,1)}, bf16[4,2176]{1,0:T(4,128)(2,1)S(1)}, u32[]{:S(2)}, u32[]{:S(2)}) collective-permute-start(bf16[4,2176]{1,0:T(4,128)(2,1)} %bitcast.14), channel_id=1, source_target_pairs={{0,8},{8,0},{1,9},{9,1},{2,10},{10,2},{3,11},{11,3},{4,12},{12,4},... | collective-permute-start | bytes 52232 | tf_op jit(solution)/shard_map/ppermute | solution.py:196
  15.4 36.6 %collective-permute-start.2 = (bf16[32,16,384]{2,1,0:T(8,128)(2,1)S(1)}, bf16[32,16,384]{2,1,0:T(8,128)(2,1)S(1)}, u32[]{:S(2)}, u32[]{:S(2)}) collective-permute-start(bf16[32,16,384]{2,1,0:T(8,128)(2,1)S(1)} %get-tuple-element.13.a), channel_id=1, source_target_pairs={{384,0},{0,128},{128,256},{256,384},{385,1},{1,129},{129,257},{257... | collective-permute-start | bytes 1179656 | tf_op jit(solution)/shard_map/ppermute | solution.py:211
  18.8 33.4 %collective-permute-start.1 = (bf16[32,16,384]{2,1,0:T(8,128)(2,1)S(1)}, bf16[32,16,384]{2,1,0:T(8,128)(2,1)S(1)}, u32[]{:S(2)}, u32[]{:S(2)}) collective-permute-start(bf16[32,16,384]{2,1,0:T(8,128)(2,1)S(1)} %get-tuple-element.13.a), channel_id=1, source_target_pairs={{256,0},{384,128},{0,256},{128,384},{257,1},{385,129},{1,257},{129... | collective-permute-start | bytes 1179656 | tf_op jit(solution)/shard_map/ppermute | solution.py:211
  22.2 31.9 %collective-permute-start = (bf16[32,16,384]{2,1,0:T(8,128)(2,1)S(1)}, bf16[32,16,384]{2,1,0:T(8,128)(2,1)S(1)}, u32[]{:S(2)}, u32[]{:S(2)}) collective-permute-start(bf16[32,16,384]{2,1,0:T(8,128)(2,1)S(1)} %get-tuple-element.13.a), channel_id=1, source_target_pairs={{128,0},{256,128},{384,256},{0,384},{129,1},{257,129},{385,257},{1... | collective-permute-start | bytes 1179656 | tf_op jit(solution)/shard_map/ppermute | solution.py:211
  56.3 55.3 %all-to-all-start = ((bf16[128,16,384]{2,1,0:T(8,128)(2,1)}), bf16[128,16,384]{2,1,0:T(8,128)(2,1)S(1)}, u32[]{:S(2)}, u32[]{:S(2)}) async-start(bf16[128,16,384]{2,1,0:T(8,128)(2,1)} %shard_map.104), calls=%async_computation | async-start | bytes 3145728 | tf_op jit(solution)/shard_map/all_to_all | solution.py:227
  68.1 32.0 %collective-permute-start.6 = (bf16[64,2176]{1,0:T(8,128)(2,1)S(1)}, bf16[64,2176]{1,0:T(8,128)(2,1)S(1)}, u32[]{:S(2)}, u32[]{:S(2)}) collective-permute-start(bf16[64,2176]{1,0:T(8,128)(2,1)S(1)} %all_gather.3), channel_id=1, source_target_pairs={{0,6},{2,0},{4,2},{6,4},{1,7},{3,1},{5,3},{7,5},{8,14},{10,8},{12,... | collective-permute-start | bytes 835592 | tf_op jit(solution)/shard_map/ppermute | solution.py:219
  72.3 27.7 %collective-permute-start.5 = (bf16[64,2176]{1,0:T(8,128)(2,1)S(1)}, bf16[64,2176]{1,0:T(8,128)(2,1)S(1)}, u32[]{:S(2)}, u32[]{:S(2)}) collective-permute-start(bf16[64,2176]{1,0:T(8,128)(2,1)S(1)} %all_gather.3), channel_id=1, source_target_pairs={{0,4},{2,6},{4,0},{6,2},{1,5},{3,7},{5,1},{7,3},{8,12},{10,14},{12... | collective-permute-start | bytes 835592 | tf_op jit(solution)/shard_map/ppermute | solution.py:219
  75.1 24.9 %collective-permute-start.4 = (bf16[64,2176]{1,0:T(8,128)(2,1)S(1)}, bf16[64,2176]{1,0:T(8,128)(2,1)S(1)}, u32[]{:S(2)}, u32[]{:S(2)}) collective-permute-start(bf16[64,2176]{1,0:T(8,128)(2,1)S(1)} %all_gather.3), channel_id=1, source_target_pairs={{0,2},{2,4},{4,6},{6,0},{1,3},{3,5},{5,7},{7,1},{8,10},{10,12},{12... | collective-permute-start | bytes 835592 | tf_op jit(solution)/shard_map/ppermute | solution.py:219
  100.2 5.3 %collective-permute-start.7 = (bf16[256,2176]{1,0:T(8,128)(2,1)S(1)}, bf16[256,2176]{1,0:T(8,128)(2,1)}, u32[]{:S(2)}, u32[]{:S(2)}) collective-permute-start(bf16[256,2176]{1,0:T(8,128)(2,1)S(1)} %constant_dynamic-update-slice_fusion.rows_ref), channel_id=1, source_target_pairs={{0,1},{1,0},{2,3},{3,2},{4,5},{5,4},{6,7},{7,6},{8,9},{9,8},{10,11... | collective-permute-start | bytes 3342344 | tf_op jit(solution)/shard_map/ppermute | solution.py:221
  113.6 3.9 %collective-permute-start.8 = (bf16[2304,128]{1,0:T(8,128)(2,1)S(1)}, bf16[2304,128]{1,0:T(8,128)(2,1)S(1)}, u32[]{:S(2)}, u32[]{:S(2)}) collective-permute-start(bf16[2304,128]{1,0:T(8,128)(2,1)S(1)} %shard_map.106), channel_id=1, source_target_pairs={{0,1},{1,0},{2,3},{3,2},{4,5},{5,4},{6,7},{7,6},{8,9},{9,8},{10,11... | collective-permute-start | bytes 1769480 | tf_op jit(solution)/shard_map/ppermute | solution.py:240

commit v8 on v7

--- a/solution.py
+++ b/solution.py
@@ -49,22 +49,24 @@
     count, rows, cols = parts[0].shape
     total = count * len(parts)
 
-    def kernel(group_ref, placement_ref, a, b, c, d, out_ref):
+    def kernel(group_ref, placement_ref, a, b, c, d, out_hbm, sem):
         own = group_ref[0]
         for k, ref in enumerate((a, b, c, d)):
             base = ((own + k) % len(parts)) * count
 
             def body(i, _, ref=ref, base=base):
-                out_ref[placement_ref[own, base + i]] = ref[i]
+                pltpu.make_async_copy(ref.at[i], out_hbm.at[placement_ref[own, base + i]], sem).start()
                 return 0
 
             lax.fori_loop(0, count, body, 0, unroll=8)
+        pltpu.make_async_copy(out_hbm, out_hbm, sem).wait()
 
     return pl.pallas_call(
         kernel,
         out_shape=jax.ShapeDtypeStruct((total, rows, cols), parts[0].dtype),
         in_specs=[pl.BlockSpec(memory_space=pltpu.SMEM)] * 2 + [pl.BlockSpec(memory_space=pltpu.VMEM)] * 4,
-        out_specs=pl.BlockSpec(memory_space=pltpu.VMEM),
+        out_specs=pl.BlockSpec(memory_space=pltpu.HBM),
+        scratch_shapes=[pltpu.SemaphoreType.DMA],
         compiler_params=pltpu.CompilerParams(vmem_limit_bytes=16 * 2**20),
     )(group, placement, *parts)
 

time: 161 us -> 160 us (level)
  no operation moved by 1% of the time
where the time goes in v8:
time: 160 us
  blocking collectives  67.5 us (42%)
  starting transfers between devices  45.7 us (29%)
  waiting for transfers between devices  31 us (19%)
  Pallas kernels  7.88 us (5%)
  other arithmetic  4 us (2%)
  between operations  3.45 us (2%)
    all_to_all x1, blocking collectives, per_device(): lax.all_to_all(chunks, ('y', 'zh', 'x'), split_axis=0, concat_axis=0, til...  41.1 us
    all_gather x1, blocking collectives, per_device(): column = lax.all_gather(pair, 'y', axis=0, tiled=True)  26.4 us
    ppermute x3, waiting for transfers between devices, per_device(): lax.ppermute(column, 'x', [(k, (k + t) % XS) for k in range(XS)])  22.1 us
    all_to_all x1, starting transfers between devices, per_device(): lax.all_to_all(ordered, ALONG, split_axis=0, concat_axis=0, tiled=True)  11.8 us
    ppermute x1, starting transfers between devices, per_device(): other_rows = lax.ppermute(own_rows, 'zh', [(0, 1), (1, 0)])  10.1 us
    ppermute x3, starting transfers between devices, per_device(): lax.ppermute(rounded, 'g', [((i + s) % GROUPS, i) for i in range(GROUPS)])  10.1 us
    ppermute x3, starting transfers between devices, per_device(): lax.ppermute(column, 'x', [(k, (k + t) % XS) for k in range(XS)])  9.78 us
    all_to_all x1, waiting for transfers between devices, per_device(): lax.all_to_all(ordered, ALONG, split_axis=0, concat_axis=0, tiled=True)  6.1 us
  transfers between devices with their start and end apart: 10, of which 5 were waited for; matrix products, arithmetic and copies ran while one was open for 3% of the time, Pallas kernels for 1%

profile of v8, /device:TPU:64, one launch (start us, length us, event | category | flops | bytes accessed | tf_op | source)
XLA Modules:
  0.0 159.6 jit_solution(7232252051297048353)
XLA Ops:
  0.6 1.4 shard_map.103
  2.1 0.0 copy-start.1
  2.1 0.0 copy-start
  2.1 10.1 %collective-permute-start.3 = (bf16[4,2176]{1,0:T(4,128)(2,1)}, bf16[4,2176]{1,0:T(4,128)(2,1)S(1)}, u32[]{:S(2)}, u32[]{:S(2)}) collective-permute-start(bf16[4,2176]{1,0:T(4,128)(2,1)} %bitcast.14), channel_id=1, source_target_pairs={{0,8},{8,0},{1,9},{9,1},{2,10},{10,2},{3,11},{11,3},{4,12},{12,4},... | collective-permute-start | bytes 52232 | tf_op jit(solution)/shard_map/ppermute | solution.py:198
  12.2 3.2 %fusion.22 = (bf16[32,16,384]{2,1,0:T(8,128)(2,1)S(1)}, f32[32,16,384]{2,1,0:T(8,128)}) fusion(f32[32,16,384]{2,1,0:T(8,128)} %param.8, f32[32,16,384]{2,1,0:T(8,128)} %param.10, bf16[32,16,384]{2,1,0:T(8,128)(2,1)} %param.11, f32[32,16,384]{2,1,0:T(8,128)} %param.9), kind=kLoop, calls=%fused_computation.45 | loop fusion | flops 3145728 | bytes 3932160 | tf_op jit(solution)/shard_map/convert_element_type | solution.py:209
  15.4 3.4 %collective-permute-start.2 = (bf16[32,16,384]{2,1,0:T(8,128)(2,1)S(1)}, bf16[32,16,384]{2,1,0:T(8,128)(2,1)S(1)}, u32[]{:S(2)}, u32[]{:S(2)}) collective-permute-start(bf16[32,16,384]{2,1,0:T(8,128)(2,1)S(1)} %get-tuple-element.13.a), channel_id=1, source_target_pairs={{384,0},{0,128},{128,256},{256,384},{385,1},{1,129},{129,257},{257... | collective-permute-start | bytes 1179656 | tf_op jit(solution)/shard_map/ppermute | solution.py:213
  18.8 3.3 %collective-permute-start.1 = (bf16[32,16,384]{2,1,0:T(8,128)(2,1)S(1)}, bf16[32,16,384]{2,1,0:T(8,128)(2,1)S(1)}, u32[]{:S(2)}, u32[]{:S(2)}) collective-permute-start(bf16[32,16,384]{2,1,0:T(8,128)(2,1)S(1)} %get-tuple-element.13.a), channel_id=1, source_target_pairs={{256,0},{384,128},{0,256},{128,384},{257,1},{385,129},{1,257},{129... | collective-permute-start | bytes 1179656 | tf_op jit(solution)/shard_map/ppermute | solution.py:213
  22.2 3.4 %collective-permute-start = (bf16[32,16,384]{2,1,0:T(8,128)(2,1)S(1)}, bf16[32,16,384]{2,1,0:T(8,128)(2,1)S(1)}, u32[]{:S(2)}, u32[]{:S(2)}) collective-permute-start(bf16[32,16,384]{2,1,0:T(8,128)(2,1)S(1)} %get-tuple-element.13.a), channel_id=1, source_target_pairs={{128,0},{256,128},{384,256},{0,384},{129,1},{257,129},{385,257},{1... | collective-permute-start | bytes 1179656 | tf_op jit(solution)/shard_map/ppermute | solution.py:213
  25.6 0.0 collective-permute-done.3
  25.6 0.0 copy-done.1
  25.6 26.4 %all_gather.3 = bf16[64,2176]{1,0:T(8,128)(2,1)S(1)} all-gather(bf16[8,2176]{1,0:T(8,128)(2,1)S(1)} %pad_maximum_fusion), channel_id=1, replica_groups=mesh['g'=4,'y'=8,'zh'=2,'x'=4,'c'=2] {'y'}, dimensions={0}, use_global_device_ids=true | all-gather | bytes 313344 | tf_op jit(solution)/shard_map/all_gather | solution.py:218
  52.1 0.0 collective-permute-done.2.d
  52.1 0.1 collective-permute-done.1.c
  52.2 1.9 %collective-permute-done.b = bf16[32,16,384]{2,1,0:T(8,128)(2,1)S(1)} collective-permute-done((bf16[32,16,384]{2,1,0:T(8,128)(2,1)S(1)}, bf16[32,16,384]{2,1,0:T(8,128)(2,1)S(1)}, u32[]{:S(2)}, u32[]{:S(2)}) %collective-permute-start) | collective-permute-done | bytes 393248 | tf_op jit(solution)/shard_map/ppermute | solution.py:213
  54.1 0.0 copy-done
  54.1 1.7 %shard_map.104 = bf16[128,16,384]{2,1,0:T(8,128)(2,1)} custom-call(s32[1]{0:T(128)} %bitcast.3.group_ref, s32[4,128]{1,0:T(4,128)S(1)} %copy-done, bf16[32,16,384]{2,1,0:T(8,128)(2,1)S(1)} %get-tuple-element.13.a, bf16[32,16,384]{2,1,0:T(8,128)(2,1)S(1)} %collective-permute-done.b, bf16[32,16,384]{2,1,0:T(8,128)(2,1)S(1)} %collective-permute-done.1.c, ...), custom_call_target="tpu_custom_call" | custom-call | tf_op jit(solution)/shard_map/pallas_call | solution.py:64
  55.8 11.8 %all-to-all-start = ((bf16[128,16,384]{2,1,0:T(8,128)(2,1)}), bf16[128,16,384]{2,1,0:T(8,128)(2,1)S(1)}, u32[]{:S(2)}, u32[]{:S(2)}) async-start(bf16[128,16,384]{2,1,0:T(8,128)(2,1)} %shard_map.104), calls=%async_computation | async-start | bytes 3145728 | tf_op jit(solution)/shard_map/all_to_all | solution.py:229
  67.6 4.3 %collective-permute-start.6 = (bf16[64,2176]{1,0:T(8,128)(2,1)S(1)}, bf16[64,2176]{1,0:T(8,128)(2,1)S(1)}, u32[]{:S(2)}, u32[]{:S(2)}) collective-permute-start(bf16[64,2176]{1,0:T(8,128)(2,1)S(1)} %all_gather.3), channel_id=1, source_target_pairs={{0,6},{2,0},{4,2},{6,4},{1,7},{3,1},{5,3},{7,5},{8,14},{10,8},{12,... | collective-permute-start | bytes 835592 | tf_op jit(solution)/shard_map/ppermute | solution.py:221
  71.9 2.8 %collective-permute-start.5 = (bf16[64,2176]{1,0:T(8,128)(2,1)S(1)}, bf16[64,2176]{1,0:T(8,128)(2,1)S(1)}, u32[]{:S(2)}, u32[]{:S(2)}) collective-permute-start(bf16[64,2176]{1,0:T(8,128)(2,1)S(1)} %all_gather.3), channel_id=1, source_target_pairs={{0,4},{2,6},{4,0},{6,2},{1,5},{3,7},{5,1},{7,3},{8,12},{10,14},{12... | collective-permute-start | bytes 835592 | tf_op jit(solution)/shard_map/ppermute | solution.py:221
  74.7 2.8 %collective-permute-start.4 = (bf16[64,2176]{1,0:T(8,128)(2,1)S(1)}, bf16[64,2176]{1,0:T(8,128)(2,1)S(1)}, u32[]{:S(2)}, u32[]{:S(2)}) collective-permute-start(bf16[64,2176]{1,0:T(8,128)(2,1)S(1)} %all_gather.3), channel_id=1, source_target_pairs={{0,2},{2,4},{4,6},{6,0},{1,3},{3,5},{5,7},{7,1},{8,10},{10,12},{12... | collective-permute-start | bytes 835592 | tf_op jit(solution)/shard_map/ppermute | solution.py:221
  77.5 22.1 %collective-permute-done.4 = bf16[64,2176]{1,0:T(8,128)(2,1)S(1)} collective-permute-done((bf16[64,2176]{1,0:T(8,128)(2,1)S(1)}, bf16[64,2176]{1,0:T(8,128)(2,1)S(1)}, u32[]{:S(2)}, u32[]{:S(2)}) %collective-permute-start.4) | collective-permute-done | bytes 278560 | tf_op jit(solution)/shard_map/ppermute | solution.py:221
  99.6 0.0 collective-permute-done.5
  99.7 0.0 collective-permute-done.6
  99.7 1.9 %collective-permute-start.7 = (bf16[256,2176]{1,0:T(8,128)(2,1)S(1)}, bf16[256,2176]{1,0:T(8,128)(2,1)}, u32[]{:S(2)}, u32[]{:S(2)}) collective-permute-start(bf16[256,2176]{1,0:T(8,128)(2,1)S(1)} %constant_dynamic-update-slice_fusion.rows_ref), channel_id=1, source_target_pairs={{0,1},{1,0},{2,3},{3,2},{4,5},{5,4},{6,7},{7,6},{8,9},{9,8},{10,11... | collective-permute-start | bytes 3342344 | tf_op jit(solution)/shard_map/ppermute | solution.py:223
  101.6 0.6 fusion.21
  104.9 0.1 fusion.9.pick_ref
  105.0 0.0 collective-permute-done.7.rows_ref
  105.0 6.1 %all-to-all-done = bf16[128,16,384]{2,1,0:T(8,128)(2,1)S(1)} async-done(((bf16[128,16,384]{2,1,0:T(8,128)(2,1)}), bf16[128,16,384]{2,1,0:T(8,128)(2,1)S(1)}, u32[]{:S(2)}, u32[]{:S(2)}) %all-to-all-start) | async-done | bytes 1572896 | tf_op jit(solution)/shard_map/all_to_all | solution.py:229
  111.1 2.0 %shard_map.106 = bf16[2304,128]{1,0:T(8,128)(2,1)S(1)} custom-call(s32[1]{0:T(128)S(6)} %select_n.58.expert_ref, bf16[256,256]{1,0:T(8,128)(2,1)S(1)} %fusion.9.pick_ref, bf16[256,2176]{1,0:T(8,128)(2,1)} %collective-permute-done.7.rows_ref, bf16[2048,384]{1,0:T(8,128)(2,1)S(1)} %bitcast.11), custom_call_target="tpu_custom_call" | custom-call | tf_op jit(solution)/shard_map/pallas_call | solution.py:112
  113.1 1.9 %collective-permute-start.8 = (bf16[2304,128]{1,0:T(8,128)(2,1)S(1)}, bf16[2304,128]{1,0:T(8,128)(2,1)S(1)}, u32[]{:S(2)}, u32[]{:S(2)}) collective-permute-start(bf16[2304,128]{1,0:T(8,128)(2,1)S(1)} %shard_map.106), channel_id=1, source_target_pairs={{0,1},{1,0},{2,3},{3,2},{4,5},{5,4},{6,7},{7,6},{8,9},{9,8},{10,11... | collective-permute-start | bytes 1769480 | tf_op jit(solution)/shard_map/ppermute | solution.py:242
  115.1 1.2 shard_map.105
  116.3 0.7 collective-permute-done.8.recv_ref
  117.0 0.7 shard_map.107
  117.8 41.1 %all_to_all.10.ref = bf16[64,64,128]{2,1,0:T(8,128)(2,1)S(1)} all-to-all(bf16[64,64,128]{2,1,0:T(8,128)(2,1)S(1)} %bitcast.13), channel_id=1, replica_groups=mesh['g'=4,'y'=8,'zh'=2,'x'=4,'c'=2] {'y','zh','x'}, dimensions={0} | all-to-all | bytes 2097152 | tf_op jit(solution)/shard_map/all_to_all | solution.py:244
  158.8 0.8 shard_map.108
  (6 shorter events, 0.1 us)
Async XLA Ops:
  2.1 23.5 %copy-start.1 = (bf16[1,4,2176]{2,1,0:T(4,128)(2,1)S(1)}, bf16[1,4,2176]{2,1,0:T(4,128)(2,1)}, u32[]{:S(2)}) copy-start(bf16[1,4,2176]{2,1,0:T(4,128)(2,1)} %shard_map.103) | copy-start | bytes 52228
  2.1 52.0 %copy-start = (s32[4,128]{1,0:T(4,128)S(1)}, s32[4,128]{1,0:T(4,128)}, u32[]{:S(2)}) copy-start(s32[4,128]{1,0:T(4,128)} %placement_ref.1) | copy-start | bytes 6148
  2.1 23.5 %collective-permute-start.3 = (bf16[4,2176]{1,0:T(4,128)(2,1)}, bf16[4,2176]{1,0:T(4,128)(2,1)S(1)}, u32[]{:S(2)}, u32[]{:S(2)}) collective-permute-start(bf16[4,2176]{1,0:T(4,128)(2,1)} %bitcast.14), channel_id=1, source_target_pairs={{0,8},{8,0},{1,9},{9,1},{2,10},{10,2},{3,11},{11,3},{4,12},{12,4},... | collective-permute-start | bytes 52232 | tf_op jit(solution)/shard_map/ppermute | solution.py:198
  15.4 36.6 %collective-permute-start.2 = (bf16[32,16,384]{2,1,0:T(8,128)(2,1)S(1)}, bf16[32,16,384]{2,1,0:T(8,128)(2,1)S(1)}, u32[]{:S(2)}, u32[]{:S(2)}) collective-permute-start(bf16[32,16,384]{2,1,0:T(8,128)(2,1)S(1)} %get-tuple-element.13.a), channel_id=1, source_target_pairs={{384,0},{0,128},{128,256},{256,384},{385,1},{1,129},{129,257},{257... | collective-permute-start | bytes 1179656 | tf_op jit(solution)/shard_map/ppermute | solution.py:213
  18.8 33.4 %collective-permute-start.1 = (bf16[32,16,384]{2,1,0:T(8,128)(2,1)S(1)}, bf16[32,16,384]{2,1,0:T(8,128)(2,1)S(1)}, u32[]{:S(2)}, u32[]{:S(2)}) collective-permute-start(bf16[32,16,384]{2,1,0:T(8,128)(2,1)S(1)} %get-tuple-element.13.a), channel_id=1, source_target_pairs={{256,0},{384,128},{0,256},{128,384},{257,1},{385,129},{1,257},{129... | collective-permute-start | bytes 1179656 | tf_op jit(solution)/shard_map/ppermute | solution.py:213
  22.2 31.9 %collective-permute-start = (bf16[32,16,384]{2,1,0:T(8,128)(2,1)S(1)}, bf16[32,16,384]{2,1,0:T(8,128)(2,1)S(1)}, u32[]{:S(2)}, u32[]{:S(2)}) collective-permute-start(bf16[32,16,384]{2,1,0:T(8,128)(2,1)S(1)} %get-tuple-element.13.a), channel_id=1, source_target_pairs={{128,0},{256,128},{384,256},{0,384},{129,1},{257,129},{385,257},{1... | collective-permute-start | bytes 1179656 | tf_op jit(solution)/shard_map/ppermute | solution.py:213
  55.8 55.3 %all-to-all-start = ((bf16[128,16,384]{2,1,0:T(8,128)(2,1)}), bf16[128,16,384]{2,1,0:T(8,128)(2,1)S(1)}, u32[]{:S(2)}, u32[]{:S(2)}) async-start(bf16[128,16,384]{2,1,0:T(8,128)(2,1)} %shard_map.104), calls=%async_computation | async-start | bytes 3145728 | tf_op jit(solution)/shard_map/all_to_all | solution.py:229
  67.6 32.0 %collective-permute-start.6 = (bf16[64,2176]{1,0:T(8,128)(2,1)S(1)}, bf16[64,2176]{1,0:T(8,128)(2,1)S(1)}, u32[]{:S(2)}, u32[]{:S(2)}) collective-permute-start(bf16[64,2176]{1,0:T(8,128)(2,1)S(1)} %all_gather.3), channel_id=1, source_target_pairs={{0,6},{2,0},{4,2},{6,4},{1,7},{3,1},{5,3},{7,5},{8,14},{10,8},{12,... | collective-permute-start | bytes 835592 | tf_op jit(solution)/shard_map/ppermute | solution.py:221
  71.9 27.7 %collective-permute-start.5 = (bf16[64,2176]{1,0:T(8,128)(2,1)S(1)}, bf16[64,2176]{1,0:T(8,128)(2,1)S(1)}, u32[]{:S(2)}, u32[]{:S(2)}) collective-permute-start(bf16[64,2176]{1,0:T(8,128)(2,1)S(1)} %all_gather.3), channel_id=1, source_target_pairs={{0,4},{2,6},{4,0},{6,2},{1,5},{3,7},{5,1},{7,3},{8,12},{10,14},{12... | collective-permute-start | bytes 835592 | tf_op jit(solution)/shard_map/ppermute | solution.py:221
  74.7 24.9 %collective-permute-start.4 = (bf16[64,2176]{1,0:T(8,128)(2,1)S(1)}, bf16[64,2176]{1,0:T(8,128)(2,1)S(1)}, u32[]{:S(2)}, u32[]{:S(2)}) collective-permute-start(bf16[64,2176]{1,0:T(8,128)(2,1)S(1)} %all_gather.3), channel_id=1, source_target_pairs={{0,2},{2,4},{4,6},{6,0},{1,3},{3,5},{5,7},{7,1},{8,10},{10,12},{12... | collective-permute-start | bytes 835592 | tf_op jit(solution)/shard_map/ppermute | solution.py:221
  99.7 5.3 %collective-permute-start.7 = (bf16[256,2176]{1,0:T(8,128)(2,1)S(1)}, bf16[256,2176]{1,0:T(8,128)(2,1)}, u32[]{:S(2)}, u32[]{:S(2)}) collective-permute-start(bf16[256,2176]{1,0:T(8,128)(2,1)S(1)} %constant_dynamic-update-slice_fusion.rows_ref), channel_id=1, source_target_pairs={{0,1},{1,0},{2,3},{3,2},{4,5},{5,4},{6,7},{7,6},{8,9},{9,8},{10,11... | collective-permute-start | bytes 3342344 | tf_op jit(solution)/shard_map/ppermute | solution.py:223
  113.1 3.9 %collective-permute-start.8 = (bf16[2304,128]{1,0:T(8,128)(2,1)S(1)}, bf16[2304,128]{1,0:T(8,128)(2,1)S(1)}, u32[]{:S(2)}, u32[]{:S(2)}) collective-permute-start(bf16[2304,128]{1,0:T(8,128)(2,1)S(1)} %shard_map.106), channel_id=1, source_target_pairs={{0,1},{1,0},{2,3},{3,2},{4,5},{5,4},{6,7},{7,6},{8,9},{9,8},{10,11... | collective-permute-start | bytes 1769480 | tf_op jit(solution)/shard_map/ppermute | solution.py:242

commit v9 on v8

--- a/solution.py
+++ b/solution.py
@@ -218,7 +218,7 @@
     column = lax.all_gather(pair, "y", axis=0, tiled=True)
     parts, column = lax.optimization_barrier((parts, column))
 
-    others = [lax.ppermute(column, "x", [(k, (k + t) % XS) for k in range(XS)]) for t in range(1, XS)]
+    others = [lax.ppermute(column, "x", [(k, (k + t) % XS) for k in range(XS)]) for t in (2, 1, 3)]
     own_rows = jnp.concatenate([column] + others, axis=0)
     other_rows = lax.ppermute(own_rows, "c", [(0, 1), (1, 0)])
 
@@ -232,6 +232,7 @@
     row_ids = jnp.arange(own_rows.shape[0], dtype=jnp.int32)
     i, x, y_zh = row_ids % row_count, row_ids // row_count % XS, row_ids // (row_count * XS)
     away = (lax.axis_index("x") + XS - x) % XS
+    away = jnp.where(away == 1, 2, jnp.where(away == 2, 1, away))
     source = (away * (YS * ZHS) + (y_zh ^ lax.axis_index("zh"))) * row_count + i
     pick = (source[:, None] == row_ids[None, :]).astype(jnp.bfloat16)
 

time: 160 us -> 160 us (level)
  the two profiles are of different devices: /device:TPU:64 before, /device:TPU:6 now
where the time goes in v9:
time: 160 us; the launch traced here: 157 us
  blocking collectives  67.3 us (42%)
  starting transfers between devices  44.8 us (28%)
  waiting for transfers between devices  29.1 us (18%)
  Pallas kernels  7.87 us (5%)
  other arithmetic  4 us (2%)
  between operations  3.44 us (2%)
    all_to_all x1, blocking collectives, per_device(): lax.all_to_all(chunks, ('y', 'zh', 'x'), split_axis=0, concat_axis=0, til...  40.8 us
    all_gather x1, blocking collectives, per_device(): column = lax.all_gather(pair, 'y', axis=0, tiled=True)  26.5 us
    ppermute x3, waiting for transfers between devices, per_device(): lax.ppermute(column, 'x', [(k, (k + t) % XS) for k in range(XS)])  18.9 us
    ppermute x1, starting transfers between devices, per_device(): other_rows = lax.ppermute(own_rows, 'zh', [(0, 1), (1, 0)])  11 us
    ppermute x3, starting transfers between devices, per_device(): lax.ppermute(rounded, 'g', [((i + s) % GROUPS, i) for i in range(GROUPS)])  11 us
    all_to_all x1, starting transfers between devices, per_device(): lax.all_to_all(ordered, ALONG, split_axis=0, concat_axis=0, tiled=True)  9.71 us
    all_to_all x1, waiting for transfers between devices, per_device(): lax.all_to_all(ordered, ALONG, split_axis=0, concat_axis=0, tiled=True)  9.44 us
    ppermute x3, starting transfers between devices, per_device(): lax.ppermute(column, 'x', [(k, (k + t) % XS) for k in range(XS)])  9.21 us
  transfers between devices with their start and end apart: 10, of which 4 were waited for; matrix products, arithmetic and copies ran while one was open for 3% of the time, Pallas kernels for 1%

profile of v9, /device:TPU:6, one launch (start us, length us, event | category | flops | bytes accessed | tf_op | source)
XLA Modules:
  0.0 156.6 jit_solution(10531486880883205985)
XLA Ops:
  0.6 1.4 shard_map.103
  2.1 0.0 copy-start.1
  2.1 0.0 copy-start
  2.1 11.0 %collective-permute-start.3 = (bf16[4,2176]{1,0:T(4,128)(2,1)}, bf16[4,2176]{1,0:T(4,128)(2,1)S(1)}, u32[]{:S(2)}, u32[]{:S(2)}) collective-permute-start(bf16[4,2176]{1,0:T(4,128)(2,1)} %bitcast.14), channel_id=1, source_target_pairs={{0,8},{8,0},{1,9},{9,1},{2,10},{10,2},{3,11},{11,3},{4,12},{12,4},... | collective-permute-start | bytes 52232 | tf_op jit(solution)/shard_map/ppermute | solution.py:198
  13.1 3.2 %fusion.22 = (bf16[32,16,384]{2,1,0:T(8,128)(2,1)S(1)}, f32[32,16,384]{2,1,0:T(8,128)}) fusion(f32[32,16,384]{2,1,0:T(8,128)} %param.8, f32[32,16,384]{2,1,0:T(8,128)} %param.10, bf16[32,16,384]{2,1,0:T(8,128)(2,1)} %param.11, f32[32,16,384]{2,1,0:T(8,128)} %param.9), kind=kLoop, calls=%fused_computation.47 | loop fusion | flops 3145728 | bytes 3932160 | tf_op jit(solution)/shard_map/convert_element_type | solution.py:209
  16.3 3.4 %collective-permute-start.2 = (bf16[32,16,384]{2,1,0:T(8,128)(2,1)S(1)}, bf16[32,16,384]{2,1,0:T(8,128)(2,1)S(1)}, u32[]{:S(2)}, u32[]{:S(2)}) collective-permute-start(bf16[32,16,384]{2,1,0:T(8,128)(2,1)S(1)} %get-tuple-element.13.a), channel_id=1, source_target_pairs={{384,0},{0,128},{128,256},{256,384},{385,1},{1,129},{129,257},{257... | collective-permute-start | bytes 1179656 | tf_op jit(solution)/shard_map/ppermute | solution.py:213
  19.7 4.3 %collective-permute-start.1 = (bf16[32,16,384]{2,1,0:T(8,128)(2,1)S(1)}, bf16[32,16,384]{2,1,0:T(8,128)(2,1)S(1)}, u32[]{:S(2)}, u32[]{:S(2)}) collective-permute-start(bf16[32,16,384]{2,1,0:T(8,128)(2,1)S(1)} %get-tuple-element.13.a), channel_id=1, source_target_pairs={{256,0},{384,128},{0,256},{128,384},{257,1},{385,129},{1,257},{129... | collective-permute-start | bytes 1179656 | tf_op jit(solution)/shard_map/ppermute | solution.py:213
  24.0 3.4 %collective-permute-start = (bf16[32,16,384]{2,1,0:T(8,128)(2,1)S(1)}, bf16[32,16,384]{2,1,0:T(8,128)(2,1)S(1)}, u32[]{:S(2)}, u32[]{:S(2)}) collective-permute-start(bf16[32,16,384]{2,1,0:T(8,128)(2,1)S(1)} %get-tuple-element.13.a), channel_id=1, source_target_pairs={{128,0},{256,128},{384,256},{0,384},{129,1},{257,129},{385,257},{1... | collective-permute-start | bytes 1179656 | tf_op jit(solution)/shard_map/ppermute | solution.py:213
  27.4 0.0 collective-permute-done.3
  27.4 0.0 copy-done.1
  27.4 26.5 %all_gather.3 = bf16[64,2176]{1,0:T(8,128)(2,1)S(1)} all-gather(bf16[8,2176]{1,0:T(8,128)(2,1)S(1)} %pad_maximum_fusion), channel_id=1, replica_groups=mesh['g'=4,'y'=8,'zh'=2,'x'=4,'c'=2] {'y'}, dimensions={0}, use_global_device_ids=true | all-gather | bytes 313344 | tf_op jit(solution)/shard_map/all_gather | solution.py:218
  54.0 0.0 collective-permute-done.2.d
  54.0 0.0 collective-permute-done.1.c
  54.0 0.0 collective-permute-done.b
  54.0 0.0 copy-done
  54.0 1.7 %shard_map.104 = bf16[128,16,384]{2,1,0:T(8,128)(2,1)} custom-call(s32[1]{0:T(128)} %bitcast.3.group_ref, s32[4,128]{1,0:T(4,128)S(1)} %copy-done, bf16[32,16,384]{2,1,0:T(8,128)(2,1)S(1)} %get-tuple-element.13.a, bf16[32,16,384]{2,1,0:T(8,128)(2,1)S(1)} %collective-permute-done.b, bf16[32,16,384]{2,1,0:T(8,128)(2,1)S(1)} %collective-permute-done.1.c, ...), custom_call_target="tpu_custom_call" | custom-call | tf_op jit(solution)/shard_map/pallas_call | solution.py:64
  55.7 9.7 %all-to-all-start = ((bf16[128,16,384]{2,1,0:T(8,128)(2,1)}), bf16[128,16,384]{2,1,0:T(8,128)(2,1)S(1)}, u32[]{:S(2)}, u32[]{:S(2)}) async-start(bf16[128,16,384]{2,1,0:T(8,128)(2,1)} %shard_map.104), calls=%async_computation | async-start | bytes 3145728 | tf_op jit(solution)/shard_map/all_to_all | solution.py:229
  65.4 2.8 %collective-permute-start.6 = (bf16[64,2176]{1,0:T(8,128)(2,1)S(1)}, bf16[64,2176]{1,0:T(8,128)(2,1)S(1)}, u32[]{:S(2)}, u32[]{:S(2)}) collective-permute-start(bf16[64,2176]{1,0:T(8,128)(2,1)S(1)} %all_gather.3), channel_id=1, source_target_pairs={{0,6},{2,0},{4,2},{6,4},{1,7},{3,1},{5,3},{7,5},{8,14},{10,8},{12,... | collective-permute-start | bytes 835592 | tf_op jit(solution)/shard_map/ppermute | solution.py:221
  68.2 4.3 %collective-permute-start.5 = (bf16[64,2176]{1,0:T(8,128)(2,1)S(1)}, bf16[64,2176]{1,0:T(8,128)(2,1)S(1)}, u32[]{:S(2)}, u32[]{:S(2)}) collective-permute-start(bf16[64,2176]{1,0:T(8,128)(2,1)S(1)} %all_gather.3), channel_id=1, source_target_pairs={{0,2},{2,4},{4,6},{6,0},{1,3},{3,5},{5,7},{7,1},{8,10},{10,12},{12... | collective-permute-start | bytes 835592 | tf_op jit(solution)/shard_map/ppermute | solution.py:221
  72.5 2.2 %collective-permute-start.4 = (bf16[64,2176]{1,0:T(8,128)(2,1)S(1)}, bf16[64,2176]{1,0:T(8,128)(2,1)S(1)}, u32[]{:S(2)}, u32[]{:S(2)}) collective-permute-start(bf16[64,2176]{1,0:T(8,128)(2,1)S(1)} %all_gather.3), channel_id=1, source_target_pairs={{0,4},{2,6},{4,0},{6,2},{1,5},{3,7},{5,1},{7,3},{8,12},{10,14},{12... | collective-permute-start | bytes 835592 | tf_op jit(solution)/shard_map/ppermute | solution.py:221
  74.7 16.3 %collective-permute-done.4 = bf16[64,2176]{1,0:T(8,128)(2,1)S(1)} collective-permute-done((bf16[64,2176]{1,0:T(8,128)(2,1)S(1)}, bf16[64,2176]{1,0:T(8,128)(2,1)S(1)}, u32[]{:S(2)}, u32[]{:S(2)}) %collective-permute-start.4) | collective-permute-done | bytes 278560 | tf_op jit(solution)/shard_map/ppermute | solution.py:221
  91.0 2.6 %collective-permute-done.5 = bf16[64,2176]{1,0:T(8,128)(2,1)S(1)} collective-permute-done((bf16[64,2176]{1,0:T(8,128)(2,1)S(1)}, bf16[64,2176]{1,0:T(8,128)(2,1)S(1)}, u32[]{:S(2)}, u32[]{:S(2)}) %collective-permute-start.5) | collective-permute-done | bytes 278560 | tf_op jit(solution)/shard_map/ppermute | solution.py:221
  93.6 0.0 collective-permute-done.6
  93.7 1.9 %collective-permute-start.7 = (bf16[256,2176]{1,0:T(8,128)(2,1)S(1)}, bf16[256,2176]{1,0:T(8,128)(2,1)}, u32[]{:S(2)}, u32[]{:S(2)}) collective-permute-start(bf16[256,2176]{1,0:T(8,128)(2,1)S(1)} %constant_dynamic-update-slice_fusion.rows_ref), channel_id=1, source_target_pairs={{0,1},{1,0},{2,3},{3,2},{4,5},{5,4},{6,7},{7,6},{8,9},{9,8},{10,11... | collective-permute-start | bytes 3342344 | tf_op jit(solution)/shard_map/ppermute | solution.py:223
  95.6 0.6 fusion.21
  98.9 0.1 fusion.9.pick_ref
  99.0 0.0 collective-permute-done.7.rows_ref
  99.0 9.4 %all-to-all-done = bf16[128,16,384]{2,1,0:T(8,128)(2,1)S(1)} async-done(((bf16[128,16,384]{2,1,0:T(8,128)(2,1)}), bf16[128,16,384]{2,1,0:T(8,128)(2,1)S(1)}, u32[]{:S(2)}, u32[]{:S(2)}) %all-to-all-start) | async-done | bytes 1572896 | tf_op jit(solution)/shard_map/all_to_all | solution.py:229
  108.4 2.0 %shard_map.106 = bf16[2304,128]{1,0:T(8,128)(2,1)S(1)} custom-call(s32[1]{0:T(128)S(6)} %select_n.73.expert_ref, bf16[256,256]{1,0:T(8,128)(2,1)S(1)} %fusion.9.pick_ref, bf16[256,2176]{1,0:T(8,128)(2,1)} %collective-permute-done.7.rows_ref, bf16[2048,384]{1,0:T(8,128)(2,1)S(1)} %bitcast.11), custom_call_target="tpu_custom_call" | custom-call | tf_op jit(solution)/shard_map/pallas_call | solution.py:112
  110.5 2.0 %collective-permute-start.8 = (bf16[2304,128]{1,0:T(8,128)(2,1)S(1)}, bf16[2304,128]{1,0:T(8,128)(2,1)S(1)}, u32[]{:S(2)}, u32[]{:S(2)}) collective-permute-start(bf16[2304,128]{1,0:T(8,128)(2,1)S(1)} %shard_map.106), channel_id=1, source_target_pairs={{0,1},{1,0},{2,3},{3,2},{4,5},{5,4},{6,7},{7,6},{8,9},{9,8},{10,11... | collective-permute-start | bytes 1769480 | tf_op jit(solution)/shard_map/ppermute | solution.py:243
  112.4 1.2 shard_map.105
  113.7 0.7 collective-permute-done.8.recv_ref
  114.4 0.7 shard_map.107
  115.1 40.8 %all_to_all.10.ref = bf16[64,64,128]{2,1,0:T(8,128)(2,1)S(1)} all-to-all(bf16[64,64,128]{2,1,0:T(8,128)(2,1)S(1)} %bitcast.13), channel_id=1, replica_groups=mesh['g'=4,'y'=8,'zh'=2,'x'=4,'c'=2] {'y','zh','x'}, dimensions={0} | all-to-all | bytes 2097152 | tf_op jit(solution)/shard_map/all_to_all | solution.py:245
  155.9 0.8 shard_map.108
  (6 shorter events, 0.1 us)
Async XLA Ops:
  2.1 25.3 %copy-start.1 = (bf16[1,4,2176]{2,1,0:T(4,128)(2,1)S(1)}, bf16[1,4,2176]{2,1,0:T(4,128)(2,1)}, u32[]{:S(2)}) copy-start(bf16[1,4,2176]{2,1,0:T(4,128)(2,1)} %shard_map.103) | copy-start | bytes 52228
  2.1 51.9 %copy-start = (s32[4,128]{1,0:T(4,128)S(1)}, s32[4,128]{1,0:T(4,128)}, u32[]{:S(2)}) copy-start(s32[4,128]{1,0:T(4,128)} %placement_ref.1) | copy-start | bytes 6148
  2.1 25.3 %collective-permute-start.3 = (bf16[4,2176]{1,0:T(4,128)(2,1)}, bf16[4,2176]{1,0:T(4,128)(2,1)S(1)}, u32[]{:S(2)}, u32[]{:S(2)}) collective-permute-start(bf16[4,2176]{1,0:T(4,128)(2,1)} %bitcast.14), channel_id=1, source_target_pairs={{0,8},{8,0},{1,9},{9,1},{2,10},{10,2},{3,11},{11,3},{4,12},{12,4},... | collective-permute-start | bytes 52232 | tf_op jit(solution)/shard_map/ppermute | solution.py:198
  16.3 37.6 %collective-permute-start.2 = (bf16[32,16,384]{2,1,0:T(8,128)(2,1)S(1)}, bf16[32,16,384]{2,1,0:T(8,128)(2,1)S(1)}, u32[]{:S(2)}, u32[]{:S(2)}) collective-permute-start(bf16[32,16,384]{2,1,0:T(8,128)(2,1)S(1)} %get-tuple-element.13.a), channel_id=1, source_target_pairs={{384,0},{0,128},{128,256},{256,384},{385,1},{1,129},{129,257},{257... | collective-permute-start | bytes 1179656 | tf_op jit(solution)/shard_map/ppermute | solution.py:213
  19.7 34.3 %collective-permute-start.1 = (bf16[32,16,384]{2,1,0:T(8,128)(2,1)S(1)}, bf16[32,16,384]{2,1,0:T(8,128)(2,1)S(1)}, u32[]{:S(2)}, u32[]{:S(2)}) collective-permute-start(bf16[32,16,384]{2,1,0:T(8,128)(2,1)S(1)} %get-tuple-element.13.a), channel_id=1, source_target_pairs={{256,0},{384,128},{0,256},{128,384},{257,1},{385,129},{1,257},{129... | collective-permute-start | bytes 1179656 | tf_op jit(solution)/shard_map/ppermute | solution.py:213
  24.0 30.0 %collective-permute-start = (bf16[32,16,384]{2,1,0:T(8,128)(2,1)S(1)}, bf16[32,16,384]{2,1,0:T(8,128)(2,1)S(1)}, u32[]{:S(2)}, u32[]{:S(2)}) collective-permute-start(bf16[32,16,384]{2,1,0:T(8,128)(2,1)S(1)} %get-tuple-element.13.a), channel_id=1, source_target_pairs={{128,0},{256,128},{384,256},{0,384},{129,1},{257,129},{385,257},{1... | collective-permute-start | bytes 1179656 | tf_op jit(solution)/shard_map/ppermute | solution.py:213
  55.7 52.7 %all-to-all-start = ((bf16[128,16,384]{2,1,0:T(8,128)(2,1)}), bf16[128,16,384]{2,1,0:T(8,128)(2,1)S(1)}, u32[]{:S(2)}, u32[]{:S(2)}) async-start(bf16[128,16,384]{2,1,0:T(8,128)(2,1)} %shard_map.104), calls=%async_computation | async-start | bytes 3145728 | tf_op jit(solution)/shard_map/all_to_all | solution.py:229
  65.4 28.2 %collective-permute-start.6 = (bf16[64,2176]{1,0:T(8,128)(2,1)S(1)}, bf16[64,2176]{1,0:T(8,128)(2,1)S(1)}, u32[]{:S(2)}, u32[]{:S(2)}) collective-permute-start(bf16[64,2176]{1,0:T(8,128)(2,1)S(1)} %all_gather.3), channel_id=1, source_target_pairs={{0,6},{2,0},{4,2},{6,4},{1,7},{3,1},{5,3},{7,5},{8,14},{10,8},{12,... | collective-permute-start | bytes 835592 | tf_op jit(solution)/shard_map/ppermute | solution.py:221
  68.2 25.4 %collective-permute-start.5 = (bf16[64,2176]{1,0:T(8,128)(2,1)S(1)}, bf16[64,2176]{1,0:T(8,128)(2,1)S(1)}, u32[]{:S(2)}, u32[]{:S(2)}) collective-permute-start(bf16[64,2176]{1,0:T(8,128)(2,1)S(1)} %all_gather.3), channel_id=1, source_target_pairs={{0,2},{2,4},{4,6},{6,0},{1,3},{3,5},{5,7},{7,1},{8,10},{10,12},{12... | collective-permute-start | bytes 835592 | tf_op jit(solution)/shard_map/ppermute | solution.py:221
  72.5 18.5 %collective-permute-start.4 = (bf16[64,2176]{1,0:T(8,128)(2,1)S(1)}, bf16[64,2176]{1,0:T(8,128)(2,1)S(1)}, u32[]{:S(2)}, u32[]{:S(2)}) collective-permute-start(bf16[64,2176]{1,0:T(8,128)(2,1)S(1)} %all_gather.3), channel_id=1, source_target_pairs={{0,4},{2,6},{4,0},{6,2},{1,5},{3,7},{5,1},{7,3},{8,12},{10,14},{12... | collective-permute-start | bytes 835592 | tf_op jit(solution)/shard_map/ppermute | solution.py:221
  93.7 5.3 %collective-permute-start.7 = (bf16[256,2176]{1,0:T(8,128)(2,1)S(1)}, bf16[256,2176]{1,0:T(8,128)(2,1)}, u32[]{:S(2)}, u32[]{:S(2)}) collective-permute-start(bf16[256,2176]{1,0:T(8,128)(2,1)S(1)} %constant_dynamic-update-slice_fusion.rows_ref), channel_id=1, source_target_pairs={{0,1},{1,0},{2,3},{3,2},{4,5},{5,4},{6,7},{7,6},{8,9},{9,8},{10,11... | collective-permute-start | bytes 3342344 | tf_op jit(solution)/shard_map/ppermute | solution.py:223
  110.5 3.9 %collective-permute-start.8 = (bf16[2304,128]{1,0:T(8,128)(2,1)S(1)}, bf16[2304,128]{1,0:T(8,128)(2,1)S(1)}, u32[]{:S(2)}, u32[]{:S(2)}) collective-permute-start(bf16[2304,128]{1,0:T(8,128)(2,1)S(1)} %shard_map.106), channel_id=1, source_target_pairs={{0,1},{1,0},{2,3},{3,2},{4,5},{5,4},{6,7},{7,6},{8,9},{9,8},{10,11... | collective-permute-start | bytes 1769480 | tf_op jit(solution)/shard_map/ppermute | solution.py:243

commit v10 on v9

--- a/solution.py
+++ b/solution.py
@@ -16,6 +16,7 @@
 ALONG = ("y", "zh", "x", "c")
 EXPERT_COUNT = 16
 EXTRA = 128
+RELAY = (1, 3, 2)
 
 
 def extend_rows(copies, tokens, routed, gates):
@@ -52,7 +53,7 @@
     def kernel(group_ref, placement_ref, a, b, c, d, out_hbm, sem):
         own = group_ref[0]
         for k, ref in enumerate((a, b, c, d)):
-            base = ((own + k) % len(parts)) * count
+            base = ((own + (0, *RELAY)[k]) % len(parts)) * count
 
             def body(i, _, ref=ref, base=base):
                 pltpu.make_async_copy(ref.at[i], out_hbm.at[placement_ref[own, base + i]], sem).start()
@@ -211,7 +212,7 @@
 
     parts = [rounded] + [
         lax.ppermute(rounded, "g", [((i + s) % GROUPS, i) for i in range(GROUPS)])
-        for s in range(1, GROUPS)
+        for s in RELAY
     ]
 
     pair = jnp.concatenate([own_rows, other_rows], axis=0)

time: 160 us -> 159 us (level)
  no operation moved by 1% of the time
where the time goes in v10:
time: 159 us; the launch traced here: 157 us
  blocking collectives  66.5 us (42%)
  starting transfers between devices  46 us (29%)
  waiting for transfers between devices  29 us (18%)
  Pallas kernels  7.87 us (5%)
  other arithmetic  4 us (3%)
  between operations  3.44 us (2%)
    all_to_all x1, blocking collectives, per_device(): lax.all_to_all(chunks, ('y', 'zh', 'x'), split_axis=0, concat_axis=0, til...  40.1 us
    all_gather x1, blocking collectives, per_device(): column = lax.all_gather(pair, 'y', axis=0, tiled=True)  26.4 us
    ppermute x3, waiting for transfers between devices, per_device(): lax.ppermute(column, 'x', [(k, (k + t) % XS) for k in range(XS)])  18.8 us
    ppermute x3, starting transfers between devices, per_device(): lax.ppermute(rounded, 'g', [((i + s) % GROUPS, i) for i in range(GROUPS)])  11.9 us
    ppermute x1, starting transfers between devices, per_device(): other_rows = lax.ppermute(own_rows, 'zh', [(0, 1), (1, 0)])  11 us
    all_to_all x1, starting transfers between devices, per_device(): lax.all_to_all(ordered, ALONG, split_axis=0, concat_axis=0, tiled=True)  9.91 us
    all_to_all x1, waiting for transfers between devices, per_device(): lax.all_to_all(ordered, ALONG, split_axis=0, concat_axis=0, tiled=True)  9.52 us
    ppermute x3, starting transfers between devices, per_device(): lax.ppermute(column, 'x', [(k, (k + t) % XS) for k in range(XS)])  9.21 us
  transfers between devices with their start and end apart: 10, of which 4 were waited for; matrix products, arithmetic and copies ran while one was open for 3% of the time, Pallas kernels for 1%

profile of v10, /device:TPU:6, one launch (start us, length us, event | category | flops | bytes accessed | tf_op | source)
XLA Modules:
  0.0 157.0 jit_solution(1355584709680543810)
XLA Ops:
  0.6 1.4 shard_map.103
  2.1 0.0 copy-start.1
  2.1 0.0 copy-start
  2.1 11.0 %collective-permute-start.3 = (bf16[4,2176]{1,0:T(4,128)(2,1)}, bf16[4,2176]{1,0:T(4,128)(2,1)S(1)}, u32[]{:S(2)}, u32[]{:S(2)}) collective-permute-start(bf16[4,2176]{1,0:T(4,128)(2,1)} %bitcast.14), channel_id=1, source_target_pairs={{0,8},{8,0},{1,9},{9,1},{2,10},{10,2},{3,11},{11,3},{4,12},{12,4},... | collective-permute-start | bytes 52232 | tf_op jit(solution)/shard_map/ppermute | solution.py:199
  13.1 3.2 %fusion.22 = (bf16[32,16,384]{2,1,0:T(8,128)(2,1)S(1)}, f32[32,16,384]{2,1,0:T(8,128)}) fusion(f32[32,16,384]{2,1,0:T(8,128)} %param.8, f32[32,16,384]{2,1,0:T(8,128)} %param.10, bf16[32,16,384]{2,1,0:T(8,128)(2,1)} %param.11, f32[32,16,384]{2,1,0:T(8,128)} %param.9), kind=kLoop, calls=%fused_computation.47 | loop fusion | flops 3145728 | bytes 3932160 | tf_op jit(solution)/shard_map/convert_element_type | solution.py:210
  16.3 4.3 %collective-permute-start.2 = (bf16[32,16,384]{2,1,0:T(8,128)(2,1)S(1)}, bf16[32,16,384]{2,1,0:T(8,128)(2,1)S(1)}, u32[]{:S(2)}, u32[]{:S(2)}) collective-permute-start(bf16[32,16,384]{2,1,0:T(8,128)(2,1)S(1)} %get-tuple-element.13.a), channel_id=1, source_target_pairs={{256,0},{384,128},{0,256},{128,384},{257,1},{385,129},{1,257},{129... | collective-permute-start | bytes 1179656 | tf_op jit(solution)/shard_map/ppermute | solution.py:214
  20.6 3.4 %collective-permute-start.1 = (bf16[32,16,384]{2,1,0:T(8,128)(2,1)S(1)}, bf16[32,16,384]{2,1,0:T(8,128)(2,1)S(1)}, u32[]{:S(2)}, u32[]{:S(2)}) collective-permute-start(bf16[32,16,384]{2,1,0:T(8,128)(2,1)S(1)} %get-tuple-element.13.a), channel_id=1, source_target_pairs={{384,0},{0,128},{128,256},{256,384},{385,1},{1,129},{129,257},{257... | collective-permute-start | bytes 1179656 | tf_op jit(solution)/shard_map/ppermute | solution.py:214
  24.0 4.3 %collective-permute-start = (bf16[32,16,384]{2,1,0:T(8,128)(2,1)S(1)}, bf16[32,16,384]{2,1,0:T(8,128)(2,1)S(1)}, u32[]{:S(2)}, u32[]{:S(2)}) collective-permute-start(bf16[32,16,384]{2,1,0:T(8,128)(2,1)S(1)} %get-tuple-element.13.a), channel_id=1, source_target_pairs={{128,0},{256,128},{384,256},{0,384},{129,1},{257,129},{385,257},{1... | collective-permute-start | bytes 1179656 | tf_op jit(solution)/shard_map/ppermute | solution.py:214
  28.3 0.0 collective-permute-done.3
  28.3 0.0 copy-done.1
  28.3 26.4 %all_gather.3 = bf16[64,2176]{1,0:T(8,128)(2,1)S(1)} all-gather(bf16[8,2176]{1,0:T(8,128)(2,1)S(1)} %pad_maximum_fusion), channel_id=1, replica_groups=mesh['g'=4,'y'=8,'zh'=2,'x'=4,'c'=2] {'y'}, dimensions={0}, use_global_device_ids=true | all-gather | bytes 313344 | tf_op jit(solution)/shard_map/all_gather | solution.py:219
  54.7 0.0 collective-permute-done.2.d
  54.8 0.0 collective-permute-done.1.c
  54.8 0.0 collective-permute-done.b
  54.8 0.0 copy-done
  54.8 1.7 %shard_map.104 = bf16[128,16,384]{2,1,0:T(8,128)(2,1)} custom-call(s32[1]{0:T(128)} %bitcast.3.group_ref, s32[4,128]{1,0:T(4,128)S(1)} %copy-done, bf16[32,16,384]{2,1,0:T(8,128)(2,1)S(1)} %get-tuple-element.13.a, bf16[32,16,384]{2,1,0:T(8,128)(2,1)S(1)} %collective-permute-done.b, bf16[32,16,384]{2,1,0:T(8,128)(2,1)S(1)} %collective-permute-done.1.c, ...), custom_call_target="tpu_custom_call" | custom-call | tf_op jit(solution)/shard_map/pallas_call | solution.py:65
  56.5 9.9 %all-to-all-start = ((bf16[128,16,384]{2,1,0:T(8,128)(2,1)}), bf16[128,16,384]{2,1,0:T(8,128)(2,1)S(1)}, u32[]{:S(2)}, u32[]{:S(2)}) async-start(bf16[128,16,384]{2,1,0:T(8,128)(2,1)} %shard_map.104), calls=%async_computation | async-start | bytes 3145728 | tf_op jit(solution)/shard_map/all_to_all | solution.py:230
  66.4 2.8 %collective-permute-start.6 = (bf16[64,2176]{1,0:T(8,128)(2,1)S(1)}, bf16[64,2176]{1,0:T(8,128)(2,1)S(1)}, u32[]{:S(2)}, u32[]{:S(2)}) collective-permute-start(bf16[64,2176]{1,0:T(8,128)(2,1)S(1)} %all_gather.3), channel_id=1, source_target_pairs={{0,6},{2,0},{4,2},{6,4},{1,7},{3,1},{5,3},{7,5},{8,14},{10,8},{12,... | collective-permute-start | bytes 835592 | tf_op jit(solution)/shard_map/ppermute | solution.py:222
  69.2 4.3 %collective-permute-start.5 = (bf16[64,2176]{1,0:T(8,128)(2,1)S(1)}, bf16[64,2176]{1,0:T(8,128)(2,1)S(1)}, u32[]{:S(2)}, u32[]{:S(2)}) collective-permute-start(bf16[64,2176]{1,0:T(8,128)(2,1)S(1)} %all_gather.3), channel_id=1, source_target_pairs={{0,2},{2,4},{4,6},{6,0},{1,3},{3,5},{5,7},{7,1},{8,10},{10,12},{12... | collective-permute-start | bytes 835592 | tf_op jit(solution)/shard_map/ppermute | solution.py:222
  73.5 2.2 %collective-permute-start.4 = (bf16[64,2176]{1,0:T(8,128)(2,1)S(1)}, bf16[64,2176]{1,0:T(8,128)(2,1)S(1)}, u32[]{:S(2)}, u32[]{:S(2)}) collective-permute-start(bf16[64,2176]{1,0:T(8,128)(2,1)S(1)} %all_gather.3), channel_id=1, source_target_pairs={{0,4},{2,6},{4,0},{6,2},{1,5},{3,7},{5,1},{7,3},{8,12},{10,14},{12... | collective-permute-start | bytes 835592 | tf_op jit(solution)/shard_map/ppermute | solution.py:222
  75.7 16.5 %collective-permute-done.4 = bf16[64,2176]{1,0:T(8,128)(2,1)S(1)} collective-permute-done((bf16[64,2176]{1,0:T(8,128)(2,1)S(1)}, bf16[64,2176]{1,0:T(8,128)(2,1)S(1)}, u32[]{:S(2)}, u32[]{:S(2)}) %collective-permute-start.4) | collective-permute-done | bytes 278560 | tf_op jit(solution)/shard_map/ppermute | solution.py:222
  92.2 2.4 %collective-permute-done.5 = bf16[64,2176]{1,0:T(8,128)(2,1)S(1)} collective-permute-done((bf16[64,2176]{1,0:T(8,128)(2,1)S(1)}, bf16[64,2176]{1,0:T(8,128)(2,1)S(1)}, u32[]{:S(2)}, u32[]{:S(2)}) %collective-permute-start.5) | collective-permute-done | bytes 278560 | tf_op jit(solution)/shard_map/ppermute | solution.py:222
  94.5 0.0 collective-permute-done.6
  94.6 1.9 %collective-permute-start.7 = (bf16[256,2176]{1,0:T(8,128)(2,1)S(1)}, bf16[256,2176]{1,0:T(8,128)(2,1)}, u32[]{:S(2)}, u32[]{:S(2)}) collective-permute-start(bf16[256,2176]{1,0:T(8,128)(2,1)S(1)} %constant_dynamic-update-slice_fusion.rows_ref), channel_id=1, source_target_pairs={{0,1},{1,0},{2,3},{3,2},{4,5},{5,4},{6,7},{7,6},{8,9},{9,8},{10,11... | collective-permute-start | bytes 3342344 | tf_op jit(solution)/shard_map/ppermute | solution.py:224
  96.5 0.6 fusion.21
  99.8 0.1 fusion.9.pick_ref
  99.9 0.0 collective-permute-done.7.rows_ref
  99.9 9.5 %all-to-all-done = bf16[128,16,384]{2,1,0:T(8,128)(2,1)S(1)} async-done(((bf16[128,16,384]{2,1,0:T(8,128)(2,1)}), bf16[128,16,384]{2,1,0:T(8,128)(2,1)S(1)}, u32[]{:S(2)}, u32[]{:S(2)}) %all-to-all-start) | async-done | bytes 1572896 | tf_op jit(solution)/shard_map/all_to_all | solution.py:230
  109.4 2.0 %shard_map.106 = bf16[2304,128]{1,0:T(8,128)(2,1)S(1)} custom-call(s32[1]{0:T(128)S(6)} %select_n.73.expert_ref, bf16[256,256]{1,0:T(8,128)(2,1)S(1)} %fusion.9.pick_ref, bf16[256,2176]{1,0:T(8,128)(2,1)} %collective-permute-done.7.rows_ref, bf16[2048,384]{1,0:T(8,128)(2,1)S(1)} %bitcast.11), custom_call_target="tpu_custom_call" | custom-call | tf_op jit(solution)/shard_map/pallas_call | solution.py:113
  111.5 2.0 %collective-permute-start.8 = (bf16[2304,128]{1,0:T(8,128)(2,1)S(1)}, bf16[2304,128]{1,0:T(8,128)(2,1)S(1)}, u32[]{:S(2)}, u32[]{:S(2)}) collective-permute-start(bf16[2304,128]{1,0:T(8,128)(2,1)S(1)} %shard_map.106), channel_id=1, source_target_pairs={{0,1},{1,0},{2,3},{3,2},{4,5},{5,4},{6,7},{7,6},{8,9},{9,8},{10,11... | collective-permute-start | bytes 1769480 | tf_op jit(solution)/shard_map/ppermute | solution.py:244
  113.4 1.2 shard_map.105
  114.7 0.7 collective-permute-done.8.recv_ref
  115.4 0.7 shard_map.107
  116.1 40.1 %all_to_all.10.ref = bf16[64,64,128]{2,1,0:T(8,128)(2,1)S(1)} all-to-all(bf16[64,64,128]{2,1,0:T(8,128)(2,1)S(1)} %bitcast.13), channel_id=1, replica_groups=mesh['g'=4,'y'=8,'zh'=2,'x'=4,'c'=2] {'y','zh','x'}, dimensions={0} | all-to-all | bytes 2097152 | tf_op jit(solution)/shard_map/all_to_all | solution.py:246
  156.2 0.8 shard_map.108
  (6 shorter events, 0.1 us)
Async XLA Ops:
  2.1 26.2 %copy-start.1 = (bf16[1,4,2176]{2,1,0:T(4,128)(2,1)S(1)}, bf16[1,4,2176]{2,1,0:T(4,128)(2,1)}, u32[]{:S(2)}) copy-start(bf16[1,4,2176]{2,1,0:T(4,128)(2,1)} %shard_map.103) | copy-start | bytes 52228
  2.1 52.7 %copy-start = (s32[4,128]{1,0:T(4,128)S(1)}, s32[4,128]{1,0:T(4,128)}, u32[]{:S(2)}) copy-start(s32[4,128]{1,0:T(4,128)} %placement_ref.1) | copy-start | bytes 6148
  2.1 26.2 %collective-permute-start.3 = (bf16[4,2176]{1,0:T(4,128)(2,1)}, bf16[4,2176]{1,0:T(4,128)(2,1)S(1)}, u32[]{:S(2)}, u32[]{:S(2)}) collective-permute-start(bf16[4,2176]{1,0:T(4,128)(2,1)} %bitcast.14), channel_id=1, source_target_pairs={{0,8},{8,0},{1,9},{9,1},{2,10},{10,2},{3,11},{11,3},{4,12},{12,4},... | collective-permute-start | bytes 52232 | tf_op jit(solution)/shard_map/ppermute | solution.py:199
  16.3 38.4 %collective-permute-start.2 = (bf16[32,16,384]{2,1,0:T(8,128)(2,1)S(1)}, bf16[32,16,384]{2,1,0:T(8,128)(2,1)S(1)}, u32[]{:S(2)}, u32[]{:S(2)}) collective-permute-start(bf16[32,16,384]{2,1,0:T(8,128)(2,1)S(1)} %get-tuple-element.13.a), channel_id=1, source_target_pairs={{256,0},{384,128},{0,256},{128,384},{257,1},{385,129},{1,257},{129... | collective-permute-start | bytes 1179656 | tf_op jit(solution)/shard_map/ppermute | solution.py:214
  20.6 34.1 %collective-permute-start.1 = (bf16[32,16,384]{2,1,0:T(8,128)(2,1)S(1)}, bf16[32,16,384]{2,1,0:T(8,128)(2,1)S(1)}, u32[]{:S(2)}, u32[]{:S(2)}) collective-permute-start(bf16[32,16,384]{2,1,0:T(8,128)(2,1)S(1)} %get-tuple-element.13.a), channel_id=1, source_target_pairs={{384,0},{0,128},{128,256},{256,384},{385,1},{1,129},{129,257},{257... | collective-permute-start | bytes 1179656 | tf_op jit(solution)/shard_map/ppermute | solution.py:214
  24.0 30.7 %collective-permute-start = (bf16[32,16,384]{2,1,0:T(8,128)(2,1)S(1)}, bf16[32,16,384]{2,1,0:T(8,128)(2,1)S(1)}, u32[]{:S(2)}, u32[]{:S(2)}) collective-permute-start(bf16[32,16,384]{2,1,0:T(8,128)(2,1)S(1)} %get-tuple-element.13.a), channel_id=1, source_target_pairs={{128,0},{256,128},{384,256},{0,384},{129,1},{257,129},{385,257},{1... | collective-permute-start | bytes 1179656 | tf_op jit(solution)/shard_map/ppermute | solution.py:214
  56.5 52.9 %all-to-all-start = ((bf16[128,16,384]{2,1,0:T(8,128)(2,1)}), bf16[128,16,384]{2,1,0:T(8,128)(2,1)S(1)}, u32[]{:S(2)}, u32[]{:S(2)}) async-start(bf16[128,16,384]{2,1,0:T(8,128)(2,1)} %shard_map.104), calls=%async_computation | async-start | bytes 3145728 | tf_op jit(solution)/shard_map/all_to_all | solution.py:230
  66.4 28.1 %collective-permute-start.6 = (bf16[64,2176]{1,0:T(8,128)(2,1)S(1)}, bf16[64,2176]{1,0:T(8,128)(2,1)S(1)}, u32[]{:S(2)}, u32[]{:S(2)}) collective-permute-start(bf16[64,2176]{1,0:T(8,128)(2,1)S(1)} %all_gather.3), channel_id=1, source_target_pairs={{0,6},{2,0},{4,2},{6,4},{1,7},{3,1},{5,3},{7,5},{8,14},{10,8},{12,... | collective-permute-start | bytes 835592 | tf_op jit(solution)/shard_map/ppermute | solution.py:222
  69.2 25.3 %collective-permute-start.5 = (bf16[64,2176]{1,0:T(8,128)(2,1)S(1)}, bf16[64,2176]{1,0:T(8,128)(2,1)S(1)}, u32[]{:S(2)}, u32[]{:S(2)}) collective-permute-start(bf16[64,2176]{1,0:T(8,128)(2,1)S(1)} %all_gather.3), channel_id=1, source_target_pairs={{0,2},{2,4},{4,6},{6,0},{1,3},{3,5},{5,7},{7,1},{8,10},{10,12},{12... | collective-permute-start | bytes 835592 | tf_op jit(solution)/shard_map/ppermute | solution.py:222
  73.5 18.7 %collective-permute-start.4 = (bf16[64,2176]{1,0:T(8,128)(2,1)S(1)}, bf16[64,2176]{1,0:T(8,128)(2,1)S(1)}, u32[]{:S(2)}, u32[]{:S(2)}) collective-permute-start(bf16[64,2176]{1,0:T(8,128)(2,1)S(1)} %all_gather.3), channel_id=1, source_target_pairs={{0,4},{2,6},{4,0},{6,2},{1,5},{3,7},{5,1},{7,3},{8,12},{10,14},{12... | collective-permute-start | bytes 835592 | tf_op jit(solution)/shard_map/ppermute | solution.py:222
  94.6 5.3 %collective-permute-start.7 = (bf16[256,2176]{1,0:T(8,128)(2,1)S(1)}, bf16[256,2176]{1,0:T(8,128)(2,1)}, u32[]{:S(2)}, u32[]{:S(2)}) collective-permute-start(bf16[256,2176]{1,0:T(8,128)(2,1)S(1)} %constant_dynamic-update-slice_fusion.rows_ref), channel_id=1, source_target_pairs={{0,1},{1,0},{2,3},{3,2},{4,5},{5,4},{6,7},{7,6},{8,9},{9,8},{10,11... | collective-permute-start | bytes 3342344 | tf_op jit(solution)/shard_map/ppermute | solution.py:224
  111.5 3.9 %collective-permute-start.8 = (bf16[2304,128]{1,0:T(8,128)(2,1)S(1)}, bf16[2304,128]{1,0:T(8,128)(2,1)S(1)}, u32[]{:S(2)}, u32[]{:S(2)}) collective-permute-start(bf16[2304,128]{1,0:T(8,128)(2,1)S(1)} %shard_map.106), channel_id=1, source_target_pairs={{0,1},{1,0},{2,3},{3,2},{4,5},{5,4},{6,7},{7,6},{8,9},{9,8},{10,11... | collective-permute-start | bytes 1769480 | tf_op jit(solution)/shard_map/ppermute | solution.py:244
